TPU v7x, 512 devices: a whole 4x8x8 slice. The times are simulated.
512 devices in a mesh: section: 2 (over core), fsdp: 64 (over z, y), tp: 4 (over x).
Axes of the slice: x: 4, y: 8, z: 8, core: 2. Of those that a mesh axis runs over, the one named last changes fastest.
Arguments:
- embeddings: bfloat16 [2, 8192, 8192], P(None, 'fsdp', 'tp'), may hold values from -80 to 80
- visual: bfloat16 [2, 64, 96, 8192], P('section', 'fsdp', None, 'tp'), may hold values from -80 to 80
- image_block_count: int32 [2, 64], P(None, 'fsdp'), may hold values from 1 to 3
- starts: int32 [2, 64], P(None, 'fsdp'), may hold values from 1 to 96, as said below
- lengths: int32 [2, 64], P(None, 'fsdp'), may hold values from 33 to 128
- queries: bfloat16 [2, 2, 8192, 8192], P('section', None, 'fsdp', 'tp'), may hold values from -100 to 100
- layer_key_vectors: bfloat16 [2, 2, 8192, 1024], P('section', None, 'fsdp', 'tp'), may hold values from -4.5 to 4.5
- input_norm_gain: bfloat16 [2, 8192], P('section', 'tp'), may hold values from 0.25 to 1.75
- frozen_value_weight: bfloat16 [2, 8192, 1024], P('section', 'tp', 'fsdp'), may hold values from -0.0625 to 0.0625
- adapter_down_map: bfloat16 [2, 8192, 16], P('section', 'tp'), may hold values from -0.0625 to 0.0625
- adapter_up_map: bfloat16 [2, 16, 1024], P('section'), may hold values from -1.5 to 1.5
- cotangent: bfloat16 [2, 8192, 8192], P(None, 'fsdp', 'tp'), may hold values from -6 to 6
Outputs:
- hidden_states: bfloat16 [2, 2, 8192, 8192], P('section', None, 'fsdp', 'tp')
- visual_grads: bfloat16 [2, 64, 96, 8192], P('section', 'fsdp', None, 'tp')
- down_map_gradient: float32 [2, 8192, 16], P('section', 'tp')
- up_map_gradient: float32 [2, 16, 1024], P('section', None, 'tp')
Inputs may be any that keep to these rules, and one draw needn't show every extreme that they name: starts + 32 * image_block_count <= lengths for every sequence.
All inputs are finite; a program needn't handle non-finite values.
Results may differ from a plain program's by a relative error of at most 0.015.
Values may be sent and summed in bfloat16 or wider, within the bound.
No kernel may reach another device: no remote copies, remote signals or barrier semaphores. Data moves between devices by JAX's collectives and lax.ppermute only.
A program may use at most 64 MiB of HBM per device.

v0:
```python
import math

import jax
import jax.numpy as jnp
from jax import lax
from jax.sharding import PartitionSpec as P

MODEL_WIDTH = 8192
HD = 128
TOKT = 32


ADAPTER_SCALE = 0.5
EPS = 1e-06
TOP_PRECISION = lax.Precision.HIGHEST


def from_behind(block, axis, distance):
    devices = range(lax.axis_size(axis))
    route = [(i - distance, i) for i in devices if i - distance in devices]
    return lax.ppermute(block, axis, route)


def spread(block, axis, source):
    block = jnp.where(lax.axis_index(axis) == source, block, jnp.zeros_like(block))
    return lax.psum(block, axis)


def slot_mask(begins, counts, row_count, slot_count):
    positions = jnp.arange(row_count, dtype=jnp.int32)[None, :, None]
    offsets = jnp.arange(slot_count, dtype=jnp.int32)[None, None, :]
    return (positions == begins[:, None, None] + offsets) & (offsets < counts[:, None, None])


def attend(query_matrix, key_matrix, value_vectors, seq_lengths):
    batch_count, row_count, local_width = query_matrix.shape
    groups = key_matrix.shape[2] // HD
    query_heads = query_matrix.reshape(
        batch_count, row_count, groups, local_width // (groups * HD), HD
    )
    key_heads = key_matrix.reshape(batch_count, row_count, groups, HD)
    value_heads = value_vectors.reshape(batch_count, row_count, groups, HD)
    scores = jnp.einsum(
        "bigkd,bjgd->bgkij", query_heads, key_heads, preferred_element_type=jnp.float32
    ) / math.sqrt(HD)
    positions = jnp.arange(row_count, dtype=jnp.int32)
    allowed = (positions[None, None, :] <= positions[None, :, None]) & (
        positions[None, None, :] < seq_lengths[:, None, None]
    )
    scores = jnp.where(allowed[:, None, None], scores, -jnp.inf)
    softmax_weights = jax.nn.softmax(scores, axis=-1).astype(jnp.bfloat16)
    attended = jnp.einsum(
        "bgkij,bjgd->bigkd", softmax_weights, value_heads, preferred_element_type=jnp.float32
    )
    return (attended.reshape(batch_count, row_count, local_width), softmax_weights)


def forward_layer(
    hidden_input,
    query_matrix,
    key_matrix,
    seq_lengths,
    input_norm_gain,
    value_columns,
    adapter_down_map,
    adapter_up_map,
    tp_index,
):
    in_float = hidden_input.astype(jnp.float32)
    squares = lax.psum(jnp.sum(in_float * in_float, axis=-1), "tp")
    inverse_norm = lax.rsqrt(squares / MODEL_WIDTH + EPS)[..., None]
    normalized_input = (in_float * inverse_norm * input_norm_gain).astype(jnp.bfloat16)
    normed_float = normalized_input.astype(jnp.float32)
    partial_values = jnp.einsum(
        "bsd,dk->bsk", normed_float, value_columns.astype(jnp.float32), precision=TOP_PRECISION
    )
    adapter_piece = jnp.einsum(
        "xhn,ny->xhy", normed_float, adapter_down_map.astype(jnp.float32), precision=TOP_PRECISION
    )
    up_single_float = adapter_up_map.astype(jnp.float32)
    local_cols = key_matrix.shape[2]
    value_portion = lax.psum_scatter(
        partial_values.astype(jnp.bfloat16), "tp", scatter_dimension=2, tiled=True
    ).astype(jnp.float32)
    adapter_rows = lax.psum(adapter_piece, "tp")
    up_columns = lax.dynamic_slice_in_dim(up_single_float, tp_index * local_cols, local_cols, 1)
    value_portion = value_portion + ADAPTER_SCALE * jnp.einsum(
        "fdj,jq->fdq", adapter_rows, up_columns, precision=TOP_PRECISION
    )
    value_vectors = value_portion.astype(jnp.bfloat16)
    attended, softmax_weights = attend(query_matrix, key_matrix, value_vectors, seq_lengths)
    final_result = (in_float + attended).astype(jnp.bfloat16)
    return (
        final_result,
        (hidden_input, normalized_input, inverse_norm, adapter_rows, softmax_weights),
    )


def layer_backward(
    output_gradient,
    saved_residuals,
    input_norm_gain,
    value_columns,
    adapter_down_map,
    adapter_up_map,
):
    hidden_input, normalized_input, inverse_norm, adapter_rows, softmax_weights = saved_residuals
    batch_count, row_count, local_width = output_gradient.shape
    groups = softmax_weights.shape[1]
    grad_heads = output_gradient.reshape(batch_count, row_count, groups, -1, HD)
    value_gradient = jnp.einsum(
        "bgkij,bigkd->bjgd", softmax_weights, grad_heads, preferred_element_type=jnp.float32
    )
    value_gradient = value_gradient.reshape(batch_count, row_count, groups * HD).astype(
        jnp.bfloat16
    )
    complete_gradient = lax.all_gather(value_gradient, "tp", axis=2, tiled=True)
    complete_float = complete_gradient.astype(jnp.float32)
    adapter_gradient = ADAPTER_SCALE * jnp.einsum(
        "unp,hp->unh", complete_float, adapter_up_map.astype(jnp.float32), precision=TOP_PRECISION
    )
    normalized_gradient = jnp.einsum(
        "bsk,dk->bsd", complete_float, value_columns.astype(jnp.float32), precision=TOP_PRECISION
    )
    normalized_gradient = normalized_gradient + jnp.einsum(
        "eqy,wy->eqw",
        adapter_gradient,
        adapter_down_map.astype(jnp.float32),
        precision=TOP_PRECISION,
    )
    down_map_gradient = jnp.einsum(
        "ofc,ofq->cq",
        normalized_input.astype(jnp.float32),
        adapter_gradient,
        precision=TOP_PRECISION,
    )
    in_float = hidden_input.astype(jnp.float32)
    scaled = normalized_gradient * input_norm_gain
    partial_dot = jnp.sum(scaled * in_float, axis=-1)
    dot_sums = lax.psum(partial_dot, "tp")
    up_map_gradient = ADAPTER_SCALE * jnp.einsum(
        "ylu,ylf->uf", adapter_rows, value_gradient.astype(jnp.float32), precision=TOP_PRECISION
    )
    grad_in = inverse_norm * scaled - in_float * inverse_norm**3 * dot_sums[..., None] / MODEL_WIDTH
    grad_total = (output_gradient.astype(jnp.float32) + grad_in).astype(jnp.bfloat16)
    return (grad_total, down_map_gradient, up_map_gradient)


def select_tree(flag, newer, earlier):
    return jax.tree.map(lambda latest, former: jnp.where(flag, latest, former), newer, earlier)


def on_device(
    embeddings,
    visual,
    image_block_count,
    starts,
    lengths,
    queries,
    layer_key_vectors,
    input_norm_gain,
    frozen_value_weight,
    adapter_down_map,
    adapter_up_map,
    cotangent,
):
    sections = lax.axis_size("section")
    section_index = lax.axis_index("section")
    tp_index = lax.axis_index("tp")
    micro = embeddings.shape[0]
    row_count = embeddings.shape[1]
    slot_count = visual.shape[2]
    gathered = lax.all_gather(visual, "section", axis=0, tiled=True)[:, 0]
    placing = slot_mask(starts[:, 0], image_block_count[:, 0] * TOKT, row_count, slot_count)
    covered = jnp.any(placing, axis=-1)
    placing_float = placing.astype(jnp.float32)
    inserted = jnp.einsum(
        "bsv,bvd->bsd", placing_float, gathered.astype(jnp.float32), precision=TOP_PRECISION
    ).astype(jnp.bfloat16)
    entry = jnp.where(covered[..., None], inserted, embeddings)
    local_queries = queries[0]
    local_keys = layer_key_vectors[0]
    gain_float = input_norm_gain[0].astype(jnp.float32)
    down_shard = adapter_down_map[0]
    up_shard = adapter_up_map[0]
    seq_lengths = lengths[:, 0]
    forward_cols = lax.all_gather(frozen_value_weight[0], "fsdp", axis=1, tiled=True)
    current = entry
    for phase_index in range(sections):
        final_result, saved_residuals = forward_layer(
            current,
            local_queries,
            local_keys,
            seq_lengths,
            gain_float,
            forward_cols,
            down_shard,
            up_shard,
            tp_index,
        )
        if phase_index == 0:
            layer_out, kept_residuals = (final_result, saved_residuals)
        else:
            active = section_index == phase_index
            layer_out = jnp.where(active, final_result, layer_out)
            kept_residuals = select_tree(active, saved_residuals, kept_residuals)
        if phase_index + 1 < sections:
            moved = from_behind(final_result, "section", 1)
            current = jnp.where(section_index == phase_index + 1, moved, current)
    backward_cols = lax.all_gather(frozen_value_weight[0], "fsdp", axis=1, tiled=True)
    current = cotangent
    for phase_index in range(sections):
        layer_section = sections - 1 - phase_index
        grad_in, down_map_gradient, up_map_gradient = layer_backward(
            current, kept_residuals, gain_float, backward_cols, down_shard, up_shard
        )
        if phase_index == 0:
            entry_grad, down_total, up_total = (grad_in, down_map_gradient, up_map_gradient)
        else:
            active = section_index == layer_section
            entry_grad = jnp.where(active, grad_in, entry_grad)
            down_total = jnp.where(active, down_map_gradient, down_total)
            up_total = jnp.where(active, up_map_gradient, up_total)
        if phase_index + 1 < sections:
            moved = from_behind(grad_in, "section", -1)
            current = jnp.where(section_index == layer_section - 1, moved, current)
    factor = 1.0 / math.sqrt(micro * row_count * lax.axis_size("fsdp"))
    down_sum, up_sum = lax.psum((down_total * factor, up_total * factor), "fsdp")
    slot_grads = jnp.einsum(
        "bsv,bsd->bvd", placing_float, entry_grad.astype(jnp.float32), precision=TOP_PRECISION
    ).astype(jnp.bfloat16)
    shared = spread(slot_grads, "section", 0)
    per_section = micro // sections
    own_slots = lax.dynamic_slice_in_dim(shared, section_index * per_section, per_section, 0)[
        :, None
    ]
    return (layer_out[None], own_slots, down_sum[None], up_sum[None])


def solution(mesh):
    return jax.shard_map(
        on_device,
        mesh=mesh,
        in_specs=(
            P(None, "fsdp", "tp"),
            P("section", "fsdp", None, "tp"),
            P(None, "fsdp"),
            P(None, "fsdp"),
            P(None, "fsdp"),
            P("section", None, "fsdp", "tp"),
            P("section", None, "fsdp", "tp"),
            P("section", "tp"),
            P("section", "tp", "fsdp"),
            P("section", "tp", None),
            P("section", None, None),
            P(None, "fsdp", "tp"),
        ),
        out_specs=(
            P("section", None, "fsdp", "tp"),
            P("section", "fsdp", None, "tp"),
            P("section", "tp", None),
            P("section", None, "tp"),
        ),
        check_vma=False,
    )
```

profile of v0, /device:TPU:1, one launch (start us, length us, event | category | flops | bytes accessed | tf_op | source)
XLA Modules:
  0.0 702.8 jit_solution(1655096675929762258)
XLA Ops:
  7.2 0.7 all-gather.3.cloned.1.call-update
  8.0 0.7 convert_element_type.141
  8.7 0.7 multiply_bitcast_fusion
  9.4 0.7 iota_add_fusion
  10.1 0.1 fusion.85
  10.3 9.1 %all_gather.13 = bf16[2,1,96,2048]{3,2,1,0:T(8,128)(2,1)S(1)} all-gather(bf16[1,1,96,2048]{3,2,1,0:T(8,128)(2,1)} %param.13), channel_id=1, replica_groups=mesh['section'=2,'fsdp'=64,'tp'=4] {'section'}, dimensions={0}, use_global_device_ids=true | all-gather | bytes 1179648 | tf_op jit(solution)/shard_map/all_gather | solution.py:173
  19.4 1.9 fusion.26
  21.3 6.1 psum.63
  27.4 0.4 fusion.70
  27.9 71.9 %all-gather.3.cloned.1.call-done = bf16[1,2048,1024]{1,2,0:T(8,128)(2,1)} async-done(((bf16[1,2048,16]{1,2,0:T(8,128)(2,1)}), bf16[1,2048,1024]{1,2,0:T(8,128)(2,1)}) %all-gather.3.cloned.1.call-update) | async-done | bytes 4194320 | tf_op jit(solution)/shard_map/all_gather | solution.py:187
  99.8 4.3 fusion.37
  104.3 0.2 copy.72
  104.5 0.5 copy-done.9
  105.1 0.4 copy-done.1
  105.4 0.7 copy.69
  106.1 13.1 %psum.64 = f32[2,128,16]{1,2,0:T(8,128)S(1)} all-reduce(f32[2,128,16]{1,2,0:T(8,128)S(1)} %fusion.70), channel_id=1, replica_groups=mesh['section'=2,'fsdp'=64,'tp'=4] {'tp'}, use_global_device_ids=true, to_apply=%region_4.5 | all-reduce | flops 4096 | bytes 32768 | tf_op jit(solution)/shard_map/psum | solution.py:85
  119.3 2.2 fusion.109
  121.5 1.9 divide_convert_fusion
  123.3 6.7 reduce-scatter.3.cloned.1.call-done
  130.0 1.2 fusion.44
  131.2 0.1 copy.63
  131.3 1.8 fusion.116
  133.1 2.9 copy.66
  136.0 3.1 fusion.29
  139.2 1.3 collective-permute-start
  140.5 0.4 fusion.45
  140.9 0.1 copy.45
  141.0 9.9 %all_gather.15 = bf16[2,128,1024]{2,1,0:T(8,128)(2,1)S(1)} all-gather(bf16[2,128,256]{2,1,0:T(8,128)(2,1)S(1)} %copy.45), channel_id=1, replica_groups=mesh['section'=2,'fsdp'=64,'tp'=4] {'tp'}, dimensions={2}, use_global_device_ids=true | all-gather | bytes 655360 | tf_op jit(solution)/shard_map/all_gather | solution.py:117
  150.9 0.2 convolution_multiply_fusion.3
  151.2 3.6 fusion.3
  154.8 4.6 fusion.34
  159.3 0.3 fusion.30
  159.6 6.6 all-reduce.1
  166.2 3.6 fusion.21
  169.8 10.7 %collective-permute-start.1 = (bf16[2,128,2048]{2,1,0:T(8,128)(2,1)}, bf16[2,128,2048]{2,1,0:T(8,128)(2,1)}, u32[]{:S(2)}, u32[]{:S(2)}) collective-permute-start(bf16[2,128,2048]{2,1,0:T(8,128)(2,1)} %fusion.21), channel_id=1, source_target_pairs={{256,0},{257,1},{258,2},{259,3},{260,4},{261,5},{262,6},{263,7},{2... | collective-permute-start | bytes 3145736 | tf_op jit(solution)/shard_map/ppermute | solution.py:21
  180.5 1.4 copy.59
  182.0 4.3 fusion.40
  186.3 0.2 all-reduce.5.cloned.1.call-start
  186.5 1.1 fusion.67
  187.6 1.1 broadcast_select_fusion
  188.7 1.6 copy.70
  190.3 1.4 copy.58
  191.8 2.0 fusion.46
  193.8 0.1 copy.48
  193.9 12.0 %all_gather.16 = bf16[2,128,1024]{2,1,0:T(8,128)(2,1)S(1)} all-gather(bf16[2,128,256]{2,1,0:T(8,128)(2,1)S(1)} %copy.48), channel_id=1, replica_groups=mesh['section'=2,'fsdp'=64,'tp'=4] {'tp'}, dimensions={2}, use_global_device_ids=true | all-gather | bytes 655360 | tf_op jit(solution)/shard_map/all_gather | solution.py:117
  205.9 0.2 convolution_multiply_fusion.2
  206.1 3.6 fusion.1
  209.7 2.7 fusion.35
  212.4 11.8 %all-reduce = (f32[2,128,16]{1,2,0:T(8,128)S(1)}, f32[2,128]{1,0:T(2,128)}) all-reduce(f32[2,128,16]{1,2,0:T(8,128)} %fusion.67, f32[2,128]{1,0:T(2,128)S(1)} %get-tuple-element.19), channel_id=1, replica_groups=mesh['section'=2,'fsdp'=64,'tp'=4] {'tp'}, use_global_device_ids=true, to_apply=%region_10.11 | all-reduce | flops 4352 | bytes 34816 | tf_op jit(solution)/shard_map/psum | solution.py:85
  224.2 0.2 fusion.51
  224.5 0.2 fusion.50
  224.7 225.5 %psum.71 = f32[1,16,256]{2,1,0:T(8,128)} all-reduce(f32[1,16,256]{2,1,0:T(8,128)S(1)} %fusion.50), channel_id=1, replica_groups=mesh['section'=2,'fsdp'=64,'tp'=4] {'fsdp'}, use_global_device_ids=true, to_apply=%region_17.18 | all-reduce | flops 4096 | bytes 32768 | tf_op jit(solution)/shard_map/psum | solution.py:228
  450.2 3.0 convolution_bitcast_fusion.1
  453.2 3.2 fusion.14
  456.6 1.2 add_convert_fusion
  457.8 0.1 copy.67
  457.9 1.8 fusion.117
  459.7 2.0 copy.68
  461.7 2.9 fusion.17
  464.6 1.4 fusion.53
  466.1 78.4 %all-reduce.5.cloned.1.call-done = bf16[2,96,2048]{2,1,0:T(8,128)(2,1)} async-done(((bf16[2,96,2048]{2,1,0:T(8,128)(2,1)}), bf16[2,96,2048]{2,1,0:T(8,128)(2,1)}) %all-reduce.5.cloned.1.call-update) | async-done | bytes 786448 | tf_op jit(solution)/shard_map/psum | solution.py:26
  544.5 1.8 dynamic-slice_bitcast_fusion
  546.3 148.4 %all-reduce.7.cloned.1.call-done = f32[1,2048,16]{1,2,0:T(8,128)} async-done(((f32[1,2048,16]{1,2,0:T(8,128)}), f32[1,2048,16]{1,2,0:T(8,128)}) %all-reduce.7.cloned.1.call-update) | async-done | bytes 131088 | tf_op jit(solution)/shard_map/psum | solution.py:228
  694.7 1.6 copy.95
  (68 shorter events, 0.7 us)
Async XLA Ops:
  7.2 20.3 %copy-start = (bf16[1,2048,16]{1,2,0:T(8,128)(2,1)S(1)}, bf16[1,2048,16]{1,2,0:T(8,128)(2,1)}, u32[]{:S(2)}) copy-start(bf16[1,2048,16]{1,2,0:T(8,128)(2,1)} %param.21) | copy-start | bytes 196612
  7.2 92.7 %all-gather.3.cloned.1.call-start = ((), (), s32[]{:S(2)}) async-start(), calls=%async_computation.6 | async-start | bytes 4259840 | tf_op jit(solution)/shard_map/all_gather | solution.py:187
  7.9 122.1 %reduce-scatter.3.cloned.1.call-start = ((), (), s32[]{:S(2)}) async-start(), calls=%async_computation.2 | async-start | bytes 655360 | tf_op jit(solution)/shard_map/reduce_scatter | solution.py:82
  9.4 11.9 %copy-start.21 = (pred[2,96]{1,0:T(4,128)(4,1)}, pred[2,96]{1,0:T(4,128)(4,1)S(1)}, u32[]{:S(2)}) copy-start(pred[2,96]{1,0:T(4,128)(4,1)S(1)} %iota_compare_fusion.3) | copy-start | bytes 580
  10.1 11.2 %copy-start.17 = (s32[2,96]{1,0:T(2,128)}, s32[2,96]{1,0:T(2,128)S(1)}, u32[]{:S(2)}) copy-start(s32[2,96]{1,0:T(2,128)S(1)} %iota_add_fusion) | copy-start | bytes 2308
  21.3 82.8 %copy-start.4 = (bf16[2,128,2048]{2,1,0:T(8,128)(2,1)}, bf16[2,128,2048]{2,1,0:T(8,128)(2,1)S(1)}, u32[]{:S(2)}) copy-start(bf16[2,128,2048]{2,1,0:T(8,128)(2,1)S(1)} %get-tuple-element.15) | copy-start | bytes 3145732
  27.4 76.7 %copy-start.15 = (f32[2,128]{1,0:T(2,128)}, f32[2,128]{1,0:T(2,128)S(1)}, u32[]{:S(2)}) copy-start(f32[2,128]{1,0:T(2,128)S(1)} %add_rsqrt_fusion.1) | copy-start | bytes 3076
  27.9 76.3 %copy-start.24 = (s32[2,1]{0,1:T(1,128)S(1)}, s32[2,1]{0,1:T(1,128)}, u32[]{:S(2)}) copy-start(s32[2,1]{0,1:T(1,128)} %param.16) | copy-start | bytes 28
  27.9 76.4 %copy-start.7 = (bf16[1,2,128,2048]{3,2,1,0:T(8,128)(2,1)S(1)}, bf16[1,2,128,2048]{3,2,1,0:T(8,128)(2,1)}, u32[]{:S(2)}) copy-start(bf16[1,2,128,2048]{3,2,1,0:T(8,128)(2,1)} %param.17) | copy-start | bytes 3145732
  104.1 0.9 copy-start.9
  104.1 1.3 copy-start.1
  104.2 352.4 %reduce-scatter.5.cloned.1.call-start = ((), (), s32[]{:S(2)}) async-start(), calls=%async_computation.3 | async-start | bytes 655360 | tf_op jit(solution)/shard_map/reduce_scatter | solution.py:82
  121.5 8.5 %copy-start.8 = (bf16[1,16,1024]{2,1,0:T(8,128)(2,1)S(1)}, bf16[1,16,1024]{2,1,0:T(8,128)(2,1)}, u32[]{:S(2)}) copy-start(bf16[1,16,1024]{2,1,0:T(8,128)(2,1)} %param.22) | copy-start | bytes 98308
  139.2 15.6 %collective-permute-start = (bf16[2,128,2048]{2,1,0:T(8,128)(2,1)}, bf16[2,128,2048]{2,1,0:T(8,128)(2,1)}, u32[]{:S(2)}, u32[]{:S(2)}) collective-permute-start(bf16[2,128,2048]{2,1,0:T(8,128)(2,1)} %fusion.29), channel_id=1, source_target_pairs={{0,256},{1,257},{2,258},{3,259},{4,260},{5,261},{6,262},{7,263},{8... | collective-permute-start | bytes 3145736 | tf_op jit(solution)/shard_map/ppermute | solution.py:21
  151.2 3.6 copy-start.10
  151.2 3.6 copy-start.5
  166.2 3.6 copy-start.13
  166.2 20.3 %copy-start.19 = (f32[2,128]{1,0:T(2,128)}, f32[2,128]{1,0:T(2,128)S(1)}, u32[]{:S(2)}) copy-start(f32[2,128]{1,0:T(2,128)S(1)} %get-tuple-element.13) | copy-start | bytes 3076
  169.8 17.8 %collective-permute-start.1 = (bf16[2,128,2048]{2,1,0:T(8,128)(2,1)}, bf16[2,128,2048]{2,1,0:T(8,128)(2,1)}, u32[]{:S(2)}, u32[]{:S(2)}) collective-permute-start(bf16[2,128,2048]{2,1,0:T(8,128)(2,1)} %fusion.21), channel_id=1, source_target_pairs={{256,0},{257,1},{258,2},{259,3},{260,4},{261,5},{262,6},{263,7},{2... | collective-permute-start | bytes 3145736 | tf_op jit(solution)/shard_map/ppermute | solution.py:21
  186.3 358.2 %all-reduce.5.cloned.1.call-start = ((), (), s32[]{:S(2)}) async-start(), calls=%async_computation.4 | async-start | bytes 1572864 | tf_op jit(solution)/shard_map/psum | solution.py:26
  206.1 3.6 copy-start.12
  206.1 3.6 copy-start.2
  224.4 228.8 %copy-start.14 = (f32[2,128]{1,0:T(2,128)S(1)}, f32[2,128]{1,0:T(2,128)}, u32[]{:S(2)}) copy-start(f32[2,128]{1,0:T(2,128)} %copy-done.13) | copy-start | bytes 3076
  224.4 228.8 %copy-start.18 = (s32[2,96]{1,0:T(2,128)S(1)}, s32[2,96]{1,0:T(2,128)}, u32[]{:S(2)}) copy-start(s32[2,96]{1,0:T(2,128)} %copy-done.17) | copy-start | bytes 2308
  224.5 228.7 %copy-start.22 = (pred[2,96]{1,0:T(4,128)(4,1)S(1)}, pred[2,96]{1,0:T(4,128)(4,1)}, u32[]{:S(2)}) copy-start(pred[2,96]{1,0:T(4,128)(4,1)} %copy-done.21) | copy-start | bytes 580
  224.5 228.7 %copy-start.23 = (f32[2,128]{1,0:T(2,128)S(1)}, f32[2,128]{1,0:T(2,128)}, u32[]{:S(2)}) copy-start(f32[2,128]{1,0:T(2,128)} %get-tuple-element.5) | copy-start | bytes 3076
  450.2 3.0 copy-start.3
  450.2 3.0 copy-start.6
  456.5 238.2 %all-reduce.7.cloned.1.call-start = ((), (), s32[]{:S(2)}) async-start(), calls=%async_computation.5 | async-start | bytes 262144 | tf_op jit(solution)/shard_map/psum | solution.py:228
  459.7 2.0 copy-start.11
  459.7 2.0 copy-start.16
  459.7 2.0 copy-start.20
  459.7 2.0 copy-start.25
Sparse Core Ops, SparseCore 0:
  11.1 88.7 all-gather.2
  104.3 25.6 reduce-scatter.2
  186.4 23.3 reduce-scatter.4
  456.6 87.8 all-reduce.4
  548.4 146.1 all-reduce.6
where the time goes:
time: 707 us; the launch traced here: 703 us
  waiting for transfers between devices  306 us (43%)
  blocking collectives  294 us (42%)
  matrix products  47 us (7%)
  local copies, waits for them, and re-layouts  15.1 us (2%)
  between operations  14.2 us (2%)
  other arithmetic  13.9 us (2%)
  starting transfers between devices  12.4 us (2%)
    psum x1, blocking collectives, on_device(): lax.psum((down_total * factor, up_total * factor), 'fsdp')  225 us
    psum x1, waiting for transfers between devices, on_device(): lax.psum((down_total * factor, up_total * factor), 'fsdp')  148 us
    psum x1, waiting for transfers between devices, spread(): return lax.psum(block, axis)  78.4 us
    all_gather x1, waiting for transfers between devices, on_device(): lax.all_gather(frozen_value_weight[0], 'fsdp', axis=1, tiled=True)  71.9 us
    psum x2, blocking collectives, forward_layer(): adapter_rows = lax.psum(adapter_piece, 'tp')  24.8 us
    all_gather x2, blocking collectives, layer_backward(): complete_gradient = lax.all_gather(value_gradient, 'tp', axis=2, tiled=True)  21.9 us
  transfers between devices with their start and end apart: 7, of which 4 were waited for; matrix products, arithmetic and copies ran while one was open for 7% of the time, Pallas kernels for 0%

commit v1 on v0

v1 whole, which is shorter than its diff:
```python
import functools
import math

import jax
import jax.numpy as jnp
from jax import lax
from jax.experimental import pallas as pl
from jax.experimental.pallas import tpu as pltpu
from jax.sharding import PartitionSpec as P

MODEL_WIDTH = 8192
HD = 128
TOKT = 32
ADAPTER_SCALE = 0.5
EPS = 1e-06

SEQ = 128
MB = 2
ROWS = MB * SEQ
VIS = 96
RANK = 16
HEADS = 8
HALF = HEADS * HD
KVH = 8
PEERS = 8
VMEM_BYTES = 40 * 1024 * 1024

BF = jnp.bfloat16
F32 = jnp.float32

R_VIS, R_Q, R_K, R_DN, R_UP, R_GN, R_END = 0, 96, 352, 384, 400, 416, 432
SMALL = 2 * RANK


def block_of(head):
    return (head % 2) * 4 + head // 2


def nt(left, right):
    return lax.dot_general(left, right, (((1,), (1,)), ((), ())), preferred_element_type=F32)


def tn(left, right):
    return lax.dot_general(left, right, (((0,), (0,)), ((), ())), preferred_element_type=F32)


def nn(left, right):
    return jnp.dot(left, right, preferred_element_type=F32)


def stack_heads(block):
    return jnp.concatenate([block[:, h * HD : (h + 1) * HD] for h in range(HEADS)], axis=0)


def unstack_heads(block):
    return jnp.concatenate([block[h * SEQ : (h + 1) * SEQ, :] for h in range(HEADS)], axis=1)


def columns_to_rows(*columns):
    lane = lax.broadcasted_iota(jnp.int32, (ROWS, HD), 1)
    square = jnp.zeros((ROWS, HD), F32)
    for at, column in enumerate(columns):
        square = jnp.where(lane == at, column, square)
    return square.T[:RANK, :]


def rows_to_columns(rows):
    padded = jnp.concatenate([rows, jnp.zeros((HD - RANK, ROWS), F32)], axis=0)
    return padded.T


def split_parts(rows):
    high = rows.astype(BF)
    low = (rows - high.astype(F32)).astype(BF)
    parts = [part[:, at : at + HD] for part in (high, low) for at in (0, HD)]
    return jnp.concatenate(parts, axis=0)


def join_parts(block, count):
    parts = [block[at * count : (at + 1) * count, :].astype(F32) for at in range(4)]
    return jnp.concatenate([parts[0] + parts[2], parts[1] + parts[3]], axis=1)


def inverse_of(squares):
    return lax.rsqrt(squares / MODEL_WIDTH + EPS)


def pack_kernel(core, visual, queries, keys, down, up, gain, out):
    other = 1 - core[0]
    at = pl.multiple_of(other * HALF, HALF)
    key_at = pl.multiple_of(other * HD, HD)
    out[R_VIS:R_Q, :] = visual[:, pl.ds(at, HALF)]
    out[R_Q:R_K, :] = queries[:, pl.ds(at, HALF)]
    for j in range(8):
        out[R_K:R_DN, j * HD : (j + 1) * HD] = keys[j * 32 : (j + 1) * 32, pl.ds(key_at, HD)]
    out[R_DN:R_UP, :] = down[:, pl.ds(at, HALF)]
    out[R_UP:R_GN, :] = up[...]
    out[R_GN:R_END, :] = gain[:, pl.ds(at, HALF)]


def softmax_of(query_rows, key_rows, length):
    scores = nt(stack_heads(query_rows), key_rows) / math.sqrt(HD)
    shape = scores.shape
    row = lax.rem(lax.broadcasted_iota(jnp.int32, shape, 0), SEQ)
    column = lax.broadcasted_iota(jnp.int32, shape, 1)
    allowed = (column <= row) & (column < length)
    scores = jnp.where(allowed, scores, -jnp.inf)
    top = jnp.max(scores, axis=-1, keepdims=True)
    weights = jnp.exp(scores - top)
    return (weights / jnp.sum(weights, axis=-1, keepdims=True)).astype(BF)


def prepare_kernel(
    core, counts, starts, lengths,
    received, visual, queries, keys, down, up, gain, embeddings, cotangent,
    weights, entry, cotangent_half, downs, ups, gains, payload,
):
    own = core[0]
    other = 1 - own
    at = pl.multiple_of(own * HALF, HALF)
    key_at = pl.multiple_of(own * HD, HD)
    half = pl.ds(at, HALF)
    downs[own] = down[:, half]
    downs[other] = received[R_DN:R_UP, :]
    ups[own] = up[...]
    ups[other] = received[R_UP:R_GN, :]
    gains[own] = gain[:, half]
    gains[other] = received[R_GN:R_END, :]
    position = lax.broadcasted_iota(jnp.int32, (SEQ, VIS), 0)
    slot = lax.broadcasted_iota(jnp.int32, (SEQ, VIS), 1)
    place = lax.broadcasted_iota(jnp.int32, (SEQ, 1), 0)
    for index, table in ((own, visual[:, half]), (other, received[R_VIS:R_Q, :])):
        begin = starts[index]
        count = counts[index] * TOKT
        placing = ((position == begin + slot) & (slot < count)).astype(F32).astype(BF)
        inserted = nn(placing, table).astype(BF)
        covered = (place >= begin) & (place < begin + count)
        rows = pl.ds(pl.multiple_of(index * SEQ, SEQ), SEQ)
        entry[rows, :] = jnp.where(covered, inserted, embeddings[index, :, half])
    for m in range(MB):
        rows = slice(m * SEQ, (m + 1) * SEQ)
        cotangent_half[rows, :] = cotangent[m, :, half]
        weights[own, m] = softmax_of(queries[rows, half], keys[rows, pl.ds(key_at, HD)], lengths[m])
        other_keys = jnp.concatenate(
            [received[R_K:R_DN, j * HD : (j + 1) * HD] for j in range(4 * m, 4 * m + 4)], axis=0
        )
        weights[other, m] = softmax_of(
            received[R_Q + m * SEQ : R_Q + (m + 1) * SEQ, :], other_keys, lengths[m]
        )
    value_gradient = jnp.concatenate(
        [
            tn(weights[1, m], stack_heads(cotangent_half[m * SEQ : (m + 1) * SEQ, :]))
            for m in range(MB)
        ],
        axis=0,
    ).astype(BF)
    entry_float = entry[...].astype(F32)
    squares = jnp.sum(entry_float * entry_float, axis=-1, keepdims=True)
    gained = (entry_float * gains[0][0:1, :].astype(F32)).astype(BF)
    small = jnp.concatenate([nt(downs[0], gained), columns_to_rows(squares)], axis=0)
    block = jnp.concatenate([value_gradient, split_parts(small)], axis=0)
    for peer in range(PEERS):
        payload[peer] = block


def entry_norm_kernel(
    received, entry, downs, ups, gains, normed, inverse, adapter_rows, full_gradient, lora_gradient
):
    total = jnp.zeros((SMALL, ROWS), F32)
    for peer in range(PEERS):
        total = total + join_parts(received[peer, ROWS:, :], SMALL)
    column = inverse_of(rows_to_columns(total[RANK:, :])[:, 0:1])
    inverse[...] = jnp.broadcast_to(column, (ROWS, HD))
    adapter_rows[...] = total[:RANK, :] * inverse_of(total[RANK : RANK + 1, :])
    gain = gains[0][0:1, :].astype(F32)
    normed[...] = (entry[...].astype(F32) * column * gain).astype(BF)
    for head in range(KVH):
        full_gradient[:, head * HD : (head + 1) * HD] = received[block_of(head), :ROWS, :]
    lora_gradient[...] = ADAPTER_SCALE * nt(ups[1], full_gradient[...])


def values_kernel(layer, normed, columns, downs, ups, out):
    rows = normed[...]
    adapter = (ADAPTER_SCALE * nt(rows, downs[layer])).astype(BF)
    for pair in range(KVH // 2):
        weight = columns[2 * pair : 2 * pair + 2, layer].reshape(2 * HD, HALF)
        up = ups[layer][:, 2 * pair * HD : (2 * pair + 2) * HD]
        partial = (nt(rows, weight) + nn(adapter, up)).astype(BF)
        out[block_of(2 * pair)] = partial[:, :HD]
        out[block_of(2 * pair + 1)] = partial[:, HD:]


def scaled_kernel(full_gradient, lora_gradient, columns, downs, gains, scaled):
    weight = columns[:, 1].reshape(KVH * HD, HALF)
    grad = nn(full_gradient[...], weight) + tn(lora_gradient[...].astype(BF), downs[1])
    scaled[...] = grad * gains[1][0:1, :].astype(F32)


def attended_rows(weights, layer, value_rows):
    return jnp.concatenate(
        [
            unstack_heads(nn(weights[layer, m], value_rows[m * SEQ : (m + 1) * SEQ, :]))
            for m in range(MB)
        ],
        axis=0,
    )


def first_output_kernel(
    received, weights, entry, scaled, downs, gains, hidden, value_rows, payload
):
    values = received[0].astype(F32)
    for peer in range(1, PEERS):
        values = values + received[peer].astype(F32)
    value_rows[...] = values
    attended = attended_rows(weights, 0, values.astype(BF))
    output = (entry[...].astype(F32) + attended).astype(BF)
    hidden[...] = output
    output_float = output.astype(F32)
    squares = jnp.sum(output_float * output_float, axis=-1, keepdims=True)
    dots = jnp.sum(output_float * scaled[...], axis=-1, keepdims=True)
    gained = (output_float * gains[1][0:1, :].astype(F32)).astype(BF)
    small = jnp.concatenate([nt(downs[1], gained), columns_to_rows(squares, dots)], axis=0)
    for peer in range(PEERS):
        payload[peer] = small


def first_gradient_kernel(
    received, weights, hidden, scaled, cotangent_half, gains, value_rows,
    gradient, normed, adapter_rows, payload,
):
    total = received[0]
    for peer in range(1, PEERS):
        total = total + received[peer]
    sums = rows_to_columns(total[RANK:, :])
    column = inverse_of(sums[:, 0:1])
    factor = column * column * column * sums[:, 1:2] / MODEL_WIDTH
    adapter_rows[...] = total[:RANK, :] * inverse_of(total[RANK : RANK + 1, :])
    hidden_float = hidden[...].astype(F32)
    gain = gains[1][0:1, :].astype(F32)
    normed[...] = (hidden_float * column * gain).astype(BF)
    grad = (
        cotangent_half[...].astype(F32) + column * scaled[...] - hidden_float * factor
    ).astype(BF)
    gradient[...] = grad
    value_gradient = jnp.concatenate(
        [tn(weights[0, m], stack_heads(grad[m * SEQ : (m + 1) * SEQ, :])) for m in range(MB)],
        axis=0,
    ).astype(BF)
    dots = jnp.sum(value_gradient.astype(F32) * value_rows[...], axis=-1, keepdims=True)
    block = jnp.concatenate([value_gradient, split_parts(columns_to_rows(dots))], axis=0)
    for peer in range(PEERS):
        payload[peer] = block


def map_chunks(down_gradient, up_gradient):
    quarter = HALF // 4
    left = jnp.concatenate(
        [down_gradient[:, q * quarter : (q + 1) * quarter] for q in range(4)], axis=0
    )
    right = jnp.concatenate([up_gradient, jnp.zeros((3 * RANK, HD), F32)], axis=0)
    return jnp.concatenate([left, right], axis=1)


def map_gradient_kernel(
    core, received, ups, normed_0, adapter_0, normed_1, adapter_1, full_gradient, lora_gradient_1,
    last_gradient, lora_gradient_0, out,
):
    own = core[0] * 4 + core[1]
    for head in range(KVH):
        last_gradient[:, head * HD : (head + 1) * HD] = received[block_of(head), :ROWS, :]
    lora_0 = ADAPTER_SCALE * nt(ups[0], last_gradient[...])
    lora_gradient_0[...] = lora_0
    down_0 = nn(lora_0.astype(BF), normed_0[...])
    up_0 = ADAPTER_SCALE * nn(adapter_0[...].astype(BF), received[own, :ROWS, :])
    out[0] = map_chunks(down_0, up_0)
    own_columns = pl.ds(pl.multiple_of((2 * core[1] + core[0]) * HD, HD), HD)
    down_1 = nn(lora_gradient_1[...].astype(BF), normed_1[...])
    up_1 = ADAPTER_SCALE * nn(adapter_1[...].astype(BF), full_gradient[:, own_columns])
    out[1] = map_chunks(down_1, up_1)


def slot_gradient_kernel(
    core, counts, starts,
    received, last_gradient, lora_gradient, columns, downs, gains, entry, inverse, gradient,
    slots,
):
    total = jnp.zeros((RANK, ROWS), F32)
    for peer in range(PEERS):
        total = total + join_parts(received[peer, ROWS:, :], RANK)
    column = inverse[:, 0:1]
    factor = column * column * rows_to_columns(total)[:, 0:1] / MODEL_WIDTH
    weight = columns[:, 0].reshape(KVH * HD, HALF)
    grad = nn(last_gradient[...], weight) + tn(lora_gradient[...].astype(BF), downs[0])
    scaled = grad * gains[0][0:1, :].astype(F32)
    rows = (
        gradient[...].astype(F32) + column * scaled - entry[...].astype(F32) * factor
    ).astype(BF)
    slot = lax.broadcasted_iota(jnp.int32, (VIS, SEQ), 0)
    position = lax.broadcasted_iota(jnp.int32, (VIS, SEQ), 1)
    for m in range(MB):
        picking = ((position == starts[m] + slot) & (slot < counts[m] * TOKT)).astype(F32).astype(BF)
        slots[m] = nn(picking, rows[m * SEQ : (m + 1) * SEQ, :]).astype(BF)


def second_output_kernel(values, weights, hidden, out):
    attended = attended_rows(weights, 1, values[...])
    out[...] = (hidden[...].astype(F32) + attended).astype(BF)


def call(kernel, name, shapes, scalars, arrays, flops=0):
    in_specs = [pl.BlockSpec(memory_space=pltpu.SMEM)] * len(scalars)
    in_specs += [pl.BlockSpec(memory_space=pltpu.VMEM)] * len(arrays)
    outs = [jax.ShapeDtypeStruct(shape, dtype) for shape, dtype in shapes]
    moved = sum(a.size * a.dtype.itemsize for a in arrays)
    moved += sum(math.prod(shape) * jnp.dtype(dtype).itemsize for shape, dtype in shapes)
    result = pl.pallas_call(
        kernel,
        out_shape=outs,
        in_specs=in_specs,
        out_specs=[pl.BlockSpec(memory_space=pltpu.VMEM)] * len(outs),
        compiler_params=pltpu.CompilerParams(vmem_limit_bytes=VMEM_BYTES),
        cost_estimate=pl.CostEstimate(flops=flops, bytes_accessed=moved, transcendentals=0),
        name=name,
    )(*scalars, *arrays)
    return result


def swap_cores(block):
    return lax.ppermute(block, "section", [(0, 1), (1, 0)])


def to_heads(block):
    return lax.all_to_all(block, ("section", "tp"), 0, 0)


def on_device(
    embeddings,
    visual,
    image_block_count,
    starts,
    lengths,
    queries,
    layer_key_vectors,
    input_norm_gain,
    frozen_value_weight,
    adapter_down_map,
    adapter_up_map,
    cotangent,
):
    section = lax.axis_index("section")
    tp = lax.axis_index("tp")
    n_fsdp = lax.axis_size("fsdp")
    n_y = n_fsdp // KVH
    core = jnp.stack([section, tp]).astype(jnp.int32)
    counts = image_block_count[:, 0]
    begins = starts[:, 0]
    seq_lengths = lengths[:, 0]

    shard = frozen_value_weight[0].T
    pieces = shard.reshape(shard.shape[0], 2, HALF).transpose(1, 0, 2)
    pieces = jnp.broadcast_to(pieces[:, None], (2, n_y) + pieces.shape[1:])
    pieces = pieces.reshape((2 * n_y,) + pieces.shape[2:])
    head_groups = [
        [s * n_fsdp + z * n_y + y for s in range(2) for y in range(n_y)] for z in range(KVH)
    ]
    head_columns = lax.all_to_all(
        pieces, ("section", "fsdp"), 0, 0, axis_index_groups=head_groups
    ).reshape(2, HD, HALF)
    row_groups = [[z * n_y + y for z in range(KVH)] for y in range(n_y)]
    columns = lax.all_gather(head_columns, "fsdp", axis=0, axis_index_groups=row_groups)

    own_visual = visual[0, 0]
    own_queries = queries[0].reshape(ROWS, 2 * HALF)
    own_keys = layer_key_vectors[0].reshape(ROWS, 2 * HD)
    own_down = adapter_down_map[0].T
    own_up = adapter_up_map[0]
    own_gain = jnp.broadcast_to(input_norm_gain, (RANK, 2 * HALF))
    own = (own_visual, own_queries, own_keys, own_down, own_up, own_gain)
    (packed,) = call(pack_kernel, "pack", [((R_END, HALF), BF)], (core,), own)
    received = swap_cores(packed)

    wide = ((ROWS, HALF), BF)
    small = ((RANK, ROWS), F32)
    maps = ((2, RANK, HALF), BF)
    weights, entry, cotangent_half, downs, ups, gains, payload = call(
        prepare_kernel,
        "prepare",
        [
            ((2, MB, HEADS * SEQ, SEQ), BF),
            wide,
            wide,
            maps,
            maps,
            maps,
            ((PEERS, ROWS + 4 * SMALL, HD), BF),
        ],
        (core, counts, begins, seq_lengths),
        (received, *own, embeddings, cotangent),
    )
    normed_0, inverse_0, adapter_0, full_gradient, lora_gradient_1 = call(
        entry_norm_kernel,
        "entry_norm",
        [wide, ((ROWS, HD), F32), small, wide, small],
        (),
        (to_heads(payload), entry, downs, ups, gains),
    )

    blocks = ((PEERS, ROWS, HD), BF)
    (partial_0,) = call(
        functools.partial(values_kernel, 0), "values_0", [blocks], (), (normed_0, columns, downs, ups)
    )
    (scaled_1,) = call(
        scaled_kernel,
        "scaled_1",
        [((ROWS, HALF), F32)],
        (),
        (full_gradient, lora_gradient_1, columns, downs, gains),
    )
    hidden_0, value_rows, payload = call(
        first_output_kernel,
        "first_output",
        [wide, ((ROWS, HD), F32), ((PEERS, SMALL, ROWS), F32)],
        (),
        (to_heads(partial_0), weights, entry, scaled_1, downs, gains),
    )
    gradient, normed_1, adapter_1, payload = call(
        first_gradient_kernel,
        "first_gradient",
        [wide, wide, small, ((PEERS, ROWS + 4 * RANK, HD), BF)],
        (),
        (to_heads(payload), weights, hidden_0, scaled_1, cotangent_half, gains, value_rows),
    )
    gathered = to_heads(payload)
    (partial_1,) = call(
        functools.partial(values_kernel, 1), "values_1", [blocks], (), (normed_1, columns, downs, ups)
    )
    values_1 = lax.psum_scatter(partial_1, ("section", "tp"), scatter_dimension=0)

    last_gradient, lora_gradient_0, chunks = call(
        map_gradient_kernel,
        "map_gradient",
        [wide, small, ((2, 4 * RANK, HALF // 4 + HD), F32)],
        (core,),
        (gathered, ups, normed_0, adapter_0, normed_1, adapter_1, full_gradient, lora_gradient_1),
    )
    width = HALF // 4 + HD
    arrived = lax.all_to_all(
        chunks.reshape(2 * n_fsdp, 1, width), ("section", "fsdp"), 0, 0
    ).reshape(2, n_fsdp, width)
    summed = jnp.sum(arrived, axis=1)
    everywhere = lax.all_to_all(
        jnp.broadcast_to(summed.reshape(1, 1, 2 * width), (n_fsdp, 1, 2 * width)), "fsdp", 0, 0
    ).reshape(4, RANK, 2, width)
    everywhere = everywhere * (1.0 / math.sqrt(MB * SEQ * n_fsdp))
    down_sum = (
        everywhere[..., : HALF // 4].transpose(1, 2, 0, 3).reshape(RANK, 2 * HALF).T
    )
    up_sum = everywhere[0, :, :, HALF // 4 :].reshape(RANK, 2 * HD)

    (slots,) = call(
        slot_gradient_kernel,
        "slot_gradient",
        [((MB, VIS, HALF), BF)],
        (core, counts, begins),
        (
            gathered,
            last_gradient,
            lora_gradient_0,
            columns,
            downs,
            gains,
            entry,
            inverse_0,
            gradient,
        ),
    )
    (hidden_1,) = call(
        second_output_kernel, "second_output", [wide], (), (values_1, weights, hidden_0)
    )

    first = section == 0

    def halves(mine, theirs):
        left = jnp.where(first, mine, theirs)
        right = jnp.where(first, theirs, mine)
        return jnp.concatenate([left, right], axis=-1)

    slot_rows = halves(
        jnp.where(first, slots[0], slots[1]), swap_cores(jnp.where(first, slots[1], slots[0]))
    )
    hidden = halves(
        jnp.where(first, hidden_0, hidden_1), swap_cores(jnp.where(first, hidden_1, hidden_0))
    )
    return (
        hidden.reshape(1, MB, SEQ, 2 * HALF),
        slot_rows[None, None],
        down_sum[None],
        up_sum[None],
    )


def solution(mesh):
    return jax.shard_map(
        on_device,
        mesh=mesh,
        in_specs=(
            P(None, "fsdp", "tp"),
            P("section", "fsdp", None, "tp"),
            P(None, "fsdp"),
            P(None, "fsdp"),
            P(None, "fsdp"),
            P("section", None, "fsdp", "tp"),
            P("section", None, "fsdp", "tp"),
            P("section", "tp"),
            P("section", "tp", "fsdp"),
            P("section", "tp", None),
            P("section", None, None),
            P(None, "fsdp", "tp"),
        ),
        out_specs=(
            P("section", None, "fsdp", "tp"),
            P("section", "fsdp", None, "tp"),
            P("section", "tp", None),
            P("section", None, "tp"),
        ),
        check_vma=False,
    )
```

time: 707 us -> 208 us (0.29)
  blocking collectives: 294 us -> 50.3 us
  waiting for transfers between devices: 306 us -> 66.5 us
  matrix products: 47 us -> 0 us
  starting transfers between devices: 12.4 us -> 32.2 us
  Pallas kernels: 0 us -> 14.1 us
  other arithmetic: 13.9 us -> 2.72 us
  local copies, waits for them, and re-layouts: 15.1 us -> 25.8 us
    psum x5 -> x0, blocking collectives: 263 us -> none  [the longest x1 225 us: on_device(): lax.psum((down_total * factor, up_total * factor), 'fsdp')]
    psum x2 -> x0, waiting for transfers between devices: 227 us -> none  [the longest x1 148 us: on_device(): lax.psum((down_total * factor, up_total * factor), 'fsdp')]
    all_to_all x0 -> x3, blocking collectives: none -> 50.3 us  [the longest x2 25.3 us: to_heads(): return lax.all_to_all(block, ('section', 'tp'), 0, 0)]
    dot_general x22 -> x0, matrix products: 44.8 us -> none  [the longest x2 8.6 us: forward_layer(): jnp.einsum('bsd,dk->bsk', normed_float, value_columns.astype(jnp.float32)...]
    all_gather x1, waiting for transfers between devices: 71.9 us -> 30.7 us  [on_device(): lax.all_gather(head_columns, 'fsdp', axis=0, axis_index_groups=row_groups)]
    all_to_all x0 -> x4, waiting for transfers between devices: none -> 33.7 us  [the longest x1 14.4 us: on_device(): lax.all_to_all(chunks.reshape(2 * n_fsdp, 1, width), ('section', 'fsdp'),...]
    all_gather x3 -> x0, blocking collectives: 31 us -> none  [the longest x2 21.9 us: layer_backward(): complete_gradient = lax.all_gather(value_gradient, 'tp', axis=2, tiled=True)]
    all_to_all x0 -> x4, starting transfers between devices: none -> 24.2 us  [the longest x1 10.9 us: on_device(): lax.all_to_all(chunks.reshape(2 * n_fsdp, 1, width), ('section', 'fsdp'),...]
  transfers between devices with their start and end apart: 7 -> 9, of which waited for: 4 -> 6; matrix products, arithmetic and copies ran while one was open for 7% -> 2% of each run, Pallas kernels for 0% -> 5%
where the time goes in v1:
time: 208 us; the launch traced here: 206 us
  waiting for transfers between devices  66.5 us (32%)
  blocking collectives  50.3 us (24%)
  starting transfers between devices  32.2 us (15%)
  local copies, waits for them, and re-layouts  25.8 us (12%)
  between operations  14.4 us (7%)
  Pallas kernels  14.1 us (7%)
  other arithmetic  2.72 us (1%)
    all_gather x1, waiting for transfers between devices, on_device(): lax.all_gather(head_columns, 'fsdp', axis=0, axis_index_groups=row_groups)  30.7 us
    all_to_all x2, blocking collectives, to_heads(): return lax.all_to_all(block, ('section', 'tp'), 0, 0)  25.3 us
    all_to_all x1, blocking collectives, on_device(): lax.all_to_all(pieces, ('section', 'fsdp'), 0, 0, axis_index_groups=head_...  24.9 us
    unnamed x61, local copies, waits for them, and re-layouts  21.5 us
    all_to_all x1, waiting for transfers between devices, on_device(): lax.all_to_all(chunks.reshape(2 * n_fsdp, 1, width), ('section', 'fsdp'),...  14.4 us
    pallas_call x11, Pallas kernels, call(): pl.pallas_call(kernel, out_shape=outs, in_specs=in_specs, out_specs=[pl.B...  14.1 us
    all_to_all x2, waiting for transfers between devices, to_heads(): return lax.all_to_all(block, ('section', 'tp'), 0, 0)  12.1 us
    all_to_all x1, starting transfers between devices, on_device(): lax.all_to_all(chunks.reshape(2 * n_fsdp, 1, width), ('section', 'fsdp'),...  10.9 us
  transfers between devices with their start and end apart: 9, of which 6 were waited for; matrix products, arithmetic and copies ran while one was open for 2% of the time, Pallas kernels for 5%

profile of v1, /device:TPU:1, one launch (start us, length us, event | category | flops | bytes accessed | tf_op | source)
XLA Modules:
  0.0 206.0 jit_solution(11757690620190781499)
XLA Ops:
  7.2 0.0 copy-start.12
  7.2 0.0 all-gather.2.cloned.1.call-start
  7.3 1.0 reshape.38
  8.3 0.1 broadcast_in_dim.28
  8.4 0.0 copy-start.27
  8.4 24.9 %all_to_all.35 = bf16[16,16,1024]{2,1,0:T(8,128)(2,1)} all-to-all(bf16[16,16,1024]{2,1,0:T(8,128)(2,1)S(1)} %bitcast.52), channel_id=1, replica_groups={{0,4,8,12,16,20,24,28,256,260,264,268,272,276,280,284},{32,36,40,44,48,..., dimensions={0} | all-to-all | bytes 1048576 | tf_op jit(solution)/shard_map/all_to_all | solution.py:367
  33.3 0.0 all-gather.2.cloned.1.call-update
  33.4 0.1 pad_add_fusion.core
  33.5 0.6 pack.1
  34.1 2.9 %collective-permute-start = (bf16[432,1024]{1,0:T(8,128)(2,1)S(1)}, bf16[432,1024]{1,0:T(8,128)(2,1)S(1)}, u32[]{:S(2)}, u32[]{:S(2)}) collective-permute-start(bf16[432,1024]{1,0:T(8,128)(2,1)S(1)} %pack.1), channel_id=1, source_target_pairs={{0,256},{256,0},{1,257},{257,1},{2,258},{258,2},{3,259},{259,3},{4... | collective-permute-start | bytes 2654216 | tf_op jit(solution)/shard_map/ppermute | solution.py:330
  37.0 2.0 collective-permute-done.received
  39.1 1.0 copy-done.13
  40.1 1.2 copy-done.14
  41.3 1.2 copy-done.15
  42.5 0.8 copy-done.24
  43.3 2.6 %prepare.1 = (bf16[2,2,1024,128]{3,2,1,0:T(8,128)(2,1)S(1)}, bf16[256,1024]{1,0:T(8,128)(2,1)S(1)}, bf16[256,1024]{1,0:T(8,128)(2,1)S(1)}, bf16[2,16,1024]{2,1,0...) custom-call(s32[2]{0:T(128)S(1)} %pad_add_fusion.core, ...), custom_call_target="tpu_custom_call" | custom-call | bytes 7798784 | tf_op jit(solution)/shard_map/prepare/pallas_call | solution.py:317
  45.9 15.6 %all_to_all.36.received = bf16[8,384,128]{2,1,0:T(8,128)(2,1)S(1)} all-to-all(bf16[8,384,128]{2,1,0:T(8,128)(2,1)S(1)} %get-tuple-element.26), channel_id=1, replica_groups=mesh['section'=2,'fsdp'=64,'tp'=4] {'section','tp'}, dimensions={0} | all-to-all | bytes 1572864 | tf_op jit(solution)/shard_map/all_to_all | solution.py:334
  61.5 0.4 entry_norm.1
  61.9 30.7 %all-gather.2.cloned.1.call-done.columns = bf16[8,2,128,1024]{3,2,1,0:T(8,128)(2,1)} async-done(((bf16[1,2,128,1024]{3,2,1,0:T(8,128)(2,1)}), bf16[8,2,128,1024]{3,2,1,0:T(8,128)(2,1)}) %all-gather.2.cloned.1.call-update) | async-done | bytes 4194320 | tf_op jit(solution)/shard_map/all_gather | solution.py:371
  92.6 2.2 %copy-done = bf16[8,2,128,1024]{3,2,1,0:T(8,128)(2,1)S(1)} copy-done((bf16[8,2,128,1024]{3,2,1,0:T(8,128)(2,1)S(1)}, bf16[8,2,128,1024]{3,2,1,0:T(8,128)(2,1)}, u32[]{:S(2)}) %copy-start) | copy-done | bytes 4194328
  94.7 1.8 values_0.1
  96.6 4.9 %all-to-all-start.2 = ((bf16[8,256,128]{2,1,0:T(8,128)(2,1)}), bf16[8,256,128]{2,1,0:T(8,128)(2,1)}, u32[]{:S(2)}, u32[]{:S(2)}) async-start(bf16[8,256,128]{2,1,0:T(8,128)(2,1)} %values_0.1), calls=%async_computation.2 | async-start | bytes 1048576 | tf_op jit(solution)/shard_map/all_to_all | solution.py:334
  101.5 2.2 %copy-done.1 = bf16[8,2,128,1024]{3,2,1,0:T(8,128)(2,1)S(1)} copy-done((bf16[8,2,128,1024]{3,2,1,0:T(8,128)(2,1)S(1)}, bf16[8,2,128,1024]{3,2,1,0:T(8,128)(2,1)}, u32[]{:S(2)}) %copy-start.1) | copy-done | bytes 4194328
  103.7 0.9 scaled_1.1.scaled
  104.5 6.4 %all-to-all-done.2.received = bf16[8,256,128]{2,1,0:T(8,128)(2,1)} async-done(((bf16[8,256,128]{2,1,0:T(8,128)(2,1)}), bf16[8,256,128]{2,1,0:T(8,128)(2,1)}, u32[]{:S(2)}, u32[]{:S(2)}) %all-to-all-start.2) | async-done | bytes 524320 | tf_op jit(solution)/shard_map/all_to_all | solution.py:334
  111.0 1.8 first_output.1
  112.8 9.8 %all_to_all.37.received = f32[8,32,256]{2,1,0:T(8,128)S(1)} all-to-all(f32[8,32,256]{2,1,0:T(8,128)S(1)} %get-tuple-element.36), channel_id=1, replica_groups=mesh['section'=2,'fsdp'=64,'tp'=4] {'section','tp'}, dimensions={0} | all-to-all | bytes 524288 | tf_op jit(solution)/shard_map/all_to_all | solution.py:334
  122.6 0.8 first_gradient.1
  123.4 0.8 copy-done.9
  124.2 0.8 copy-done.16
  125.0 0.8 copy-done.20
  125.9 3.8 %all-to-all-start.4 = ((bf16[8,320,128]{2,1,0:T(8,128)(2,1)}), bf16[8,320,128]{2,1,0:T(8,128)(2,1)S(1)}, u32[]{:S(2)}, u32[]{:S(2)}) async-start(bf16[8,320,128]{2,1,0:T(8,128)(2,1)} %copy-done.16), calls=%async_computation.5 | async-start | bytes 1310720 | tf_op jit(solution)/shard_map/all_to_all | solution.py:334
  129.7 2.2 %copy-done.2 = bf16[8,2,128,1024]{3,2,1,0:T(8,128)(2,1)S(1)} copy-done((bf16[8,2,128,1024]{3,2,1,0:T(8,128)(2,1)S(1)}, bf16[8,2,128,1024]{3,2,1,0:T(8,128)(2,1)}, u32[]{:S(2)}) %copy-start.2) | copy-done | bytes 4194328
  131.9 1.0 copy-done.10
  132.9 1.8 values_1.1
  134.7 0.0 reduce-scatter.2.cloned.1.call-update
  134.8 5.7 %all-to-all-done.4.received = bf16[8,320,128]{2,1,0:T(8,128)(2,1)S(1)} async-done(((bf16[8,320,128]{2,1,0:T(8,128)(2,1)}), bf16[8,320,128]{2,1,0:T(8,128)(2,1)S(1)}, u32[]{:S(2)}, u32[]{:S(2)}) %all-to-all-start.4) | async-done | bytes 655392 | tf_op jit(solution)/shard_map/all_to_all | solution.py:334
  140.5 1.0 copy-done.6
  141.5 1.0 copy-done.8
  142.5 1.0 copy-done.11
  143.6 1.3 map_gradient.1
  144.9 2.2 %copy-done.3 = bf16[8,2,128,1024]{3,2,1,0:T(8,128)(2,1)S(1)} copy-done((bf16[8,2,128,1024]{3,2,1,0:T(8,128)(2,1)S(1)}, bf16[8,2,128,1024]{3,2,1,0:T(8,128)(2,1)}, u32[]{:S(2)}) %copy-start.3) | copy-done | bytes 4194328
  147.1 1.0 copy-done.21
  148.1 1.7 slot_gradient.1
  149.9 2.3 %collective-permute-start.2 = (bf16[96,1024]{1,0:T(8,128)(2,1)S(1)}, bf16[96,1024]{1,0:T(8,128)(2,1)S(1)}, u32[]{:S(2)}, u32[]{:S(2)}) collective-permute-start(bf16[96,1024]{1,0:T(8,128)(2,1)S(1)} %select_bitcast_fusion), channel_id=1, source_target_pairs={{0,256},{256,0},{1,257},{257,1},{2,258},{258,2},{3,259},{259,3},{4... | collective-permute-start | bytes 589832 | tf_op jit(solution)/shard_map/ppermute | solution.py:330
  152.2 0.9 copy.19
  153.1 10.9 %all-to-all-start.5 = ((f32[128,1,384]{2,1,0:T(1,128)}), f32[128,1,384]{2,1,0:T(1,128)S(1)}, u32[]{:S(2)}, u32[]{:S(2)}) async-start(f32[128,1,384]{2,1,0:T(1,128)} %copy.19), calls=%async_computation.6 | async-start | bytes 393216 | tf_op jit(solution)/shard_map/all_to_all | solution.py:448
  164.0 14.4 %all-to-all-done.5 = f32[128,1,384]{2,1,0:T(1,128)S(1)} async-done(((f32[128,1,384]{2,1,0:T(1,128)}), f32[128,1,384]{2,1,0:T(1,128)S(1)}, u32[]{:S(2)}, u32[]{:S(2)}) %all-to-all-start.5) | async-done | bytes 196640 | tf_op jit(solution)/shard_map/all_to_all | solution.py:448
  178.4 0.8 broadcast_in_dim.31
  179.2 4.6 %all-to-all-start.6 = ((f32[64,1,768]{2,1,0:T(1,128)}), f32[64,1,768]{2,1,0:T(1,128)S(1)}, u32[]{:S(2)}, u32[]{:S(2)}) async-start(f32[64,1,768]{2,1,0:T(1,128)} %broadcast_in_dim.31), calls=%async_computation.7 | async-start | bytes 393216 | tf_op jit(solution)/shard_map/all_to_all | solution.py:452
  183.8 0.0 reduce-scatter.2.cloned.1.call-done
  183.8 0.8 copy-done.25
  184.7 0.3 second_output.1
  185.0 0.1 broadcast_select_fusion.2
  185.0 2.8 %collective-permute-start.1 = (bf16[256,1024]{1,0:T(8,128)(2,1)S(1)}, bf16[256,1024]{1,0:T(8,128)(2,1)S(1)}, u32[]{:S(2)}, u32[]{:S(2)}) collective-permute-start(bf16[256,1024]{1,0:T(8,128)(2,1)S(1)} %broadcast_select_fusion.2), channel_id=1, source_target_pairs={{0,256},{256,0},{1,257},{257,1},{2,258},{258,2},{3,259},{259,3},{4... | collective-permute-start | bytes 1572872 | tf_op jit(solution)/shard_map/ppermute | solution.py:330
  187.8 0.8 maximum_bitcast_fusion
  188.6 7.2 %all-to-all-done.6 = f32[64,1,768]{2,1,0:T(1,128)S(1)} async-done(((f32[64,1,768]{2,1,0:T(1,128)}), f32[64,1,768]{2,1,0:T(1,128)S(1)}, u32[]{:S(2)}, u32[]{:S(2)}) %all-to-all-start.6) | async-done | bytes 196640 | tf_op jit(solution)/shard_map/all_to_all | solution.py:452
  195.8 0.5 multiply_reduce_fusion
  196.4 0.1 mul.11
  196.5 0.1 copy.20
  196.6 0.7 reshape.43
  197.3 0.6 broadcast_in_dim_reshape_squeeze.3
  198.0 0.1 broadcast_select_fusion.1
  198.1 1.1 pad_maximum_fusion
  (54 shorter events, 0.3 us)
Async XLA Ops:
  7.2 26.2 %copy-start.29 = (bf16[1,2048]{1,0:T(2,128)(2,1)S(1)}, bf16[1,2048]{1,0:T(2,128)(2,1)}, u32[]{:S(2)}) copy-start(bf16[1,2048]{1,0:T(2,128)(2,1)} %param.19) | copy-start | bytes 12292
  7.2 26.3 %copy-start.23 = (bf16[1,16,1024]{2,1,0:T(8,128)(2,1)S(1)}, bf16[1,16,1024]{2,1,0:T(8,128)(2,1)}, u32[]{:S(2)}) copy-start(bf16[1,16,1024]{2,1,0:T(8,128)(2,1)} %param.22) | copy-start | bytes 98308
  7.2 26.3 %copy-start.22 = (bf16[1,2048,16]{1,2,0:T(8,128)(2,1)S(1)}, bf16[1,2048,16]{1,2,0:T(8,128)(2,1)}, u32[]{:S(2)}) copy-start(bf16[1,2048,16]{1,2,0:T(8,128)(2,1)} %param.21) | copy-start | bytes 196612
  7.2 26.3 %copy-start.19 = (bf16[1,2,128,256]{3,2,1,0:T(8,128)(2,1)S(1)}, bf16[1,2,128,256]{3,2,1,0:T(8,128)(2,1)}, u32[]{:S(2)}) copy-start(bf16[1,2,128,256]{3,2,1,0:T(8,128)(2,1)} %param.18) | copy-start | bytes 393220
  7.2 26.3 %copy-start.4 = (bf16[1,2,128,2048]{3,2,1,0:T(8,128)(2,1)S(1)}, bf16[1,2,128,2048]{3,2,1,0:T(8,128)(2,1)}, u32[]{:S(2)}) copy-start(bf16[1,2,128,2048]{3,2,1,0:T(8,128)(2,1)} %param.17) | copy-start | bytes 3145732
  7.2 26.3 %copy-start.12 = (bf16[1,1,96,2048]{3,2,1,0:T(8,128)(2,1)S(1)}, bf16[1,1,96,2048]{3,2,1,0:T(8,128)(2,1)}, u32[]{:S(2)}) copy-start(bf16[1,1,96,2048]{3,2,1,0:T(8,128)(2,1)} %param.13) | copy-start | bytes 1179652
  7.2 85.3 %all-gather.2.cloned.1.call-start = ((), (), s32[]{:S(2)}) async-start(), calls=%async_computation.8 | async-start | bytes 4718592 | tf_op jit(solution)/shard_map/all_gather | solution.py:371
  8.3 30.7 %copy-start.26 = (s32[2,1]{0,1:T(1,128)S(1)}, s32[2,1]{0,1:T(1,128)}, u32[]{:S(2)}) copy-start(s32[2,1]{0,1:T(1,128)} %param.14) | copy-start | bytes 28
  8.4 30.7 %copy-start.27 = (s32[2,1]{0,1:T(1,128)S(1)}, s32[2,1]{0,1:T(1,128)}, u32[]{:S(2)}) copy-start(s32[2,1]{0,1:T(1,128)} %param.15) | copy-start | bytes 28
  8.4 30.7 %copy-start.28 = (s32[2,1]{0,1:T(1,128)S(1)}, s32[2,1]{0,1:T(1,128)}, u32[]{:S(2)}) copy-start(s32[2,1]{0,1:T(1,128)} %param.16) | copy-start | bytes 28
  34.1 4.9 %collective-permute-start = (bf16[432,1024]{1,0:T(8,128)(2,1)S(1)}, bf16[432,1024]{1,0:T(8,128)(2,1)S(1)}, u32[]{:S(2)}, u32[]{:S(2)}) collective-permute-start(bf16[432,1024]{1,0:T(8,128)(2,1)S(1)} %pack.1), channel_id=1, source_target_pairs={{0,256},{256,0},{1,257},{257,1},{2,258},{258,2},{3,259},{259,3},{4... | collective-permute-start | bytes 2654216 | tf_op jit(solution)/shard_map/ppermute | solution.py:330
  39.1 1.0 copy-start.13
  40.1 1.2 copy-start.14
  41.3 1.2 copy-start.15
  42.5 0.8 copy-start.24
  45.9 15.6 %copy-start.17 = (bf16[256,1024]{1,0:T(8,128)(2,1)}, bf16[256,1024]{1,0:T(8,128)(2,1)S(1)}, u32[]{:S(2)}) copy-start(bf16[256,1024]{1,0:T(8,128)(2,1)S(1)} %get-tuple-element.37.cotangent_half) | copy-start | bytes 1572868
  61.9 34.7 %copy-start.7 = (bf16[256,1024]{1,0:T(8,128)(2,1)}, bf16[256,1024]{1,0:T(8,128)(2,1)S(1)}, u32[]{:S(2)}) copy-start(bf16[256,1024]{1,0:T(8,128)(2,1)S(1)} %get-tuple-element.31.normed.normed_0) | copy-start | bytes 1572868
  61.9 39.6 %copy-start.5 = (bf16[256,1024]{1,0:T(8,128)(2,1)}, bf16[256,1024]{1,0:T(8,128)(2,1)S(1)}, u32[]{:S(2)}) copy-start(bf16[256,1024]{1,0:T(8,128)(2,1)S(1)} %get-tuple-element.33.full_gradient) | copy-start | bytes 1572868
  92.6 2.2 %copy-start = (bf16[8,2,128,1024]{3,2,1,0:T(8,128)(2,1)S(1)}, bf16[8,2,128,1024]{3,2,1,0:T(8,128)(2,1)}, u32[]{:S(2)}) copy-start(bf16[8,2,128,1024]{3,2,1,0:T(8,128)(2,1)} %all-gather.2.cloned.1.call-done.columns) | copy-start | bytes 12582916
  96.6 14.4 %all-to-all-start.2 = ((bf16[8,256,128]{2,1,0:T(8,128)(2,1)}), bf16[8,256,128]{2,1,0:T(8,128)(2,1)}, u32[]{:S(2)}, u32[]{:S(2)}) async-start(bf16[8,256,128]{2,1,0:T(8,128)(2,1)} %values_0.1), calls=%async_computation.2 | async-start | bytes 1048576 | tf_op jit(solution)/shard_map/all_to_all | solution.py:334
  101.5 2.2 %copy-start.1 = (bf16[8,2,128,1024]{3,2,1,0:T(8,128)(2,1)S(1)}, bf16[8,2,128,1024]{3,2,1,0:T(8,128)(2,1)}, u32[]{:S(2)}) copy-start(bf16[8,2,128,1024]{3,2,1,0:T(8,128)(2,1)} %all-gather.2.cloned.1.call-done.columns) | copy-start | bytes 12582916
  111.0 11.6 %copy-start.18 = (bf16[256,1024]{1,0:T(8,128)(2,1)S(1)}, bf16[256,1024]{1,0:T(8,128)(2,1)}, u32[]{:S(2)}) copy-start(bf16[256,1024]{1,0:T(8,128)(2,1)} %copy-done.17) | copy-start | bytes 1572868
  123.4 0.8 copy-start.9
  124.2 0.8 copy-start.16
  125.0 0.8 copy-start.20
  125.9 14.6 %all-to-all-start.4 = ((bf16[8,320,128]{2,1,0:T(8,128)(2,1)}), bf16[8,320,128]{2,1,0:T(8,128)(2,1)S(1)}, u32[]{:S(2)}, u32[]{:S(2)}) async-start(bf16[8,320,128]{2,1,0:T(8,128)(2,1)} %copy-done.16), calls=%async_computation.5 | async-start | bytes 1310720 | tf_op jit(solution)/shard_map/all_to_all | solution.py:334
  129.7 54.2 %reduce-scatter.2.cloned.1.call-start = ((), (), s32[]{:S(2)}) async-start(), calls=%async_computation.9 | async-start | bytes 589824 | tf_op jit(solution)/shard_map/reduce_scatter | solution.py:438
  129.7 2.2 %copy-start.2 = (bf16[8,2,128,1024]{3,2,1,0:T(8,128)(2,1)S(1)}, bf16[8,2,128,1024]{3,2,1,0:T(8,128)(2,1)}, u32[]{:S(2)}) copy-start(bf16[8,2,128,1024]{3,2,1,0:T(8,128)(2,1)} %all-gather.2.cloned.1.call-done.columns) | copy-start | bytes 12582916
  131.9 1.0 copy-start.10
  140.5 1.0 copy-start.6
  141.5 1.0 copy-start.8
  142.5 1.0 copy-start.11
  144.9 2.2 %copy-start.3 = (bf16[8,2,128,1024]{3,2,1,0:T(8,128)(2,1)S(1)}, bf16[8,2,128,1024]{3,2,1,0:T(8,128)(2,1)}, u32[]{:S(2)}) copy-start(bf16[8,2,128,1024]{3,2,1,0:T(8,128)(2,1)} %all-gather.2.cloned.1.call-done.columns) | copy-start | bytes 12582916
  147.1 1.0 copy-start.21
  149.9 14.0 %collective-permute-start.2 = (bf16[96,1024]{1,0:T(8,128)(2,1)S(1)}, bf16[96,1024]{1,0:T(8,128)(2,1)S(1)}, u32[]{:S(2)}, u32[]{:S(2)}) collective-permute-start(bf16[96,1024]{1,0:T(8,128)(2,1)S(1)} %select_bitcast_fusion), channel_id=1, source_target_pairs={{0,256},{256,0},{1,257},{257,1},{2,258},{258,2},{3,259},{259,3},{4... | collective-permute-start | bytes 589832 | tf_op jit(solution)/shard_map/ppermute | solution.py:330
  153.1 25.3 %all-to-all-start.5 = ((f32[128,1,384]{2,1,0:T(1,128)}), f32[128,1,384]{2,1,0:T(1,128)S(1)}, u32[]{:S(2)}, u32[]{:S(2)}) async-start(f32[128,1,384]{2,1,0:T(1,128)} %copy.19), calls=%async_computation.6 | async-start | bytes 393216 | tf_op jit(solution)/shard_map/all_to_all | solution.py:448
  179.2 16.6 %all-to-all-start.6 = ((f32[64,1,768]{2,1,0:T(1,128)}), f32[64,1,768]{2,1,0:T(1,128)S(1)}, u32[]{:S(2)}, u32[]{:S(2)}) async-start(f32[64,1,768]{2,1,0:T(1,128)} %broadcast_in_dim.31), calls=%async_computation.7 | async-start | bytes 393216 | tf_op jit(solution)/shard_map/all_to_all | solution.py:452
  183.8 0.8 copy-start.25
  185.0 12.9 %collective-permute-start.1 = (bf16[256,1024]{1,0:T(8,128)(2,1)S(1)}, bf16[256,1024]{1,0:T(8,128)(2,1)S(1)}, u32[]{:S(2)}, u32[]{:S(2)}) collective-permute-start(bf16[256,1024]{1,0:T(8,128)(2,1)S(1)} %broadcast_select_fusion.2), channel_id=1, source_target_pairs={{0,256},{256,0},{1,257},{257,1},{2,258},{258,2},{3,259},{259,3},{4... | collective-permute-start | bytes 1572872 | tf_op jit(solution)/shard_map/ppermute | solution.py:330
Sparse Core Ops, SparseCore 0:
  33.5 59.0 all-gather.1
  134.9 35.9 reduce-scatter.1

commit v2 on v1

v2 whole, which is shorter than its diff:
```python
import functools
import math

import jax
import jax.numpy as jnp
from jax import lax
from jax.experimental import pallas as pl
from jax.experimental.pallas import tpu as pltpu
from jax.sharding import PartitionSpec as P

MODEL_WIDTH = 8192
HD = 128
TOKT = 32
ADAPTER_SCALE = 0.5
EPS = 1e-06

SEQ = 128
MB = 2
ROWS = MB * SEQ
VIS = 96
RANK = 16
HEADS = 8
HALF = HEADS * HD
KVH = 8
PEERS = 8
VMEM_BYTES = 60 * 1024 * 1024

BF = jnp.bfloat16
F32 = jnp.float32

R_VIS, R_Q, R_K, R_DN, R_UP, R_GN, R_END = 0, 96, 352, 384, 400, 416, 432
R_SUM, R_LOW, R_PAY = ROWS, ROWS + RANK, ROWS + RANK + 2 * RANK
SUBLANES = 8


def block_of(head):
    return (head % 2) * 4 + head // 2


def nt(left, right):
    return lax.dot_general(left, right, (((1,), (1,)), ((), ())), preferred_element_type=F32)


def tn(left, right):
    return lax.dot_general(left, right, (((0,), (0,)), ((), ())), preferred_element_type=F32)


def nn(left, right):
    return jnp.dot(left, right, preferred_element_type=F32)


def stack_heads(block):
    return jnp.concatenate([block[:, h * HD : (h + 1) * HD] for h in range(HEADS)], axis=0)


def unstack_heads(block):
    return jnp.concatenate([block[h * SEQ : (h + 1) * SEQ, :] for h in range(HEADS)], axis=1)


def columns_to_rows(*columns):
    lane = lax.broadcasted_iota(jnp.int32, (ROWS, HD), 1)
    square = jnp.zeros((ROWS, HD), F32)
    for at, column in enumerate(columns):
        square = jnp.where(lane == at, column, square)
    return square.T[:SUBLANES, :]


def rows_to_columns(rows):
    padded = jnp.concatenate([rows, jnp.zeros((HD - SUBLANES, ROWS), F32)], axis=0)
    return padded.T


def payload_block(values, column, low_rank):
    row = columns_to_rows(column)[0:1, :]
    high = row.astype(BF).astype(F32)
    low = row - high
    at = lax.broadcasted_iota(jnp.int32, (RANK, HD), 0)
    sums = jnp.zeros((RANK, HD), F32)
    for index, part in enumerate((high[:, :HD], high[:, HD:], low[:, :HD], low[:, HD:])):
        sums = jnp.where(at == index, part, sums)
    low_rank = low_rank.astype(BF)
    return jnp.concatenate(
        [values, sums.astype(BF), low_rank[:, :HD], low_rank[:, HD:]], axis=0
    )


def total_of_payloads(blocks):
    sums = blocks[0, R_SUM:R_LOW, :].astype(F32)
    low_rank = blocks[0, R_LOW:, :].astype(F32)
    for peer in range(1, PEERS):
        sums = sums + blocks[peer, R_SUM:R_LOW, :].astype(F32)
        low_rank = low_rank + blocks[peer, R_LOW:, :].astype(F32)
    left = sums[0:1, :] + sums[2:3, :]
    right = sums[1:2, :] + sums[3:4, :]
    row = jnp.concatenate([left, right], axis=1)
    at = lax.broadcasted_iota(jnp.int32, (SUBLANES, ROWS), 0)
    rows = jnp.where(at == 0, row, 0.0)
    return rows, jnp.concatenate([low_rank[:RANK, :], low_rank[RANK:, :]], axis=1)


def inverse_of(squares):
    return lax.rsqrt(squares / MODEL_WIDTH + EPS)


class Loaded:
    def __init__(self, buffer, copies):
        self.buffer, self.copies, self.done = buffer, copies, set()
        for copy in copies:
            copy.start()

    def __call__(self, part=None):
        for at in range(len(self.copies)) if part is None else (part,):
            if at not in self.done:
                self.copies[at].wait()
                self.done.add(at)
        return self.buffer


class Stored:
    def __init__(self, buffer, target, semaphores):
        self.buffer, self.target, self.semaphores, self.copies = buffer, target, semaphores, []

    def send(self, block=None):
        at = self.semaphores.at[len(self.copies)]
        pair = (self.buffer, self.target)
        if block is not None:
            pair = (self.buffer.at[block], self.target.at[block])
        copy = pltpu.make_async_copy(*pair, at)
        copy.start()
        self.copies.append(copy)

    def finish(self):
        if not self.copies:
            self.send()
        for copy in self.copies:
            copy.wait()


def whole(scalars, ref, buffer):
    return [(ref, buffer)]


def layer_of(layer):
    return lambda scalars, ref, buffer: [(ref.at[layer], buffer)]


def half_of(other, width, rank=2):
    def view(scalars, ref, buffer):
        core = scalars[0][0]
        core = 1 - core if other else core
        part = pl.ds(pl.multiple_of(core * width, width), width)
        return [((ref.at[:, part] if rank == 2 else ref.at[:, :, part]), buffer)]

    return view


def columns_of(layer):
    def view(scalars, ref, buffer):
        pairs = [pl.ds(2 * at, 2) for at in range(KVH // 2)]
        return [(ref.at[pair, layer], buffer.at[pair]) for pair in pairs]

    return view


def call(kernel, name, results, scalars, operands, after=()):
    operands = [o if isinstance(o, tuple) else (o, o.shape, whole) for o in operands]
    arrays = [o[0] for o in operands]
    n_scalars, n_arrays, n_after, n_results = len(scalars), len(arrays), len(after), len(results)
    most = KVH // 2

    def body(*refs):
        refs = list(refs)
        scalar_refs = [refs.pop(0) for _ in range(n_scalars)]
        array_refs = [refs.pop(0) for _ in range(n_arrays)]
        del refs[:n_after]
        targets = [refs.pop(0) for _ in range(n_results)]
        buffers = [refs.pop(0) for _ in range(n_arrays)]
        out_buffers = [refs.pop(0) for _ in range(n_results)]
        in_semaphores, out_semaphores = refs
        loads = []
        for at, ref in enumerate(array_refs):
            pairs = operands[at][2](scalar_refs, ref, buffers[at])
            copies = [
                pltpu.make_async_copy(*pair, in_semaphores.at[at * most + k])
                for k, pair in enumerate(pairs)
            ]
            loads.append(Loaded(buffers[at], copies))
        stores = [
            Stored(out_buffers[at], targets[at], out_semaphores.at[at]) for at in range(n_results)
        ]
        kernel(*scalar_refs, *loads, *stores)
        for load in loads:
            load()
        for store in stores:
            store.finish()

    moved = sum(math.prod(o[1]) * o[0].dtype.itemsize for o in operands)
    moved += sum(math.prod(shape) * jnp.dtype(dtype).itemsize for shape, dtype in results)
    anywhere = pl.BlockSpec(memory_space=pltpu.HBM)
    return pl.pallas_call(
        body,
        out_shape=[jax.ShapeDtypeStruct(shape, dtype) for shape, dtype in results],
        in_specs=[pl.BlockSpec(memory_space=pltpu.SMEM)] * n_scalars
        + [anywhere] * (n_arrays + n_after),
        out_specs=[anywhere] * n_results,
        scratch_shapes=[pltpu.VMEM(o[1], o[0].dtype) for o in operands]
        + [pltpu.VMEM(shape, dtype) for shape, dtype in results]
        + [
            pltpu.SemaphoreType.DMA((n_arrays * most,)),
            pltpu.SemaphoreType.DMA((n_results, PEERS)),
        ],
        compiler_params=pltpu.CompilerParams(vmem_limit_bytes=VMEM_BYTES),
        cost_estimate=pl.CostEstimate(flops=0, bytes_accessed=moved, transcendentals=0),
        name=name,
    )(*scalars, *arrays, *after)


def send_to_all(payload, block):
    for peer in range(PEERS):
        payload.buffer[peer] = block
    payload.send()


def pack_kernel(core, visual, queries, keys, down, up, gain, packed):
    out = packed.buffer
    out[R_DN:R_UP, :] = down()[...]
    out[R_UP:R_GN, :] = up()[...]
    out[R_GN:R_END, :] = gain()[...]
    for j in range(8):
        out[R_K:R_DN, j * HD : (j + 1) * HD] = keys()[j * 32 : (j + 1) * 32, :]
    out[R_VIS:R_Q, :] = visual()[...]
    out[R_Q:R_K, :] = queries()[...]


def softmax_of(query_rows, key_rows, length):
    scores = nt(stack_heads(query_rows), key_rows) / math.sqrt(HD)
    shape = scores.shape
    row = lax.rem(lax.broadcasted_iota(jnp.int32, shape, 0), SEQ)
    column = lax.broadcasted_iota(jnp.int32, shape, 1)
    allowed = (column <= row) & (column < length)
    scores = jnp.where(allowed, scores, -jnp.inf)
    top = jnp.max(scores, axis=-1, keepdims=True)
    weights = jnp.exp(scores - top)
    return (weights / jnp.sum(weights, axis=-1, keepdims=True)).astype(BF)


def prepare_kernel(
    core, counts, starts, lengths,
    received, visual, queries, keys, down, up, gain, embeddings, cotangent,
    weights, entry, cotangent_half, downs, ups, gains, payload,
):
    own = core[0]
    other = 1 - own
    got = received()
    downs.buffer[own] = down()[...]
    downs.buffer[other] = got[R_DN:R_UP, :]
    ups.buffer[own] = up()[...]
    ups.buffer[other] = got[R_UP:R_GN, :]
    gains.buffer[own] = gain()[...]
    gains.buffer[other] = got[R_GN:R_END, :]
    for small in (downs, ups, gains):
        small.send()
    position = lax.broadcasted_iota(jnp.int32, (SEQ, VIS), 0)
    slot = lax.broadcasted_iota(jnp.int32, (SEQ, VIS), 1)
    place = lax.broadcasted_iota(jnp.int32, (SEQ, 1), 0)
    for index, table in ((own, visual()[...]), (other, got[R_VIS:R_Q, :])):
        begin = starts[index]
        count = counts[index] * TOKT
        placing = ((position == begin + slot) & (slot < count)).astype(F32).astype(BF)
        inserted = nn(placing, table).astype(BF)
        covered = (place >= begin) & (place < begin + count)
        rows = pl.ds(pl.multiple_of(index * SEQ, SEQ), SEQ)
        entry.buffer[rows, :] = jnp.where(covered, inserted, embeddings()[index])
    entry.send()
    for m in range(MB):
        rows = slice(m * SEQ, (m + 1) * SEQ)
        cotangent_half.buffer[rows, :] = cotangent()[m]
        weights.buffer[own, m] = softmax_of(queries()[rows, :], keys()[rows, :], lengths[m])
        other_keys = jnp.concatenate(
            [got[R_K:R_DN, j * HD : (j + 1) * HD] for j in range(4 * m, 4 * m + 4)], axis=0
        )
        weights.buffer[other, m] = softmax_of(
            got[R_Q + m * SEQ : R_Q + (m + 1) * SEQ, :], other_keys, lengths[m]
        )
    cotangent_half.send()
    weights.send()
    value_gradient = jnp.concatenate(
        [tn(weights.buffer[1, m], stack_heads(cotangent()[m])) for m in range(MB)], axis=0
    ).astype(BF)
    entry_float = entry.buffer[...].astype(F32)
    squares = jnp.sum(entry_float * entry_float, axis=-1, keepdims=True)
    gained = (entry_float * gains.buffer[0][0:1, :].astype(F32)).astype(BF)
    send_to_all(payload, payload_block(value_gradient, squares, nt(downs.buffer[0], gained)))


def entry_norm_kernel(
    received, entry, ups, gains, normed, inverse, adapter_rows, full_gradient, lora_gradient
):
    got = received()
    rows, low_rank = total_of_payloads(got)
    column = inverse_of(rows_to_columns(rows)[:, 0:1])
    inverse.buffer[...] = jnp.broadcast_to(column, (ROWS, HD))
    adapter_rows.buffer[...] = low_rank * inverse_of(rows[0:1, :])
    gain = gains()[0:1, :].astype(F32)
    normed.buffer[...] = (entry()[...].astype(F32) * column * gain).astype(BF)
    for head in range(KVH):
        full_gradient.buffer[:, head * HD : (head + 1) * HD] = got[block_of(head), :ROWS, :]
    lora_gradient.buffer[...] = ADAPTER_SCALE * nt(ups()[...], full_gradient.buffer[...])


def values_kernel(normed, downs, ups, columns, out):
    rows = normed()[...]
    adapter = (ADAPTER_SCALE * nt(rows, downs()[...])).astype(BF)
    ups()
    for pair in range(KVH // 2):
        weight = columns(pair)[2 * pair : 2 * pair + 2].reshape(2 * HD, HALF)
        up = ups()[:, 2 * pair * HD : (2 * pair + 2) * HD]
        partial = (nt(rows, weight) + nn(adapter, up)).astype(BF)
        for at in range(2):
            block = block_of(2 * pair + at)
            out.buffer[block] = partial[:, at * HD : (at + 1) * HD]
            out.send(block)


def weighted_gradient(full_gradient, lora_gradient, downs, gains, columns):
    grad = tn(lora_gradient.astype(BF), downs()[...])
    for pair in range(KVH // 2):
        weight = columns(pair)[2 * pair : 2 * pair + 2].reshape(2 * HD, HALF)
        grad = grad + nn(full_gradient[:, 2 * pair * HD : (2 * pair + 2) * HD], weight)
    return grad * gains()[0:1, :].astype(F32)


def scaled_kernel(full_gradient, lora_gradient, downs, gains, columns, scaled):
    scaled.buffer[...] = weighted_gradient(
        full_gradient()[...], lora_gradient()[...], downs, gains, columns
    )


def attended_rows(weights, value_rows):
    return jnp.concatenate(
        [
            unstack_heads(nn(weights[m], value_rows[m * SEQ : (m + 1) * SEQ, :]))
            for m in range(MB)
        ],
        axis=0,
    )


def first_output_kernel(received, weights, entry, scaled, hidden, value_rows, payload):
    got = received()
    values = got[0].astype(F32)
    for peer in range(1, PEERS):
        values = values + got[peer].astype(F32)
    value_rows.buffer[...] = values
    value_rows.send()
    attended = attended_rows(weights(), values.astype(BF))
    output = (entry()[...].astype(F32) + attended).astype(BF)
    hidden.buffer[...] = output
    hidden.send()
    output_float = output.astype(F32)
    squares = jnp.sum(output_float * output_float, axis=-1, keepdims=True)
    dots = jnp.sum(output_float * scaled()[...], axis=-1, keepdims=True)
    send_to_all(payload, columns_to_rows(squares, dots))


def first_gradient_kernel(
    received, hidden, scaled, cotangent_half, weights, value_rows, gains, downs,
    gradient, normed, inverse_row, payload,
):
    got = received()
    total = got[0]
    for peer in range(1, PEERS):
        total = total + got[peer]
    sums = rows_to_columns(total)
    column = inverse_of(sums[:, 0:1])
    factor = column * column * column * sums[:, 1:2] / MODEL_WIDTH
    inverse_row.buffer[...] = inverse_of(total)
    hidden_float = hidden()[...].astype(F32)
    grad = (
        cotangent_half()[...].astype(F32) + column * scaled()[...] - hidden_float * factor
    ).astype(BF)
    gradient.buffer[...] = grad
    gradient.send()
    gained = hidden_float * gains()[0:1, :].astype(F32)
    low_rank = nt(downs()[...], gained.astype(BF))
    value_gradient = jnp.concatenate(
        [tn(weights()[m], stack_heads(grad[m * SEQ : (m + 1) * SEQ, :])) for m in range(MB)],
        axis=0,
    ).astype(BF)
    dots = jnp.sum(value_gradient.astype(F32) * value_rows()[...], axis=-1, keepdims=True)
    send_to_all(payload, payload_block(value_gradient, dots, low_rank))
    normed.buffer[...] = (gained * column).astype(BF)


def map_chunks(down_gradient, up_gradient):
    quarter = HALF // 4
    left = jnp.concatenate(
        [down_gradient[:, q * quarter : (q + 1) * quarter] for q in range(4)], axis=0
    )
    right = jnp.concatenate([up_gradient, jnp.zeros((3 * RANK, HD), F32)], axis=0)
    return jnp.concatenate([left, right], axis=1)


def map_gradient_kernel(
    core, received, ups, normed_0, adapter_0, normed_1, inverse_row, gradient_1, lora_gradient_1,
    last_gradient, lora_gradient_0, column_sum, out,
):
    own = core[0] * 4 + core[1]
    got = received()
    for head in range(KVH):
        last_gradient.buffer[:, head * HD : (head + 1) * HD] = got[block_of(head), :ROWS, :]
    last_gradient.send()
    rows, low_rank = total_of_payloads(got)
    column_sum.buffer[...] = rows_to_columns(rows)
    lora_0 = ADAPTER_SCALE * nt(ups()[...], last_gradient.buffer[...])
    lora_gradient_0.buffer[...] = lora_0
    down_0 = nn(lora_0.astype(BF), normed_0()[...])
    up_0 = ADAPTER_SCALE * nn(adapter_0()[...].astype(BF), got[own, :ROWS, :])
    out.buffer[0] = map_chunks(down_0, up_0)
    down_1 = nn(lora_gradient_1()[...].astype(BF), normed_1()[...])
    adapter_1 = (low_rank * inverse_row()[0:1, :]).astype(BF)
    up_1 = ADAPTER_SCALE * nn(adapter_1, gradient_1()[...])
    out.buffer[1] = map_chunks(down_1, up_1)


def slot_gradient_kernel(
    counts, starts,
    last_gradient, lora_gradient, downs, gains, columns, entry, inverse, gradient, column_sum,
    slots,
):
    scaled = weighted_gradient(last_gradient()[...], lora_gradient()[...], downs, gains, columns)
    column = inverse()[:, 0:1]
    factor = column * column * column_sum()[:, 0:1] / MODEL_WIDTH
    rows = (
        gradient()[...].astype(F32) + column * scaled - entry()[...].astype(F32) * factor
    ).astype(BF)
    slot = lax.broadcasted_iota(jnp.int32, (VIS, SEQ), 0)
    position = lax.broadcasted_iota(jnp.int32, (VIS, SEQ), 1)
    for m in range(MB):
        picking = ((position == starts[m] + slot) & (slot < counts[m] * TOKT)).astype(F32).astype(BF)
        slots.buffer[m] = nn(picking, rows[m * SEQ : (m + 1) * SEQ, :]).astype(BF)


def second_output_kernel(values, weights, hidden, out):
    attended = attended_rows(weights(), values()[...])
    out.buffer[...] = (hidden()[...].astype(F32) + attended).astype(BF)


def maps_kernel(arrived, down_sum, up_sum, *, scale):
    rows = arrived()[...].reshape(4 * RANK, 2 * (HALF // 4 + HD)) * scale
    quarter, width = HALF // 4, HALF // 4 + HD
    for half in range(2):
        for q in range(4):
            to = half * HALF + q * quarter
            down_sum.buffer[:, to : to + quarter] = rows[
                q * RANK : (q + 1) * RANK, half * width : half * width + quarter
            ]
        up_sum.buffer[:, half * HD : (half + 1) * HD] = rows[
            :RANK, half * width + quarter : (half + 1) * width
        ]


def swap_cores(block):
    return lax.ppermute(block, "section", [(0, 1), (1, 0)])


def to_heads(block):
    return lax.all_to_all(block, ("section", "tp"), 0, 0)


def on_device(
    embeddings,
    visual,
    image_block_count,
    starts,
    lengths,
    queries,
    layer_key_vectors,
    input_norm_gain,
    frozen_value_weight,
    adapter_down_map,
    adapter_up_map,
    cotangent,
):
    section = lax.axis_index("section")
    tp = lax.axis_index("tp")
    n_fsdp = lax.axis_size("fsdp")
    n_y = n_fsdp // KVH
    core = jnp.stack([section, tp]).astype(jnp.int32)
    counts = image_block_count[:, 0]
    begins = starts[:, 0]
    seq_lengths = lengths[:, 0]

    shard = frozen_value_weight[0].T
    pieces = shard.reshape(shard.shape[0], 2, HALF).transpose(1, 0, 2)
    pieces = jnp.broadcast_to(pieces[:, None], (2, n_y) + pieces.shape[1:])
    pieces = pieces.reshape((2 * n_y,) + pieces.shape[2:])
    head_groups = [
        [s * n_fsdp + z * n_y + y for s in range(2) for y in range(n_y)] for z in range(KVH)
    ]
    head_columns = lax.all_to_all(
        pieces, ("section", "fsdp"), 0, 0, axis_index_groups=head_groups
    ).reshape(2, HD, HALF)
    row_groups = [[z * n_y + y for z in range(KVH)] for y in range(n_y)]
    columns = lax.all_gather(head_columns, "fsdp", axis=0, axis_index_groups=row_groups)

    def own(other):
        return (
            (visual[0, 0], (VIS, HALF), half_of(other, HALF)),
            (queries[0].reshape(ROWS, 2 * HALF), (ROWS, HALF), half_of(other, HALF)),
            (layer_key_vectors[0].reshape(ROWS, 2 * HD), (ROWS, HD), half_of(other, HD)),
            (adapter_down_map[0].T, (RANK, HALF), half_of(other, HALF)),
            adapter_up_map[0],
            (gain_rows, (RANK, HALF), half_of(other, HALF)),
        )

    gain_rows = jnp.broadcast_to(input_norm_gain, (RANK, 2 * HALF))
    (packed,) = call(pack_kernel, "pack", [((R_END, HALF), BF)], (core,), own(True))

    wide = ((ROWS, HALF), BF)
    low = ((RANK, ROWS), F32)
    lanes = ((ROWS, HD), F32)
    maps = ((2, RANK, HALF), BF)
    blocks = ((PEERS, ROWS, HD), BF)
    mixed = ((PEERS, R_PAY, HD), BF)
    half_rows = ((MB, SEQ, HALF), half_of(False, HALF, 3))
    weights, entry, cotangent_half, downs, ups, gains, payload = call(
        prepare_kernel,
        "prepare",
        [((2, MB, HEADS * SEQ, SEQ), BF), wide, wide, maps, maps, maps, mixed],
        (core, counts, begins, seq_lengths),
        (swap_cores(packed), *own(False), (embeddings, *half_rows), (cotangent, *half_rows)),
    )

    def at(layer, array):
        return (array, array.shape[1:], layer_of(layer))

    def weight_of(layer):
        return (columns, (KVH, HD, HALF), columns_of(layer))

    normed_0, inverse_0, adapter_0, gradient_values_1, lora_gradient_1 = call(
        entry_norm_kernel,
        "entry_norm",
        [wide, lanes, low, wide, low],
        (),
        (to_heads(payload), entry, at(1, ups), at(0, gains)),
    )
    (partial_0,) = call(
        values_kernel, "values_0", [blocks], (), (normed_0, at(0, downs), at(0, ups), weight_of(0))
    )
    (scaled_1,) = call(
        scaled_kernel,
        "scaled_1",
        [((ROWS, HALF), F32)],
        (),
        (gradient_values_1, lora_gradient_1, at(1, downs), at(1, gains), weight_of(1)),
    )
    hidden_0, value_rows, payload = call(
        first_output_kernel,
        "first_output",
        [wide, lanes, ((PEERS, SUBLANES, ROWS), F32)],
        (),
        (to_heads(partial_0), at(0, weights), entry, scaled_1),
    )
    gradient, normed_1, inverse_row, payload = call(
        first_gradient_kernel,
        "first_gradient",
        [wide, wide, ((SUBLANES, ROWS), F32), mixed],
        (),
        (
            to_heads(payload),
            hidden_0,
            scaled_1,
            cotangent_half,
            at(0, weights),
            value_rows,
            at(1, gains),
            at(1, downs),
        ),
    )
    gathered = to_heads(payload)
    (partial_1,) = call(
        values_kernel, "values_1", [blocks], (), (normed_1, at(1, downs), at(1, ups), weight_of(1))
    )
    values_1 = lax.psum_scatter(partial_1, ("section", "tp"), scatter_dimension=0)

    def own_columns(scalars, ref, buffer):
        head = 2 * scalars[0][1] + scalars[0][0]
        return [(ref.at[:, pl.ds(pl.multiple_of(head * HD, HD), HD)], buffer)]

    width = HALF // 4 + HD
    last_gradient, lora_gradient_0, column_sum, chunks = call(
        map_gradient_kernel,
        "map_gradient",
        [wide, low, lanes, ((2, 4 * RANK, width), F32)],
        (core,),
        (
            gathered,
            at(0, ups),
            normed_0,
            adapter_0,
            normed_1,
            inverse_row,
            (gradient_values_1, (ROWS, HD), own_columns),
            lora_gradient_1,
        ),
    )
    arrived = lax.all_to_all(
        chunks.reshape(2 * n_fsdp, 1, width), ("section", "fsdp"), 0, 0
    ).reshape(2, n_fsdp, width)
    summed = jnp.sum(arrived, axis=1).reshape(1, 1, 2 * width)
    everywhere = lax.all_to_all(
        jnp.broadcast_to(summed, (n_fsdp, 1, 2 * width)), "fsdp", 0, 0
    )
    down_sum, up_sum = call(
        functools.partial(maps_kernel, scale=1.0 / math.sqrt(MB * SEQ * n_fsdp)),
        "maps",
        [((RANK, 2 * HALF), F32), ((RANK, 2 * HD), F32)],
        (),
        (everywhere,),
    )

    (slots,) = call(
        slot_gradient_kernel,
        "slot_gradient",
        [((MB, VIS, HALF), BF)],
        (counts, begins),
        (
            last_gradient,
            lora_gradient_0,
            at(0, downs),
            at(0, gains),
            weight_of(0),
            entry,
            inverse_0,
            gradient,
            column_sum,
        ),
        after=(summed,),
    )
    (hidden_1,) = call(
        second_output_kernel,
        "second_output",
        [wide],
        (),
        (values_1, at(1, weights), hidden_0),
        after=(summed,),
    )

    first = section == 0

    def halves(mine, theirs):
        left = jnp.where(first, mine, theirs)
        right = jnp.where(first, theirs, mine)
        return jnp.concatenate([left, right], axis=-1)

    slot_rows = halves(
        jnp.where(first, slots[0], slots[1]), swap_cores(jnp.where(first, slots[1], slots[0]))
    )
    hidden = halves(
        jnp.where(first, hidden_0, hidden_1), swap_cores(jnp.where(first, hidden_1, hidden_0))
    )
    return (
        hidden.reshape(1, MB, SEQ, 2 * HALF),
        slot_rows[None, None],
        down_sum.T[None],
        up_sum[None],
    )


def solution(mesh):
    return jax.shard_map(
        on_device,
        mesh=mesh,
        in_specs=(
            P(None, "fsdp", "tp"),
            P("section", "fsdp", None, "tp"),
            P(None, "fsdp"),
            P(None, "fsdp"),
            P(None, "fsdp"),
            P("section", None, "fsdp", "tp"),
            P("section", None, "fsdp", "tp"),
            P("section", "tp"),
            P("section", "tp", "fsdp"),
            P("section", "tp", None),
            P("section", None, None),
            P(None, "fsdp", "tp"),
        ),
        out_specs=(
            P("section", None, "fsdp", "tp"),
            P("section", "fsdp", None, "tp"),
            P("section", "tp", None),
            P("section", None, "tp"),
        ),
        check_vma=False,
    )
```

time: 208 us -> 222 us (1.067)
  Pallas kernels: 14.1 us -> 50.3 us
  local copies, waits for them, and re-layouts: 25.8 us -> 8.06 us
  waiting for transfers between devices: 66.5 us -> 62.2 us
    pallas_call x11 -> x12, Pallas kernels: 14.1 us -> 50.3 us  [call(): pl.pallas_call(body, out_shape=[jax.ShapeDtypeStruct(shape, dtype) for sh...]
    unnamed x61 -> x17, local copies, waits for them, and re-layouts: 21.5 us -> 3.28 us
    all_gather x1, waiting for transfers between devices: 30.7 us -> 21.5 us  [on_device(): lax.all_gather(head_columns, 'fsdp', axis=0, axis_index_groups=row_groups)]
    all_to_all x1, waiting for transfers between devices: 7.25 us -> 11.9 us  [on_device(): lax.all_to_all(jnp.broadcast_to(summed, (n_fsdp, 1, 2 * width)), 'fsdp',...]
  transfers between devices with their start and end apart: 9 -> 9, of which waited for: 6 -> 6; matrix products, arithmetic and copies ran while one was open for 2% -> 3% of each run, Pallas kernels for 5% -> 17%
where the time goes in v2:
time: 222 us; the launch traced here: 221 us
  waiting for transfers between devices  62.2 us (28%)
  Pallas kernels  50.3 us (23%)
  blocking collectives  49.3 us (22%)
  starting transfers between devices  33.2 us (15%)
  between operations  14.3 us (6%)
  local copies, waits for them, and re-layouts  8.06 us (4%)
  other arithmetic  3.8 us (2%)
    pallas_call x12, Pallas kernels, call(): pl.pallas_call(body, out_shape=[jax.ShapeDtypeStruct(shape, dtype) for sh...  50.3 us
    all_to_all x1, blocking collectives, on_device(): lax.all_to_all(pieces, ('section', 'fsdp'), 0, 0, axis_index_groups=head_...  24.8 us
    all_to_all x2, blocking collectives, to_heads(): return lax.all_to_all(block, ('section', 'tp'), 0, 0)  24.5 us
    all_gather x1, waiting for transfers between devices, on_device(): lax.all_gather(head_columns, 'fsdp', axis=0, axis_index_groups=row_groups)  21.5 us
    all_to_all x1, waiting for transfers between devices, on_device(): lax.all_to_all(chunks.reshape(2 * n_fsdp, 1, width), ('section', 'fsdp'),...  14.3 us
    all_to_all x2, waiting for transfers between devices, to_heads(): return lax.all_to_all(block, ('section', 'tp'), 0, 0)  12.1 us
    all_to_all x1, waiting for transfers between devices, on_device(): lax.all_to_all(jnp.broadcast_to(summed, (n_fsdp, 1, 2 * width)), 'fsdp',...  11.9 us
    all_to_all x1, starting transfers between devices, on_device(): lax.all_to_all(chunks.reshape(2 * n_fsdp, 1, width), ('section', 'fsdp'),...  11.1 us
  transfers between devices with their start and end apart: 9, of which 6 were waited for; matrix products, arithmetic and copies ran while one was open for 3% of the time, Pallas kernels for 17%

profile of v2, /device:TPU:1, one launch (start us, length us, event | category | flops | bytes accessed | tf_op | source)
XLA Modules:
  0.0 221.2 jit_solution(10066052035344550023)
XLA Ops:
  7.2 0.0 copy-start.7
  7.2 0.0 all-gather.2.cloned.1.call-start
  7.2 0.9 reshape.34
  8.1 0.1 broadcast_in_dim.31
  8.2 24.8 %all_to_all.35 = bf16[16,16,1024]{2,1,0:T(8,128)(2,1)} all-to-all(bf16[16,16,1024]{2,1,0:T(8,128)(2,1)S(1)} %bitcast.36), channel_id=1, replica_groups={{0,4,8,12,16,20,24,28,256,260,264,268,272,276,280,284},{32,36,40,44,48,..., dimensions={0} | all-to-all | bytes 1048576 | tf_op jit(solution)/shard_map/all_to_all | solution.py:501
  33.0 0.0 all-gather.2.cloned.1.call-update
  33.0 0.0 copy-done.7
  33.1 0.6 pad_add_fusion.refs_0_
  33.7 0.6 broadcast_in_dim.30.refs_6_.refs_10_
  34.3 3.0 %pack.1 = bf16[432,1024]{1,0:T(8,128)(2,1)} custom-call(s32[2]{0:T(128)} %pad_add_fusion.refs_0_, bf16[96,2048]{1,0:T(8,128)(2,1)} %bitcast.37, bf16[256,2048]{1,0:T(8,128)(2,1)} %bitcast.33, bf16[256,256]{1,0:T(8,128)(2,1)} %bitcast.41, bf16[16,2048]{1,0:T(8,128)(2,1)} %bitcast.43, bf16[16,1024]{1,0:T(8,128)(2,1)} %bitcast.47, ...), custom_call_target="tpu_custom_call" | custom-call | bytes 1769472 | tf_op jit(solution)/shard_map/pack/pallas_call | solution.py:200
  37.3 2.9 %collective-permute-start = (bf16[432,1024]{1,0:T(8,128)(2,1)}, bf16[432,1024]{1,0:T(8,128)(2,1)S(1)}, u32[]{:S(2)}, u32[]{:S(2)}) collective-permute-start(bf16[432,1024]{1,0:T(8,128)(2,1)} %pack.1), channel_id=1, source_target_pairs={{0,256},{256,0},{1,257},{257,1},{2,258},{258,2},{3,259},{259,3},{4... | collective-permute-start | bytes 2654216 | tf_op jit(solution)/shard_map/ppermute | solution.py:464
  40.2 2.2 %collective-permute-done.refs_4_ = bf16[432,1024]{1,0:T(8,128)(2,1)S(1)} collective-permute-done((bf16[432,1024]{1,0:T(8,128)(2,1)}, bf16[432,1024]{1,0:T(8,128)(2,1)S(1)}, u32[]{:S(2)}, u32[]{:S(2)}) %collective-permute-start) | collective-permute-done | bytes 884768 | tf_op jit(solution)/shard_map/ppermute | solution.py:464
  42.5 0.0 copy-start.5
  42.5 0.9 copy-done.5
  43.4 6.6 %prepare.1 = (bf16[2,2,1024,128]{3,2,1,0:T(8,128)(2,1)}, bf16[256,1024]{1,0:T(8,128)(2,1)}, bf16[256,1024]{1,0:T(8,128)(2,1)}, bf16[2,16,1024]{2,1,0:T(8,128)(2,...) custom-call(s32[2]{0:T(128)} %pad_add_fusion.refs_0_, s32[2]{0:T(128)} %bitcast.51, ...), custom_call_target="tpu_custom_call" | custom-call | bytes 5734400 | tf_op jit(solution)/shard_map/prepare/pallas_call | solution.py:200
  50.0 15.2 %all_to_all.36.refs_0_ = bf16[8,304,128]{2,1,0:T(8,128)(2,1)} all-to-all(bf16[8,304,128]{2,1,0:T(8,128)(2,1)} %get-tuple-element.29), channel_id=1, replica_groups=mesh['section'=2,'fsdp'=64,'tp'=4] {'section','tp'}, dimensions={0} | all-to-all | bytes 1245184 | tf_op jit(solution)/shard_map/all_to_all | solution.py:468
  65.2 5.5 %entry_norm.1 = (bf16[256,1024]{1,0:T(8,128)(2,1)}, f32[256,128]{1,0:T(8,128)}, f32[16,256]{1,0:T(8,128)}, bf16[256,1024]{1,0:T(8,128)(2,1)}, f32[16,256]{1,0:T(8,128)}) custom-call(bf16[8,304,128]{2,1,0:T(8,128)(2,1)} %all_to_all.36.refs_0_, bf16[256,1024]{1,0:T(8,128)(2,1)} %get-tuple-element.30.refs_1_.refs_2_.refs_7_, ...), custom_call_target="tpu_custom_call" | custom-call | bytes 2424832 | tf_op jit(solution)/shard_map/entry_norm/pallas_call | solution.py:200
  70.7 21.5 %all-gather.2.cloned.1.call-done.refs_3_.refs_4_.refs_6_ = bf16[8,2,128,1024]{3,2,1,0:T(8,128)(2,1)} async-done(((bf16[1,2,128,1024]{3,2,1,0:T(8,128)(2,1)}), bf16[8,2,128,1024]{3,2,1,0:T(8,128)(2,1)}) %all-gather.2.cloned.1.call-update) | async-done | bytes 4194320 | tf_op jit(solution)/shard_map/all_gather | solution.py:505
  92.2 4.1 %values_0.1 = bf16[8,256,128]{2,1,0:T(8,128)(2,1)} custom-call(bf16[256,1024]{1,0:T(8,128)(2,1)} %get-tuple-element.33.refs_0_.refs_3_, bf16[2,16,1024]{2,1,0:T(8,128)(2,1)} %get-tuple-element.34.refs_1_.refs_2_.refs_7_.refs_4_, bf16[2,16,1024]{2,1,0:T(8,128)(2,1)} %get-tuple-element.31.refs_2_, ...), custom_call_target="tpu_custom_call" | custom-call | bytes 3211264 | tf_op jit(solution)/shard_map/values_0/pallas_call | solution.py:200
  96.3 4.9 %all-to-all-start.2 = ((bf16[8,256,128]{2,1,0:T(8,128)(2,1)}), bf16[8,256,128]{2,1,0:T(8,128)(2,1)S(1)}, u32[]{:S(2)}, u32[]{:S(2)}) async-start(bf16[8,256,128]{2,1,0:T(8,128)(2,1)} %values_0.1), calls=%async_computation.2 | async-start | bytes 1048576 | tf_op jit(solution)/shard_map/all_to_all | solution.py:468
  101.2 3.6 %scaled_1.1.refs_3_.refs_2_ = f32[256,1024]{1,0:T(8,128)} custom-call(bf16[256,1024]{1,0:T(8,128)(2,1)} %get-tuple-element.36.refs_0_.refs_7_, f32[16,256]{1,0:T(8,128)} %get-tuple-element.37.refs_1_.refs_8_, bf16[2,16,1024]{2,1,0:T(8,128)(2,1)} %get-tuple-element.34.refs_1_.refs_2_.refs_7_.refs_4_, ...), custom_call_target="tpu_custom_call" | custom-call | bytes 3751936 | tf_op jit(solution)/shard_map/scaled_1/pallas_call | solution.py:200
  104.8 5.8 %all-to-all-done.2.refs_0_ = bf16[8,256,128]{2,1,0:T(8,128)(2,1)S(1)} async-done(((bf16[8,256,128]{2,1,0:T(8,128)(2,1)}), bf16[8,256,128]{2,1,0:T(8,128)(2,1)S(1)}, u32[]{:S(2)}, u32[]{:S(2)}) %all-to-all-start.2) | async-done | bytes 524320 | tf_op jit(solution)/shard_map/all_to_all | solution.py:468
  110.6 0.0 copy-start.4
  110.6 0.8 copy-done.4
  111.4 2.9 %first_output.1 = (bf16[256,1024]{1,0:T(8,128)(2,1)}, f32[256,128]{1,0:T(8,128)}, f32[8,8,256]{2,1,0:T(8,128)}) custom-call(bf16[8,256,128]{2,1,0:T(8,128)(2,1)} %copy-done.4, bf16[2,2,1024,128]{3,2,1,0:T(8,128)(2,1)} %get-tuple-element.35.refs_1_.refs_4_, bf16[256,1024]{1,0:T(8,128)(2,1)} %get-tuple-element.30.refs_1_.refs_2_.refs_7_, ...), custom_call_target="tpu_custom_call" | custom-call | bytes 3342336 | tf_op jit(solution)/shard_map/first_output/pallas_call | solution.py:200
  114.3 9.3 %all_to_all.37.refs_0_ = f32[8,8,256]{2,1,0:T(8,128)} all-to-all(f32[8,8,256]{2,1,0:T(8,128)} %get-tuple-element.39), channel_id=1, replica_groups=mesh['section'=2,'fsdp'=64,'tp'=4] {'section','tp'}, dimensions={0} | all-to-all | bytes 131072 | tf_op jit(solution)/shard_map/all_to_all | solution.py:468
  123.6 5.3 %first_gradient.1 = (bf16[256,1024]{1,0:T(8,128)(2,1)}, bf16[256,1024]{1,0:T(8,128)(2,1)}, f32[8,256]{1,0:T(8,128)}, bf16[8,304,128]{2,1,0:T(8,128)(2,1)}) custom-call(f32[8,8,256]{2,1,0:T(8,128)} %all_to_all.37.refs_0_, bf16[256,1024]{1,0:T(8,128)(2,1)} %get-tuple-element.38.refs_1_.refs_2_, f32[256,1024]{1,0:T(8,128)} %scaled_1.1.refs_3_.refs_2_, ...), custom_call_target="tpu_custom_call" | custom-call | bytes 4562944 | tf_op jit(solution)/shard_map/first_gradient/pallas_call | solution.py:200
  128.9 3.9 %all-to-all-start.4 = ((bf16[8,304,128]{2,1,0:T(8,128)(2,1)}), bf16[8,304,128]{2,1,0:T(8,128)(2,1)S(1)}, u32[]{:S(2)}, u32[]{:S(2)}) async-start(bf16[8,304,128]{2,1,0:T(8,128)(2,1)} %get-tuple-element.43), calls=%async_computation.5 | async-start | bytes 1245184 | tf_op jit(solution)/shard_map/all_to_all | solution.py:468
  132.8 0.0 reduce-scatter.2.cloned.1.call-start
  132.8 4.1 %values_1.1 = bf16[8,256,128]{2,1,0:T(8,128)(2,1)} custom-call(bf16[256,1024]{1,0:T(8,128)(2,1)} %get-tuple-element.42.refs_0_.refs_5_, bf16[2,16,1024]{2,1,0:T(8,128)(2,1)} %get-tuple-element.34.refs_1_.refs_2_.refs_7_.refs_4_, bf16[2,16,1024]{2,1,0:T(8,128)(2,1)} %get-tuple-element.31.refs_2_, ...), custom_call_target="tpu_custom_call" | custom-call | bytes 3211264 | tf_op jit(solution)/shard_map/values_1/pallas_call | solution.py:200
  136.8 0.0 reduce-scatter.2.cloned.1.call-update
  136.9 6.3 %all-to-all-done.4.refs_1_ = bf16[8,304,128]{2,1,0:T(8,128)(2,1)S(1)} async-done(((bf16[8,304,128]{2,1,0:T(8,128)(2,1)}), bf16[8,304,128]{2,1,0:T(8,128)(2,1)S(1)}, u32[]{:S(2)}, u32[]{:S(2)}) %all-to-all-start.4) | async-done | bytes 622624 | tf_op jit(solution)/shard_map/all_to_all | solution.py:468
  143.2 0.0 copy-start.3
  143.2 0.8 copy-done.3
  144.0 5.6 %map_gradient.1 = (bf16[256,1024]{1,0:T(8,128)(2,1)}, f32[16,256]{1,0:T(8,128)}, f32[256,128]{1,0:T(8,128)}, f32[2,64,384]{2,1,0:T(8,128)}) custom-call(s32[2]{0:T(128)} %pad_add_fusion.refs_0_, bf16[8,304,128]{2,1,0:T(8,128)(2,1)} %copy-done.3, bf16[2,16,1024]{2,1,0:T(8,128)(2,1)} %get-tuple-element.31.refs_2_, ...), custom_call_target="tpu_custom_call" | custom-call | bytes 2678784 | tf_op jit(solution)/shard_map/map_gradient/pallas_call | solution.py:200
  149.7 1.8 copy.18
  151.5 11.1 %all-to-all-start.5 = ((f32[128,1,384]{2,1,0:T(1,128)}), f32[128,1,384]{2,1,0:T(1,128)S(1)}, u32[]{:S(2)}, u32[]{:S(2)}) async-start(f32[128,1,384]{2,1,0:T(1,128)} %copy.18), calls=%async_computation.6 | async-start | bytes 393216 | tf_op jit(solution)/shard_map/all_to_all | solution.py:608
  162.6 14.3 %all-to-all-done.5 = f32[128,1,384]{2,1,0:T(1,128)S(1)} async-done(((f32[128,1,384]{2,1,0:T(1,128)}), f32[128,1,384]{2,1,0:T(1,128)S(1)}, u32[]{:S(2)}, u32[]{:S(2)}) %all-to-all-start.5) | async-done | bytes 196640 | tf_op jit(solution)/shard_map/all_to_all | solution.py:608
  176.9 0.6 reshape.38.refs_3_.refs_11_
  177.5 4.7 %slot_gradient.1 = bf16[2,96,1024]{2,1,0:T(8,128)(2,1)} custom-call(s32[2]{0:T(128)} %bitcast.52, s32[2]{0:T(128)} %bitcast.54, bf16[256,1024]{1,0:T(8,128)(2,1)} %get-tuple-element.47.refs_2_, f32[16,256]{1,0:T(8,128)} %get-tuple-element.48.refs_3_, bf16[2,16,1024]{2,1,0:T(8,128)(2,1)} %get-tuple-element.34.refs_1_.refs_2_.refs_7_.refs_4_, ...), custom_call_target="tpu_custom_call" | custom-call | bytes 4407296 | tf_op jit(solution)/shard_map/slot_gradient/pallas_call | solution.py:200
  182.2 0.0 copy-start
  182.3 1.1 select_bitcast_fusion
  183.4 2.8 %collective-permute-start.2 = (bf16[96,1024]{1,0:T(8,128)(2,1)S(1)}, bf16[96,1024]{1,0:T(8,128)(2,1)S(1)}, u32[]{:S(2)}, u32[]{:S(2)}) collective-permute-start(bf16[96,1024]{1,0:T(8,128)(2,1)S(1)} %select_bitcast_fusion), channel_id=1, source_target_pairs={{0,256},{256,0},{1,257},{257,1},{2,258},{258,2},{3,259},{259,3},{4... | collective-permute-start | bytes 589832 | tf_op jit(solution)/shard_map/ppermute | solution.py:464
  186.2 0.0 reduce-scatter.2.cloned.1.call-done
  186.2 0.0 copy-start.2
  186.2 2.5 %second_output.1 = bf16[256,1024]{1,0:T(8,128)(2,1)} custom-call(bf16[256,128]{1,0:T(8,128)(2,1)} %bitcast.49, bf16[2,2,1024,128]{3,2,1,0:T(8,128)(2,1)} %get-tuple-element.35.refs_1_.refs_4_, bf16[256,1024]{1,0:T(8,128)(2,1)} %get-tuple-element.38.refs_1_.refs_2_, f32[1,1,768]{2,1,0:T(1,128)} %reshape.38.refs_3_.refs_11_), custom_call_target="tpu_custom_call" | custom-call | bytes 1638400 | tf_op jit(solution)/shard_map/second_output/pallas_call | solution.py:200
  188.7 0.0 copy-done
  188.8 0.0 copy-start.1
  188.8 0.1 broadcast_select_fusion.2
  188.8 3.0 %collective-permute-start.1 = (bf16[256,1024]{1,0:T(8,128)(2,1)S(1)}, bf16[256,1024]{1,0:T(8,128)(2,1)S(1)}, u32[]{:S(2)}, u32[]{:S(2)}) collective-permute-start(bf16[256,1024]{1,0:T(8,128)(2,1)S(1)} %broadcast_select_fusion.2), channel_id=1, source_target_pairs={{0,256},{256,0},{1,257},{257,1},{2,258},{258,2},{3,259},{259,3},{4... | collective-permute-start | bytes 1572872 | tf_op jit(solution)/shard_map/ppermute | solution.py:464
  191.9 0.8 broadcast_in_dim.34
  192.7 4.6 %all-to-all-start.6 = ((f32[64,1,768]{2,1,0:T(1,128)}), f32[64,1,768]{2,1,0:T(1,128)S(1)}, u32[]{:S(2)}, u32[]{:S(2)}) async-start(f32[64,1,768]{2,1,0:T(1,128)} %broadcast_in_dim.34), calls=%async_computation.7 | async-start | bytes 393216 | tf_op jit(solution)/shard_map/all_to_all | solution.py:612
  197.3 0.0 collective-permute-done.2
  197.3 0.0 copy-done.2
  197.3 0.8 maximum_bitcast_fusion
  198.1 11.9 %all-to-all-done.6.refs_0_ = f32[64,1,768]{2,1,0:T(1,128)S(1)} async-done(((f32[64,1,768]{2,1,0:T(1,128)}), f32[64,1,768]{2,1,0:T(1,128)S(1)}, u32[]{:S(2)}, u32[]{:S(2)}) %all-to-all-start.6) | async-done | bytes 196640 | tf_op jit(solution)/shard_map/all_to_all | solution.py:612
  210.1 0.0 copy-start.6
  210.1 0.7 copy-done.6
  210.7 2.4 %maps.1 = (f32[16,2048]{1,0:T(8,128)}, f32[16,256]{1,0:T(8,128)}) custom-call(f32[64,1,768]{2,1,0:T(1,128)} %copy-done.6), custom_call_target="tpu_custom_call" | custom-call | bytes 344064 | tf_op jit(solution)/shard_map/maps/pallas_call | solution.py:200
  213.2 0.0 collective-permute-done.1
  213.2 0.0 copy-done.1
  213.2 0.1 broadcast_select_fusion.1
  213.3 1.1 pad_maximum_fusion
  (6 shorter events, 0.1 us)
Async XLA Ops:
  7.2 25.9 %copy-start.7 = (bf16[1,2048]{1,0:T(2,128)(2,1)S(1)}, bf16[1,2048]{1,0:T(2,128)(2,1)}, u32[]{:S(2)}) copy-start(bf16[1,2048]{1,0:T(2,128)(2,1)} %param.19) | copy-start | bytes 12292
  7.2 85.0 %all-gather.2.cloned.1.call-start = ((), (), s32[]{:S(2)}) async-start(), calls=%async_computation.8 | async-start | bytes 4718592 | tf_op jit(solution)/shard_map/all_gather | solution.py:505
  37.3 5.1 %collective-permute-start = (bf16[432,1024]{1,0:T(8,128)(2,1)}, bf16[432,1024]{1,0:T(8,128)(2,1)S(1)}, u32[]{:S(2)}, u32[]{:S(2)}) collective-permute-start(bf16[432,1024]{1,0:T(8,128)(2,1)} %pack.1), channel_id=1, source_target_pairs={{0,256},{256,0},{1,257},{257,1},{2,258},{258,2},{3,259},{259,3},{4... | collective-permute-start | bytes 2654216 | tf_op jit(solution)/shard_map/ppermute | solution.py:464
  42.5 0.9 copy-start.5
  96.3 14.3 %all-to-all-start.2 = ((bf16[8,256,128]{2,1,0:T(8,128)(2,1)}), bf16[8,256,128]{2,1,0:T(8,128)(2,1)S(1)}, u32[]{:S(2)}, u32[]{:S(2)}) async-start(bf16[8,256,128]{2,1,0:T(8,128)(2,1)} %values_0.1), calls=%async_computation.2 | async-start | bytes 1048576 | tf_op jit(solution)/shard_map/all_to_all | solution.py:468
  110.6 0.8 copy-start.4
  128.9 14.3 %all-to-all-start.4 = ((bf16[8,304,128]{2,1,0:T(8,128)(2,1)}), bf16[8,304,128]{2,1,0:T(8,128)(2,1)S(1)}, u32[]{:S(2)}, u32[]{:S(2)}) async-start(bf16[8,304,128]{2,1,0:T(8,128)(2,1)} %get-tuple-element.43), calls=%async_computation.5 | async-start | bytes 1245184 | tf_op jit(solution)/shard_map/all_to_all | solution.py:468
  132.8 53.5 %reduce-scatter.2.cloned.1.call-start = ((), (), s32[]{:S(2)}) async-start(), calls=%async_computation.9 | async-start | bytes 589824 | tf_op jit(solution)/shard_map/reduce_scatter | solution.py:585
  143.2 0.9 copy-start.3
  151.5 25.4 %all-to-all-start.5 = ((f32[128,1,384]{2,1,0:T(1,128)}), f32[128,1,384]{2,1,0:T(1,128)S(1)}, u32[]{:S(2)}, u32[]{:S(2)}) async-start(f32[128,1,384]{2,1,0:T(1,128)} %copy.18), calls=%async_computation.6 | async-start | bytes 393216 | tf_op jit(solution)/shard_map/all_to_all | solution.py:608
  182.2 6.5 %copy-start = (bf16[256,1024]{1,0:T(8,128)(2,1)S(1)}, bf16[256,1024]{1,0:T(8,128)(2,1)}, u32[]{:S(2)}) copy-start(bf16[256,1024]{1,0:T(8,128)(2,1)} %get-tuple-element.38.refs_1_.refs_2_) | copy-start | bytes 1572868
  183.4 13.9 %collective-permute-start.2 = (bf16[96,1024]{1,0:T(8,128)(2,1)S(1)}, bf16[96,1024]{1,0:T(8,128)(2,1)S(1)}, u32[]{:S(2)}, u32[]{:S(2)}) collective-permute-start(bf16[96,1024]{1,0:T(8,128)(2,1)S(1)} %select_bitcast_fusion), channel_id=1, source_target_pairs={{0,256},{256,0},{1,257},{257,1},{2,258},{258,2},{3,259},{259,3},{4... | collective-permute-start | bytes 589832 | tf_op jit(solution)/shard_map/ppermute | solution.py:464
  186.2 11.1 %copy-start.2 = (bf16[2,96,1024]{2,1,0:T(8,128)(2,1)S(1)}, bf16[2,96,1024]{2,1,0:T(8,128)(2,1)}, u32[]{:S(2)}) copy-start(bf16[2,96,1024]{2,1,0:T(8,128)(2,1)} %slot_gradient.1) | copy-start | bytes 1179652
  188.8 24.4 %copy-start.1 = (bf16[256,1024]{1,0:T(8,128)(2,1)S(1)}, bf16[256,1024]{1,0:T(8,128)(2,1)}, u32[]{:S(2)}) copy-start(bf16[256,1024]{1,0:T(8,128)(2,1)} %second_output.1) | copy-start | bytes 1572868
  188.8 24.3 %collective-permute-start.1 = (bf16[256,1024]{1,0:T(8,128)(2,1)S(1)}, bf16[256,1024]{1,0:T(8,128)(2,1)S(1)}, u32[]{:S(2)}, u32[]{:S(2)}) collective-permute-start(bf16[256,1024]{1,0:T(8,128)(2,1)S(1)} %broadcast_select_fusion.2), channel_id=1, source_target_pairs={{0,256},{256,0},{1,257},{257,1},{2,258},{258,2},{3,259},{259,3},{4... | collective-permute-start | bytes 1572872 | tf_op jit(solution)/shard_map/ppermute | solution.py:464
  192.7 17.4 %all-to-all-start.6 = ((f32[64,1,768]{2,1,0:T(1,128)}), f32[64,1,768]{2,1,0:T(1,128)S(1)}, u32[]{:S(2)}, u32[]{:S(2)}) async-start(f32[64,1,768]{2,1,0:T(1,128)} %broadcast_in_dim.34), calls=%async_computation.7 | async-start | bytes 393216 | tf_op jit(solution)/shard_map/all_to_all | solution.py:612
  210.1 0.7 copy-start.6
Sparse Core Ops, SparseCore 0:
  33.1 59.0 all-gather.1
  137.0 35.9 reduce-scatter.1

commit v3 on v1

v3 whole, which is shorter than its diff:
```python
import functools
import math

import jax
import jax.numpy as jnp
from jax import lax
from jax.experimental import pallas as pl
from jax.experimental.pallas import tpu as pltpu
from jax.sharding import PartitionSpec as P

MODEL_WIDTH = 8192
HD = 128
TOKT = 32
ADAPTER_SCALE = 0.5
EPS = 1e-06

SEQ = 128
MB = 2
ROWS = MB * SEQ
VIS = 96
RANK = 16
HEADS = 8
HALF = HEADS * HD
KVH = 8
PEERS = 8
VMEM_BYTES = 40 * 1024 * 1024

BF = jnp.bfloat16
F32 = jnp.float32

R_VIS, R_Q, R_K, R_DN, R_UP, R_GN, R_END = 0, 96, 352, 384, 400, 416, 432
R_SUM, R_LOW, R_PAY = ROWS, ROWS + RANK, ROWS + RANK + 2 * RANK
SUBLANES = 8
M_ROWS = RANK + SUBLANES


def block_of(head):
    return (head % 2) * 4 + head // 2


def nt(left, right):
    return lax.dot_general(left, right, (((1,), (1,)), ((), ())), preferred_element_type=F32)


def tn(left, right):
    return lax.dot_general(left, right, (((0,), (0,)), ((), ())), preferred_element_type=F32)


def nn(left, right):
    return jnp.dot(left, right, preferred_element_type=F32)


def stack_heads(block):
    return jnp.concatenate([block[:, h * HD : (h + 1) * HD] for h in range(HEADS)], axis=0)


def unstack_heads(block):
    return jnp.concatenate([block[h * SEQ : (h + 1) * SEQ, :] for h in range(HEADS)], axis=1)


def columns_to_rows(*columns):
    lane = lax.broadcasted_iota(jnp.int32, (ROWS, HD), 1)
    square = jnp.zeros((ROWS, HD), F32)
    for at, column in enumerate(columns):
        square = jnp.where(lane == at, column, square)
    return square.T[:SUBLANES, :]


def rows_to_columns(rows):
    padded = jnp.concatenate([rows, jnp.zeros((HD - SUBLANES, ROWS), F32)], axis=0)
    return padded.T


def payload_block(values, column, low_rank):
    row = columns_to_rows(column)[0:1, :]
    high = row.astype(BF).astype(F32)
    low = row - high
    at = lax.broadcasted_iota(jnp.int32, (RANK, HD), 0)
    sums = jnp.zeros((RANK, HD), F32)
    for index, part in enumerate((high[:, :HD], high[:, HD:], low[:, :HD], low[:, HD:])):
        sums = jnp.where(at == index, part, sums)
    low_rank = low_rank.astype(BF)
    return jnp.concatenate(
        [values, sums.astype(BF), low_rank[:, :HD], low_rank[:, HD:]], axis=0
    )


def total_of_payloads(blocks):
    sums = blocks[0, R_SUM:R_LOW, :].astype(F32)
    low_rank = blocks[0, R_LOW:, :].astype(F32)
    for peer in range(1, PEERS):
        sums = sums + blocks[peer, R_SUM:R_LOW, :].astype(F32)
        low_rank = low_rank + blocks[peer, R_LOW:, :].astype(F32)
    left = sums[0:1, :] + sums[2:3, :]
    right = sums[1:2, :] + sums[3:4, :]
    row = jnp.concatenate([left, right], axis=1)
    at = lax.broadcasted_iota(jnp.int32, (SUBLANES, ROWS), 0)
    rows = jnp.where(at == 0, row, 0.0)
    return rows, jnp.concatenate([low_rank[:RANK, :], low_rank[RANK:, :]], axis=1)


def inverse_of(squares):
    return lax.rsqrt(squares / MODEL_WIDTH + EPS)


class Loaded:
    def __init__(self, buffer, copies):
        self.buffer, self.copies, self.done = buffer, copies, set()
        for copy in copies:
            copy.start()

    def __call__(self, part=None):
        for at in range(len(self.copies)) if part is None else (part,):
            if at not in self.done:
                self.copies[at].wait()
                self.done.add(at)
        return self.buffer


class Stored:
    def __init__(self, buffer, target, semaphores):
        self.buffer, self.target, self.semaphores, self.copies = buffer, target, semaphores, []

    def send(self, repeated=False):
        targets = [self.target.at[peer] for peer in range(PEERS)] if repeated else [self.target]
        for at, target in enumerate(targets):
            copy = pltpu.make_async_copy(self.buffer, target, self.semaphores.at[at])
            copy.start()
            self.copies.append(copy)

    def finish(self):
        for copy in self.copies:
            copy.wait()


def whole(scalars, ref, buffer):
    return [(ref, buffer)]


def columns_of(layer):
    def view(scalars, ref, buffer):
        pairs = [pl.ds(2 * at, 2) for at in range(KVH // 2)]
        return [(ref.at[pair, layer], buffer.at[pair]) for pair in pairs]

    return view


def call(kernel, name, results, scalars, operands):
    arrays = [o[0] if isinstance(o, tuple) else o for o in operands]
    manual_in = [isinstance(o, tuple) for o in operands]
    manual_out = [len(r) == 3 for r in results]
    n_scalars, n_arrays, n_results = len(scalars), len(arrays), len(results)
    most = KVH // 2

    def body(*refs):
        scalar_refs = refs[:n_scalars]
        ins = list(refs[n_scalars : n_scalars + n_arrays])
        outs = list(refs[n_scalars + n_arrays : n_scalars + n_arrays + n_results])
        scratch = list(refs[n_scalars + n_arrays + n_results :])
        in_semaphores, out_semaphores = scratch.pop(), None
        out_semaphores, in_semaphores = in_semaphores, scratch.pop()
        loads, stores = [], []
        for at in range(n_arrays):
            if manual_in[at]:
                buffer = scratch.pop(0)
                pairs = operands[at][2](scalar_refs, ins[at], buffer)
                copies = [
                    pltpu.make_async_copy(*pair, in_semaphores.at[at * most + k])
                    for k, pair in enumerate(pairs)
                ]
                ins[at] = Loaded(buffer, copies)
                loads.append(ins[at])
        for at in range(n_results):
            if manual_out[at]:
                outs[at] = Stored(scratch.pop(0), outs[at], out_semaphores.at[at])
                stores.append(outs[at])
        kernel(*scalar_refs, *ins, *outs)
        for load in loads:
            load()
        for store in stores:
            store.finish()

    moved = sum(a.size * a.dtype.itemsize for a in arrays)
    moved += sum(math.prod(r[0]) * jnp.dtype(r[1]).itemsize for r in results)
    in_vmem = pl.BlockSpec(memory_space=pltpu.VMEM)
    in_hbm = pl.BlockSpec(memory_space=pltpu.HBM)
    return pl.pallas_call(
        body,
        out_shape=[jax.ShapeDtypeStruct(r[0], r[1]) for r in results],
        in_specs=[pl.BlockSpec(memory_space=pltpu.SMEM)] * n_scalars
        + [in_hbm if manual else in_vmem for manual in manual_in],
        out_specs=[in_hbm if manual else in_vmem for manual in manual_out],
        scratch_shapes=[pltpu.VMEM(o[1], o[0].dtype) for o in operands if isinstance(o, tuple)]
        + [pltpu.VMEM(r[2], r[1]) for r in results if len(r) == 3]
        + [
            pltpu.SemaphoreType.DMA((n_arrays * most,)),
            pltpu.SemaphoreType.DMA((n_results, PEERS)),
        ],
        compiler_params=pltpu.CompilerParams(vmem_limit_bytes=VMEM_BYTES),
        cost_estimate=pl.CostEstimate(flops=0, bytes_accessed=moved, transcendentals=0),
        name=name,
    )(*scalars, *arrays)


def pack_kernel(core, visual, queries, keys, down, up, gain, out):
    other = 1 - core[0]
    at = pl.multiple_of(other * HALF, HALF)
    key_at = pl.multiple_of(other * HD, HD)
    out[R_VIS:R_Q, :] = visual[:, pl.ds(at, HALF)]
    out[R_Q:R_K, :] = queries[:, pl.ds(at, HALF)]
    for j in range(8):
        out[R_K:R_DN, j * HD : (j + 1) * HD] = keys[j * 32 : (j + 1) * 32, pl.ds(key_at, HD)]
    out[R_DN:R_UP, :] = down[:, pl.ds(at, HALF)]
    out[R_UP:R_GN, :] = up[...]
    out[R_GN:R_END, :] = gain[:, pl.ds(at, HALF)]


def softmax_of(query_rows, key_rows, length):
    scores = nt(stack_heads(query_rows), key_rows) / math.sqrt(HD)
    shape = scores.shape
    row = lax.rem(lax.broadcasted_iota(jnp.int32, shape, 0), SEQ)
    column = lax.broadcasted_iota(jnp.int32, shape, 1)
    allowed = (column <= row) & (column < length)
    scores = jnp.where(allowed, scores, -jnp.inf)
    top = jnp.max(scores, axis=-1, keepdims=True)
    weights = jnp.exp(scores - top)
    return (weights / jnp.sum(weights, axis=-1, keepdims=True)).astype(BF)


def prepare_kernel(
    core, counts, starts, lengths,
    received, visual, queries, keys, down, up, gain, embeddings, cotangent,
    weights, entry, cotangent_half, downs, ups, gains, payload,
):
    own = core[0]
    other = 1 - own
    half = pl.ds(pl.multiple_of(own * HALF, HALF), HALF)
    key_half = pl.ds(pl.multiple_of(own * HD, HD), HD)
    downs[own] = down[:, half]
    downs[other] = received[R_DN:R_UP, :]
    ups[own] = up[...]
    ups[other] = received[R_UP:R_GN, :]
    gains[own] = gain[:, half]
    gains[other] = received[R_GN:R_END, :]
    position = lax.broadcasted_iota(jnp.int32, (SEQ, VIS), 0)
    slot = lax.broadcasted_iota(jnp.int32, (SEQ, VIS), 1)
    place = lax.broadcasted_iota(jnp.int32, (SEQ, 1), 0)
    for index, table in ((own, visual[:, half]), (other, received[R_VIS:R_Q, :])):
        begin = starts[index]
        count = counts[index] * TOKT
        placing = ((position == begin + slot) & (slot < count)).astype(F32).astype(BF)
        inserted = nn(placing, table).astype(BF)
        covered = (place >= begin) & (place < begin + count)
        rows = pl.ds(pl.multiple_of(index * SEQ, SEQ), SEQ)
        entry[rows, :] = jnp.where(covered, inserted, embeddings[index, :, half])
    for m in range(MB):
        rows = slice(m * SEQ, (m + 1) * SEQ)
        cotangent_half[rows, :] = cotangent[m, :, half]
        weights[own, m] = softmax_of(queries[rows, half], keys[rows, key_half], lengths[m])
        other_keys = jnp.concatenate(
            [received[R_K:R_DN, j * HD : (j + 1) * HD] for j in range(4 * m, 4 * m + 4)], axis=0
        )
        weights[other, m] = softmax_of(
            received[R_Q + m * SEQ : R_Q + (m + 1) * SEQ, :], other_keys, lengths[m]
        )
    value_gradient = jnp.concatenate(
        [
            tn(weights[1, m], stack_heads(cotangent_half[m * SEQ : (m + 1) * SEQ, :]))
            for m in range(MB)
        ],
        axis=0,
    ).astype(BF)
    entry_float = entry[...].astype(F32)
    squares = jnp.sum(entry_float * entry_float, axis=-1, keepdims=True)
    gained = (entry_float * gains[0][0:1, :].astype(F32)).astype(BF)
    block = payload_block(value_gradient, squares, nt(downs[0], gained))
    for peer in range(PEERS):
        payload[peer] = block


def entry_norm_kernel(
    core, received, entry, ups, gains,
    normed, sums, adapter_rows, full_gradient, own_gradient, lora_gradient,
):
    rows, low_rank = total_of_payloads(received)
    sums[...] = rows
    column = inverse_of(rows_to_columns(rows)[:, 0:1])
    adapter_rows[...] = low_rank * inverse_of(rows[0:1, :])
    gain = gains[0][0:1, :].astype(F32)
    normed[...] = (entry[...].astype(F32) * column * gain).astype(BF)
    for head in range(KVH):
        full_gradient[:, head * HD : (head + 1) * HD] = received[block_of(head), :ROWS, :]
    own_gradient[...] = received[core[0] * 4 + core[1], :ROWS, :]
    lora_gradient[...] = ADAPTER_SCALE * nt(ups[1], full_gradient[...])


def partial_values(rows, down, up, columns, out):
    adapter = (ADAPTER_SCALE * nt(rows, down)).astype(BF)
    for pair in range(KVH // 2):
        weight = columns(pair)[2 * pair : 2 * pair + 2].reshape(2 * HD, HALF)
        span = slice(2 * pair * HD, (2 * pair + 2) * HD)
        partial = (nt(rows, weight) + nn(adapter, up[:, span])).astype(BF)
        for at in range(2):
            out[block_of(2 * pair + at)] = partial[:, at * HD : (at + 1) * HD]


def first_values_kernel(normed, downs, ups, columns, out):
    partial_values(normed[...], downs[0], ups[0], columns, out)


def second_values_kernel(hidden, totals, gains, downs, ups, columns, out):
    column = inverse_of(rows_to_columns(totals[...])[:, 0:1])
    gain = gains[1][0:1, :].astype(F32)
    normed = (hidden[...].astype(F32) * gain * column).astype(BF)
    partial_values(normed, downs[1], ups[1], columns, out)


def weighted_gradient(gradient_of, lora_gradient, down, gain, columns):
    grad = tn(lora_gradient.astype(BF), down)
    for pair in range(KVH // 2):
        weight = columns(pair)[2 * pair : 2 * pair + 2].reshape(2 * HD, HALF)
        grad = grad + nn(gradient_of(pair), weight)
    return grad * gain[0:1, :].astype(F32)


def scaled_kernel(full_gradient, lora_gradient, downs, gains, columns, scaled):
    scaled[...] = weighted_gradient(
        lambda pair: full_gradient[:, 2 * pair * HD : (2 * pair + 2) * HD],
        lora_gradient[...],
        downs[1],
        gains[1],
        columns,
    )


def attended_rows(weights, layer, value_rows):
    return jnp.concatenate(
        [
            unstack_heads(nn(weights[layer, m], value_rows[m * SEQ : (m + 1) * SEQ, :]))
            for m in range(MB)
        ],
        axis=0,
    )


def first_output_kernel(received, weights, entry, scaled, hidden, value_rows, payload):
    values = received[0].astype(F32)
    for peer in range(1, PEERS):
        values = values + received[peer].astype(F32)
    value_rows[...] = values
    attended = attended_rows(weights, 0, values.astype(BF))
    output = (entry[...].astype(F32) + attended).astype(BF)
    hidden[...] = output
    output_float = output.astype(F32)
    squares = jnp.sum(output_float * output_float, axis=-1, keepdims=True)
    dots = jnp.sum(output_float * scaled[...], axis=-1, keepdims=True)
    block = columns_to_rows(squares, dots)
    for peer in range(PEERS):
        payload[peer] = block


def first_gradient_kernel(
    received, hidden, scaled, cotangent_half, weights, value_rows, gains, downs, lora_gradient,
    gradient, totals, down_gradient, payload,
):
    total = received[0]
    for peer in range(1, PEERS):
        total = total + received[peer]
    totals[...] = total
    sums = rows_to_columns(total)
    column = inverse_of(sums[:, 0:1])
    factor = column * column * column * sums[:, 1:2] / MODEL_WIDTH
    hidden_float = hidden[...].astype(F32)
    grad = (
        cotangent_half[...].astype(F32) + column * scaled[...] - hidden_float * factor
    ).astype(BF)
    gradient.buffer[...] = grad
    gradient.send()
    gained = hidden_float * gains[1][0:1, :].astype(F32)
    low_rank = nt(downs[1], gained.astype(BF))
    value_gradient = jnp.concatenate(
        [tn(weights[0, m], stack_heads(grad[m * SEQ : (m + 1) * SEQ, :])) for m in range(MB)],
        axis=0,
    ).astype(BF)
    dots = jnp.sum(value_gradient.astype(F32) * value_rows[...], axis=-1, keepdims=True)
    payload.buffer[...] = payload_block(value_gradient, dots, low_rank)
    payload.send(repeated=True)
    normed = (gained * column).astype(BF)
    down_gradient[...] = nn(lora_gradient[...].astype(BF), normed)


def gathered_gradient(received):
    return jnp.concatenate([received[block_of(head), :ROWS, :] for head in range(KVH)], axis=1)


def map_gradient_kernel(
    core, received, ups, adapter_0, totals, gradient_1, down_gradient_1, normed_0, out
):
    rows, low_rank = total_of_payloads(received)
    lora_0 = ADAPTER_SCALE * nt(ups[0], gathered_gradient(received))
    own = received[core[0] * 4 + core[1], :ROWS, :]
    adapter_1 = (low_rank * inverse_of(totals[0:1, :])).astype(BF)
    down = (nn(lora_0.astype(BF), normed_0()[...]), down_gradient_1[...])
    up = (
        ADAPTER_SCALE * nn(adapter_0[...].astype(BF), own),
        ADAPTER_SCALE * nn(adapter_1, gradient_1[...]),
    )
    for layer in range(2):
        for y in range(8):
            block = out.at[layer * 8 + y]
            block[:RANK, :] = down[layer][:, y * HD : (y + 1) * HD]
            block[RANK : RANK + 2, :] = up[layer][2 * y : 2 * y + 2, :]
            block[RANK + 2 :, :] = jnp.zeros((M_ROWS - RANK - 2, HD), F32)


def near_sum_kernel(received, out):
    for half in range(2):
        total = received[half * 8]
        for y in range(1, 8):
            total = total + received[half * 8 + y]
        for peer in range(KVH):
            out[peer, half] = total.astype(BF)


def far_sum_kernel(received, out):
    total = received[0].astype(F32)
    for z in range(1, KVH):
        total = total + received[z].astype(F32)
    for peer in range(8):
        out[peer] = total.astype(BF)


def maps_kernel(received, down_sum, up_sum, *, scale):
    for half in range(2):
        for y in range(8):
            block = received[y, half].astype(F32) * scale
            at = half * HALF + y * HD
            down_sum[:, at : at + HD] = block[:RANK, :]
            up_sum[2 * y : 2 * y + 2, half * HD : (half + 1) * HD] = block[RANK : RANK + 2, :]


def slot_gradient_kernel(
    counts, starts, received, ups, downs, gains, sums, columns, gradient, entry, slots
):
    rows, _ = total_of_payloads(received)
    lora_gradient = ADAPTER_SCALE * nt(ups[0], gathered_gradient(received))
    scaled = weighted_gradient(
        lambda pair: jnp.concatenate(
            [received[block_of(2 * pair + at), :ROWS, :] for at in range(2)], axis=1
        ),
        lora_gradient,
        downs[0],
        gains[0],
        columns,
    )
    column = inverse_of(rows_to_columns(sums[...])[:, 0:1])
    factor = column * column * rows_to_columns(rows)[:, 0:1] / MODEL_WIDTH
    grad = (
        gradient()[...].astype(F32) + column * scaled - entry()[...].astype(F32) * factor
    ).astype(BF)
    slot = lax.broadcasted_iota(jnp.int32, (VIS, SEQ), 0)
    position = lax.broadcasted_iota(jnp.int32, (VIS, SEQ), 1)
    for m in range(MB):
        picking = ((position == starts[m] + slot) & (slot < counts[m] * TOKT)).astype(F32).astype(BF)
        slots[m] = nn(picking, grad[m * SEQ : (m + 1) * SEQ, :]).astype(BF)


def second_output_kernel(values, weights, hidden, out):
    attended = attended_rows(weights, 1, values[...])
    out[...] = (hidden[...].astype(F32) + attended).astype(BF)


def swap_cores(block):
    return lax.ppermute(block, "section", [(0, 1), (1, 0)])


def to_heads(block):
    return lax.all_to_all(block, ("section", "tp"), 0, 0)


def on_device(
    embeddings,
    visual,
    image_block_count,
    starts,
    lengths,
    queries,
    layer_key_vectors,
    input_norm_gain,
    frozen_value_weight,
    adapter_down_map,
    adapter_up_map,
    cotangent,
):
    section = lax.axis_index("section")
    tp = lax.axis_index("tp")
    n_fsdp = lax.axis_size("fsdp")
    n_y = n_fsdp // KVH
    core = jnp.stack([section, tp]).astype(jnp.int32)
    counts = image_block_count[:, 0]
    begins = starts[:, 0]
    seq_lengths = lengths[:, 0]

    shard = frozen_value_weight[0].T
    pieces = shard.reshape(shard.shape[0], 2, HALF).transpose(1, 0, 2)
    pieces = jnp.broadcast_to(pieces[:, None], (2, n_y) + pieces.shape[1:])
    pieces = pieces.reshape((2 * n_y,) + pieces.shape[2:])
    head_groups = [
        [s * n_fsdp + z * n_y + y for s in range(2) for y in range(n_y)] for z in range(KVH)
    ]
    head_columns = lax.all_to_all(
        pieces, ("section", "fsdp"), 0, 0, axis_index_groups=head_groups
    ).reshape(2, HD, HALF)
    row_groups = [[z * n_y + y for z in range(KVH)] for y in range(n_y)]
    columns = lax.all_gather(head_columns, "fsdp", axis=0, axis_index_groups=row_groups)

    own = (
        visual[0, 0],
        queries[0].reshape(ROWS, 2 * HALF),
        layer_key_vectors[0].reshape(ROWS, 2 * HD),
        adapter_down_map[0].T,
        adapter_up_map[0],
        jnp.broadcast_to(input_norm_gain, (RANK, 2 * HALF)),
    )
    (packed,) = call(pack_kernel, "pack", [((R_END, HALF), BF)], (core,), own)

    wide = ((ROWS, HALF), BF)
    low = ((RANK, ROWS), F32)
    sums = ((SUBLANES, ROWS), F32)
    maps = ((2, RANK, HALF), BF)
    blocks = ((PEERS, ROWS, HD), BF)
    mixed = ((PEERS, R_PAY, HD), BF)
    weights, entry, cotangent_half, downs, ups, gains, payload = call(
        prepare_kernel,
        "prepare",
        [((2, MB, HEADS * SEQ, SEQ), BF), wide, wide, maps, maps, maps, mixed],
        (core, counts, begins, seq_lengths),
        (swap_cores(packed), *own, embeddings, cotangent),
    )

    def weight_of(layer):
        return (columns, (KVH, HD, HALF), columns_of(layer))

    normed_0, sums_0, adapter_0, full_gradient_1, own_gradient_1, lora_gradient_1 = call(
        entry_norm_kernel,
        "entry_norm",
        [wide, sums, low, wide, ((ROWS, HD), BF), low],
        (core,),
        (to_heads(payload), entry, ups, gains),
    )
    (partial_0,) = call(
        first_values_kernel, "values_0", [blocks], (), (normed_0, downs, ups, weight_of(0))
    )
    (scaled_1,) = call(
        scaled_kernel,
        "scaled_1",
        [((ROWS, HALF), F32)],
        (),
        (full_gradient_1, lora_gradient_1, downs, gains, weight_of(1)),
    )
    hidden_0, value_rows, payload = call(
        first_output_kernel,
        "first_output",
        [wide, ((ROWS, HD), F32), ((PEERS, SUBLANES, ROWS), F32)],
        (),
        (to_heads(partial_0), weights, entry, scaled_1),
    )
    gradient, totals, down_gradient_1, payload = call(
        first_gradient_kernel,
        "first_gradient",
        [
            wide + ((ROWS, HALF),),
            sums,
            ((RANK, HALF), F32),
            mixed + ((R_PAY, HD),),
        ],
        (),
        (
            to_heads(payload),
            hidden_0,
            scaled_1,
            cotangent_half,
            weights,
            value_rows,
            gains,
            downs,
            lora_gradient_1,
        ),
    )
    gathered = to_heads(payload)
    (partial_1,) = call(
        second_values_kernel,
        "values_1",
        [blocks],
        (),
        (hidden_0, totals, gains, downs, ups, weight_of(1)),
    )
    values_1 = lax.psum_scatter(partial_1, ("section", "tp"), scatter_dimension=0)

    (chunks,) = call(
        map_gradient_kernel,
        "map_gradient",
        [((2 * n_y, M_ROWS, HD), F32)],
        (core,),
        (
            gathered,
            ups,
            adapter_0,
            totals,
            own_gradient_1,
            down_gradient_1,
            (normed_0, normed_0.shape, whole),
        ),
    )
    halves_of_maps = ((8, 2, M_ROWS, HD), BF)
    near = lax.all_to_all(chunks, ("section", "fsdp"), 0, 0, axis_index_groups=head_groups)
    (near,) = call(near_sum_kernel, "near_sum", [halves_of_maps], (), (near,))
    far = lax.all_to_all(near, "fsdp", 0, 0, axis_index_groups=row_groups)
    (far,) = call(far_sum_kernel, "far_sum", [halves_of_maps], (), (far,))
    y_groups = [[z * n_y + y for y in range(n_y)] for z in range(KVH)]
    summed = lax.all_to_all(far, "fsdp", 0, 0, axis_index_groups=y_groups)
    down_sum, up_sum = call(
        functools.partial(maps_kernel, scale=1.0 / math.sqrt(MB * SEQ * n_fsdp)),
        "maps",
        [((RANK, 2 * HALF), F32), ((RANK, 2 * HD), F32)],
        (),
        (summed,),
    )

    (slots,) = call(
        slot_gradient_kernel,
        "slot_gradient",
        [((MB, VIS, HALF), BF)],
        (counts, begins),
        (
            gathered,
            ups,
            downs,
            gains,
            sums_0,
            weight_of(0),
            (gradient, gradient.shape, whole),
            (entry, entry.shape, whole),
        ),
    )
    (hidden_1,) = call(
        second_output_kernel, "second_output", [wide], (), (values_1, weights, hidden_0)
    )

    first = section == 0

    def halves(mine, theirs):
        left = jnp.where(first, mine, theirs)
        right = jnp.where(first, theirs, mine)
        return jnp.concatenate([left, right], axis=-1)

    slot_rows = halves(
        jnp.where(first, slots[0], slots[1]), swap_cores(jnp.where(first, slots[1], slots[0]))
    )
    hidden = halves(
        jnp.where(first, hidden_0, hidden_1), swap_cores(jnp.where(first, hidden_1, hidden_0))
    )
    return (
        hidden.reshape(1, MB, SEQ, 2 * HALF),
        slot_rows[None, None],
        down_sum.T[None],
        up_sum[None],
    )


def solution(mesh):
    return jax.shard_map(
        on_device,
        mesh=mesh,
        in_specs=(
            P(None, "fsdp", "tp"),
            P("section", "fsdp", None, "tp"),
            P(None, "fsdp"),
            P(None, "fsdp"),
            P(None, "fsdp"),
            P("section", None, "fsdp", "tp"),
            P("section", None, "fsdp", "tp"),
            P("section", "tp"),
            P("section", "tp", "fsdp"),
            P("section", "tp", None),
            P("section", None, None),
            P(None, "fsdp", "tp"),
        ),
        out_specs=(
            P("section", None, "fsdp", "tp"),
            P("section", "fsdp", None, "tp"),
            P("section", "tp", None),
            P("section", None, "tp"),
        ),
        check_vma=False,
    )
```

time: 208 us -> 213 us (1.024)
  Pallas kernels: 14.1 us -> 26.5 us
  local copies, waits for them, and re-layouts: 25.8 us -> 20.2 us
  waiting for transfers between devices: 66.5 us -> 62.1 us
  blocking collectives: 50.3 us -> 46.9 us
  starting transfers between devices: 32.2 us -> 35.6 us
    pallas_call x11 -> x14, Pallas kernels: 14.1 us -> 26.5 us  [call(): pl.pallas_call(body, out_shape=[jax.ShapeDtypeStruct(r[0], r[1]) for r in...]
    all_to_all x2 -> x3, waiting for transfers between devices: 21.6 us -> 13.3 us  [the longest x1 6.82 us: on_device(): summed = lax.all_to_all(far, 'fsdp', 0, 0, axis_index_groups=y_groups)]
    all_to_all x2 -> x3, starting transfers between devices: 15.5 us -> 19.6 us  [the longest x1 6.88 us: on_device(): lax.all_to_all(chunks, ('section', 'fsdp'), 0, 0, axis_index_groups=head_...]
    all_to_all x2, waiting for transfers between devices: 12.1 us -> 16.1 us  [to_heads(): return lax.all_to_all(block, ('section', 'tp'), 0, 0)]
    all_to_all x2, blocking collectives: 25.3 us -> 21.9 us  [to_heads(): return lax.all_to_all(block, ('section', 'tp'), 0, 0)]
    unnamed x61 -> x56, local copies, waits for them, and re-layouts: 21.5 us -> 19.1 us
  transfers between devices with their start and end apart: 9 -> 10, of which waited for: 6 -> 6; matrix products, arithmetic and copies ran while one was open for 2% -> 1% of each run, Pallas kernels for 5% -> 8%
where the time goes in v3:
time: 213 us; the launch traced here: 210 us
  waiting for transfers between devices  62.1 us (29%)
  blocking collectives  46.9 us (22%)
  starting transfers between devices  35.6 us (17%)
  Pallas kernels  26.5 us (12%)
  local copies, waits for them, and re-layouts  20.2 us (9%)
  between operations  14.4 us (7%)
  other arithmetic  4.8 us (2%)
    all_gather x1, waiting for transfers between devices, on_device(): lax.all_gather(head_columns, 'fsdp', axis=0, axis_index_groups=row_groups)  30.6 us
    pallas_call x14, Pallas kernels, call(): pl.pallas_call(body, out_shape=[jax.ShapeDtypeStruct(r[0], r[1]) for r in...  26.5 us
    all_to_all x1, blocking collectives, on_device(): lax.all_to_all(pieces, ('section', 'fsdp'), 0, 0, axis_index_groups=head_...  24.9 us
    all_to_all x2, blocking collectives, to_heads(): return lax.all_to_all(block, ('section', 'tp'), 0, 0)  21.9 us
    unnamed x56, local copies, waits for them, and re-layouts  19.1 us
    all_to_all x2, waiting for transfers between devices, to_heads(): return lax.all_to_all(block, ('section', 'tp'), 0, 0)  16.1 us
    all_to_all x2, starting transfers between devices, to_heads(): return lax.all_to_all(block, ('section', 'tp'), 0, 0)  8.81 us
    ppermute x3, starting transfers between devices, swap_cores(): return lax.ppermute(block, 'section', [(0, 1), (1, 0)])  7.19 us
  transfers between devices with their start and end apart: 10, of which 6 were waited for; matrix products, arithmetic and copies ran while one was open for 1% of the time, Pallas kernels for 8%

profile of v3, /device:TPU:1, one launch (start us, length us, event | category | flops | bytes accessed | tf_op | source)
XLA Modules:
  0.0 210.5 jit_solution(3349179977149997583)
XLA Ops:
  7.2 0.0 copy-start.21
  7.2 0.0 all-gather.2.cloned.1.call-start
  7.3 1.0 reshape.22
  8.3 0.1 broadcast_in_dim.24
  8.3 0.0 copy-start.24
  8.4 0.0 copy-start.25
  8.4 0.0 copy-start.26
  8.4 24.9 %all_to_all.40 = bf16[16,16,1024]{2,1,0:T(8,128)(2,1)} all-to-all(bf16[16,16,1024]{2,1,0:T(8,128)(2,1)S(1)} %bitcast.48), channel_id=1, replica_groups={{0,4,8,12,16,20,24,28,256,260,264,268,272,276,280,284},{32,36,40,44,48,..., dimensions={0} | all-to-all | bytes 1048576 | tf_op jit(solution)/shard_map/all_to_all | solution.py:511
  33.3 0.0 all-gather.2.cloned.1.call-update
  33.4 0.1 pad_add_fusion.refs_0_
  33.5 0.9 pack.1
  34.4 2.9 %collective-permute-start = (bf16[432,1024]{1,0:T(8,128)(2,1)S(1)}, bf16[432,1024]{1,0:T(8,128)(2,1)S(1)}, u32[]{:S(2)}, u32[]{:S(2)}) collective-permute-start(bf16[432,1024]{1,0:T(8,128)(2,1)S(1)} %pack.1), channel_id=1, source_target_pairs={{0,256},{256,0},{1,257},{257,1},{2,258},{258,2},{3,259},{259,3},{4... | collective-permute-start | bytes 2654216 | tf_op jit(solution)/shard_map/ppermute | solution.py:474
  37.3 2.0 collective-permute-done.refs_4_
  39.4 1.2 copy-done.10
  40.6 1.2 copy-done.11
  41.8 0.8 copy-done.22
  42.6 3.4 %prepare.1 = (bf16[2,2,1024,128]{3,2,1,0:T(8,128)(2,1)S(1)}, bf16[256,1024]{1,0:T(8,128)(2,1)S(1)}, bf16[256,1024]{1,0:T(8,128)(2,1)S(1)}, bf16[2,16,1024]{2,1,0...) custom-call(s32[2]{0:T(128)S(1)} %pad_add_fusion.refs_0_, ...), custom_call_target="tpu_custom_call" | custom-call | bytes 7634944 | tf_op jit(solution)/shard_map/prepare/pallas_call | solution.py:187
  46.0 13.6 %all_to_all.41.refs_1_ = bf16[8,304,128]{2,1,0:T(8,128)(2,1)S(1)} all-to-all(bf16[8,304,128]{2,1,0:T(8,128)(2,1)S(1)} %get-tuple-element.26), channel_id=1, replica_groups=mesh['section'=2,'fsdp'=64,'tp'=4] {'section','tp'}, dimensions={0} | all-to-all | bytes 1245184 | tf_op jit(solution)/shard_map/all_to_all | solution.py:478
  59.6 1.5 entry_norm.1
  61.1 0.8 copy-done.13
  61.9 30.6 %all-gather.2.cloned.1.call-done.refs_3_.refs_4_.refs_5_.refs_7_ = bf16[8,2,128,1024]{3,2,1,0:T(8,128)(2,1)} async-done(((bf16[1,2,128,1024]{3,2,1,0:T(8,128)(2,1)}), bf16[8,2,128,1024]{3,2,1,0:T(8,128)(2,1)}) %all-gather.2.cloned.1.call-update) | async-done | bytes 4194320 | tf_op jit(solution)/shard_map/all_gather | solution.py:515
  92.6 2.2 %copy-done = bf16[8,2,128,1024]{3,2,1,0:T(8,128)(2,1)S(1)} copy-done((bf16[8,2,128,1024]{3,2,1,0:T(8,128)(2,1)S(1)}, bf16[8,2,128,1024]{3,2,1,0:T(8,128)(2,1)}, u32[]{:S(2)}) %copy-start) | copy-done | bytes 4194328
  94.8 3.3 %values_0.1 = bf16[8,256,128]{2,1,0:T(8,128)(2,1)} custom-call(bf16[256,1024]{1,0:T(8,128)(2,1)S(1)} %get-tuple-element.30.refs_0_.refs_7_, bf16[2,16,1024]{2,1,0:T(8,128)(2,1)S(1)} %get-tuple-element.31.refs_1_.refs_2_.refs_7_.refs_3_.refs_4_, bf16[2,16,1024]{2,1,0:T(8,128)(2,1)S(1)} %get-tuple-element.28.refs_3_.refs_2_.refs_4_, ...), custom_call_target="tpu_custom_call" | custom-call | bytes 5373952 | tf_op jit(solution)/shard_map/values_0/pallas_call | solution.py:187
  98.0 4.9 %all-to-all-start.2 = ((bf16[8,256,128]{2,1,0:T(8,128)(2,1)}), bf16[8,256,128]{2,1,0:T(8,128)(2,1)S(1)}, u32[]{:S(2)}, u32[]{:S(2)}) async-start(bf16[8,256,128]{2,1,0:T(8,128)(2,1)} %values_0.1), calls=%async_computation.2 | async-start | bytes 1048576 | tf_op jit(solution)/shard_map/all_to_all | solution.py:478
  103.0 2.2 %copy-done.1 = bf16[8,2,128,1024]{3,2,1,0:T(8,128)(2,1)S(1)} copy-done((bf16[8,2,128,1024]{3,2,1,0:T(8,128)(2,1)S(1)}, bf16[8,2,128,1024]{3,2,1,0:T(8,128)(2,1)}, u32[]{:S(2)}) %copy-start.1) | copy-done | bytes 4194328
  105.2 1.0 copy-done.14
  106.2 1.4 scaled_1.1.refs_3_.refs_2_
  107.6 4.7 %all-to-all-done.2.refs_0_ = bf16[8,256,128]{2,1,0:T(8,128)(2,1)S(1)} async-done(((bf16[8,256,128]{2,1,0:T(8,128)(2,1)}), bf16[8,256,128]{2,1,0:T(8,128)(2,1)S(1)}, u32[]{:S(2)}, u32[]{:S(2)}) %all-to-all-start.2) | async-done | bytes 524320 | tf_op jit(solution)/shard_map/all_to_all | solution.py:478
  112.3 0.8 copy-done.5
  113.1 1.0 copy-done.6
  114.2 1.0 first_output.1
  115.2 8.3 %all_to_all.42.refs_0_ = f32[8,8,256]{2,1,0:T(8,128)S(1)} all-to-all(f32[8,8,256]{2,1,0:T(8,128)S(1)} %get-tuple-element.36), channel_id=1, replica_groups=mesh['section'=2,'fsdp'=64,'tp'=4] {'section','tp'}, dimensions={0} | all-to-all | bytes 131072 | tf_op jit(solution)/shard_map/all_to_all | solution.py:478
  123.5 1.0 copy-done.17
  124.5 2.7 %first_gradient.1 = (bf16[256,1024]{1,0:T(8,128)(2,1)S(1)}, f32[8,256]{1,0:T(8,128)S(1)}, f32[16,1024]{1,0:T(8,128)S(1)}, bf16[8,304,128]{2,1,0:T(8,128)(2,1)S(1)}) custom-call(f32[8,8,256]{2,1,0:T(8,128)S(1)} %all_to_all.42.refs_0_, bf16[256,1024]{1,0:T(8,128)(2,1)S(1)} %get-tuple-element.35.refs_1_.refs_0_.refs_2_, ...), custom_call_target="tpu_custom_call" | custom-call | bytes 4710400 | tf_op jit(solution)/shard_map/first_gradient/pallas_call | solution.py:187
  127.2 0.8 copy-done.12
  128.0 0.8 copy-done.18
  128.9 3.6 %values_1.1 = bf16[8,256,128]{2,1,0:T(8,128)(2,1)} custom-call(bf16[256,1024]{1,0:T(8,128)(2,1)S(1)} %get-tuple-element.35.refs_1_.refs_0_.refs_2_, f32[8,256]{1,0:T(8,128)S(1)} %get-tuple-element.39.refs_1_.refs_4_, bf16[2,16,1024]{2,1,0:T(8,128)(2,1)S(1)} %get-tuple-element.29.refs_4_.refs_3_.refs_6_.refs_2_.refs_5_, ...), custom_call_target="tpu_custom_call" | custom-call | bytes 5447680 | tf_op jit(solution)/shard_map/values_1/pallas_call | solution.py:187
  132.5 0.0 reduce-scatter.2.cloned.1.call-update
  132.5 3.9 %all-to-all-start.4 = ((bf16[8,304,128]{2,1,0:T(8,128)(2,1)}), bf16[8,304,128]{2,1,0:T(8,128)(2,1)S(1)}, u32[]{:S(2)}, u32[]{:S(2)}) async-start(bf16[8,304,128]{2,1,0:T(8,128)(2,1)} %copy-done.12), calls=%async_computation.5 | async-start | bytes 1245184 | tf_op jit(solution)/shard_map/all_to_all | solution.py:478
  136.3 11.4 %all-to-all-done.4.refs_2_.refs_1_ = bf16[8,304,128]{2,1,0:T(8,128)(2,1)S(1)} async-done(((bf16[8,304,128]{2,1,0:T(8,128)(2,1)}), bf16[8,304,128]{2,1,0:T(8,128)(2,1)S(1)}, u32[]{:S(2)}, u32[]{:S(2)}) %all-to-all-start.4) | async-done | bytes 622624 | tf_op jit(solution)/shard_map/all_to_all | solution.py:478
  147.7 1.0 copy-done.8
  148.8 2.2 %map_gradient.1 = f32[16,24,128]{2,1,0:T(8,128)} custom-call(s32[2]{0:T(128)S(1)} %pad_add_fusion.refs_0_, bf16[8,304,128]{2,1,0:T(8,128)(2,1)S(1)} %all-to-all-done.4.refs_2_.refs_1_, bf16[2,16,1024]{2,1,0:T(8,128)(2,1)S(1)} %get-tuple-element.28.refs_3_.refs_2_.refs_4_, f32[16,256]{1,0:T(8,128)S(1)} %get-tuple-element.43.refs_3_, ...), custom_call_target="tpu_custom_call" | custom-call | bytes 1564672 | tf_op jit(solution)/shard_map/map_gradient/pallas_call | solution.py:187
  150.9 6.9 %all-to-all-start.5 = ((f32[16,24,128]{2,1,0:T(8,128)}), f32[16,24,128]{2,1,0:T(8,128)S(1)}, u32[]{:S(2)}, u32[]{:S(2)}) async-start(f32[16,24,128]{2,1,0:T(8,128)} %map_gradient.1), calls=%async_computation.6 | async-start | bytes 393216 | tf_op jit(solution)/shard_map/all_to_all | solution.py:616
  157.8 2.2 %copy-done.3 = bf16[8,2,128,1024]{3,2,1,0:T(8,128)(2,1)S(1)} copy-done((bf16[8,2,128,1024]{3,2,1,0:T(8,128)(2,1)S(1)}, bf16[8,2,128,1024]{3,2,1,0:T(8,128)(2,1)}, u32[]{:S(2)}) %copy-start.3) | copy-done | bytes 4194328
  160.0 1.0 copy-done.19
  161.1 3.7 %slot_gradient.1 = bf16[2,96,1024]{2,1,0:T(8,128)(2,1)S(1)} custom-call(s32[2]{0:T(128)S(1)} %bitcast.43, s32[2]{0:T(128)S(1)} %bitcast.45, bf16[8,304,128]{2,1,0:T(8,128)(2,1)S(1)} %all-to-all-done.4.refs_2_.refs_1_, bf16[2,16,1024]{2,1,0:T(8,128)(2,1)S(1)} %get-tuple-element.28.refs_3_.refs_2_.refs_4_, ...), custom_call_target="tpu_custom_call" | custom-call | bytes 6463488 | tf_op jit(solution)/shard_map/slot_gradient/pallas_call | solution.py:187
  164.8 0.7 select_bitcast_fusion
  165.5 2.0 collective-permute-start.2
  167.5 0.0 reduce-scatter.2.cloned.1.call-done
  167.5 0.8 copy-done.23
  168.4 0.5 second_output.1
  168.9 0.1 broadcast_select_fusion.2
  168.9 2.3 %collective-permute-start.1 = (bf16[256,1024]{1,0:T(8,128)(2,1)S(1)}, bf16[256,1024]{1,0:T(8,128)(2,1)}, u32[]{:S(2)}, u32[]{:S(2)}) collective-permute-start(bf16[256,1024]{1,0:T(8,128)(2,1)S(1)} %broadcast_select_fusion.2), channel_id=1, source_target_pairs={{0,256},{256,0},{1,257},{257,1},{2,258},{258,2},{3,259},{259,3},{4... | collective-permute-start | bytes 1572872 | tf_op jit(solution)/shard_map/ppermute | solution.py:474
  171.2 0.8 near_sum.1
  172.0 6.3 %all-to-all-start.6 = ((bf16[8,2,24,128]{3,2,1,0:T(8,128)(2,1)}), bf16[8,2,24,128]{3,2,1,0:T(8,128)(2,1)S(1)}, u32[]{:S(2)}, u32[]{:S(2)}) async-start(bf16[8,2,24,128]{3,2,1,0:T(8,128)(2,1)} %near_sum.1), calls=%async_computation.7 | async-start | bytes 196608 | tf_op jit(solution)/shard_map/all_to_all | solution.py:618
  178.3 1.0 bitcast_select_fusion.1
  179.3 6.5 %all-to-all-done.6.refs_0_ = bf16[8,2,24,128]{3,2,1,0:T(8,128)(2,1)S(1)} async-done(((bf16[8,2,24,128]{3,2,1,0:T(8,128)(2,1)}), bf16[8,2,24,128]{3,2,1,0:T(8,128)(2,1)S(1)}, u32[]{:S(2)}, u32[]{:S(2)}) %all-to-all-start.6) | async-done | bytes 98336 | tf_op jit(solution)/shard_map/all_to_all | solution.py:618
  185.7 0.8 far_sum.1
  186.5 6.5 %all-to-all-start.7 = ((bf16[8,2,24,128]{3,2,1,0:T(8,128)(2,1)}), bf16[8,2,24,128]{3,2,1,0:T(8,128)(2,1)S(1)}, u32[]{:S(2)}, u32[]{:S(2)}) async-start(bf16[8,2,24,128]{3,2,1,0:T(8,128)(2,1)} %far_sum.1), calls=%async_computation.8 | async-start | bytes 196608 | tf_op jit(solution)/shard_map/all_to_all | solution.py:621
  193.0 0.8 maximum_bitcast_fusion
  193.7 6.8 %all-to-all-done.7.refs_0_ = bf16[8,2,24,128]{3,2,1,0:T(8,128)(2,1)S(1)} async-done(((bf16[8,2,24,128]{3,2,1,0:T(8,128)(2,1)}), bf16[8,2,24,128]{3,2,1,0:T(8,128)(2,1)S(1)}, u32[]{:S(2)}, u32[]{:S(2)}) %all-to-all-start.7) | async-done | bytes 98336 | tf_op jit(solution)/shard_map/all_to_all | solution.py:621
  200.6 0.9 maps.1
  201.4 1.1 broadcast_select_fusion.1
  202.6 1.1 pad_maximum_fusion
  (43 shorter events, 0.1 us)
Async XLA Ops:
  7.2 26.2 %copy-start.27 = (bf16[1,2048]{1,0:T(2,128)(2,1)S(1)}, bf16[1,2048]{1,0:T(2,128)(2,1)}, u32[]{:S(2)}) copy-start(bf16[1,2048]{1,0:T(2,128)(2,1)} %param.19) | copy-start | bytes 12292
  7.2 26.3 %copy-start.21 = (bf16[1,16,1024]{2,1,0:T(8,128)(2,1)S(1)}, bf16[1,16,1024]{2,1,0:T(8,128)(2,1)}, u32[]{:S(2)}) copy-start(bf16[1,16,1024]{2,1,0:T(8,128)(2,1)} %param.22) | copy-start | bytes 98308
  7.2 26.3 %copy-start.20 = (bf16[1,2048,16]{1,2,0:T(8,128)(2,1)S(1)}, bf16[1,2048,16]{1,2,0:T(8,128)(2,1)}, u32[]{:S(2)}) copy-start(bf16[1,2048,16]{1,2,0:T(8,128)(2,1)} %param.21) | copy-start | bytes 196612
  7.2 26.3 %copy-start.15 = (bf16[1,2,128,256]{3,2,1,0:T(8,128)(2,1)S(1)}, bf16[1,2,128,256]{3,2,1,0:T(8,128)(2,1)}, u32[]{:S(2)}) copy-start(bf16[1,2,128,256]{3,2,1,0:T(8,128)(2,1)} %param.18) | copy-start | bytes 393220
  7.2 26.3 %copy-start.4 = (bf16[1,2,128,2048]{3,2,1,0:T(8,128)(2,1)S(1)}, bf16[1,2,128,2048]{3,2,1,0:T(8,128)(2,1)}, u32[]{:S(2)}) copy-start(bf16[1,2,128,2048]{3,2,1,0:T(8,128)(2,1)} %param.17) | copy-start | bytes 3145732
  7.2 26.3 %copy-start.9 = (bf16[1,1,96,2048]{3,2,1,0:T(8,128)(2,1)S(1)}, bf16[1,1,96,2048]{3,2,1,0:T(8,128)(2,1)}, u32[]{:S(2)}) copy-start(bf16[1,1,96,2048]{3,2,1,0:T(8,128)(2,1)} %param.13) | copy-start | bytes 1179652
  7.2 85.3 %all-gather.2.cloned.1.call-start = ((), (), s32[]{:S(2)}) async-start(), calls=%async_computation.9 | async-start | bytes 4718592 | tf_op jit(solution)/shard_map/all_gather | solution.py:515
  8.3 31.0 %copy-start.24 = (s32[2,1]{0,1:T(1,128)S(1)}, s32[2,1]{0,1:T(1,128)}, u32[]{:S(2)}) copy-start(s32[2,1]{0,1:T(1,128)} %param.14) | copy-start | bytes 28
  8.4 31.0 %copy-start.25 = (s32[2,1]{0,1:T(1,128)S(1)}, s32[2,1]{0,1:T(1,128)}, u32[]{:S(2)}) copy-start(s32[2,1]{0,1:T(1,128)} %param.15) | copy-start | bytes 28
  8.4 31.0 %copy-start.26 = (s32[2,1]{0,1:T(1,128)S(1)}, s32[2,1]{0,1:T(1,128)}, u32[]{:S(2)}) copy-start(s32[2,1]{0,1:T(1,128)} %param.16) | copy-start | bytes 28
  34.4 4.9 %collective-permute-start = (bf16[432,1024]{1,0:T(8,128)(2,1)S(1)}, bf16[432,1024]{1,0:T(8,128)(2,1)S(1)}, u32[]{:S(2)}, u32[]{:S(2)}) collective-permute-start(bf16[432,1024]{1,0:T(8,128)(2,1)S(1)} %pack.1), channel_id=1, source_target_pairs={{0,256},{256,0},{1,257},{257,1},{2,258},{258,2},{3,259},{259,3},{4... | collective-permute-start | bytes 2654216 | tf_op jit(solution)/shard_map/ppermute | solution.py:474
  39.4 1.2 copy-start.10
  40.6 1.2 copy-start.11
  41.8 0.8 copy-start.22
  46.0 13.6 %copy-start.16 = (bf16[256,1024]{1,0:T(8,128)(2,1)}, bf16[256,1024]{1,0:T(8,128)(2,1)S(1)}, u32[]{:S(2)}) copy-start(bf16[256,1024]{1,0:T(8,128)(2,1)S(1)} %get-tuple-element.37.refs_3_) | copy-start | bytes 1572868
  61.1 0.8 copy-start.13
  61.9 36.1 %copy-start.7 = (bf16[256,1024]{1,0:T(8,128)(2,1)}, bf16[256,1024]{1,0:T(8,128)(2,1)S(1)}, u32[]{:S(2)}) copy-start(bf16[256,1024]{1,0:T(8,128)(2,1)S(1)} %get-tuple-element.30.refs_0_.refs_7_) | copy-start | bytes 1572868
  92.6 2.2 %copy-start = (bf16[8,2,128,1024]{3,2,1,0:T(8,128)(2,1)S(1)}, bf16[8,2,128,1024]{3,2,1,0:T(8,128)(2,1)}, u32[]{:S(2)}) copy-start(bf16[8,2,128,1024]{3,2,1,0:T(8,128)(2,1)} %all-gather.2.cloned.1.call-done.refs_3_.refs_4_.refs_5_.refs_7_) | copy-start | bytes 12582916
  98.0 14.3 %all-to-all-start.2 = ((bf16[8,256,128]{2,1,0:T(8,128)(2,1)}), bf16[8,256,128]{2,1,0:T(8,128)(2,1)S(1)}, u32[]{:S(2)}, u32[]{:S(2)}) async-start(bf16[8,256,128]{2,1,0:T(8,128)(2,1)} %values_0.1), calls=%async_computation.2 | async-start | bytes 1048576 | tf_op jit(solution)/shard_map/all_to_all | solution.py:478
  103.0 64.6 %reduce-scatter.2.cloned.1.call-start = ((), (), s32[]{:S(2)}) async-start(), calls=%async_computation.10 | async-start | bytes 589824 | tf_op jit(solution)/shard_map/reduce_scatter | solution.py:598
  103.0 2.2 %copy-start.1 = (bf16[8,2,128,1024]{3,2,1,0:T(8,128)(2,1)S(1)}, bf16[8,2,128,1024]{3,2,1,0:T(8,128)(2,1)}, u32[]{:S(2)}) copy-start(bf16[8,2,128,1024]{3,2,1,0:T(8,128)(2,1)} %all-gather.2.cloned.1.call-done.refs_3_.refs_4_.refs_5_.refs_7_) | copy-start | bytes 12582916
  105.2 1.0 copy-start.14
  112.3 0.8 copy-start.5
  113.1 1.0 copy-start.6
  114.2 14.7 %copy-start.2 = (bf16[8,2,128,1024]{3,2,1,0:T(8,128)(2,1)S(1)}, bf16[8,2,128,1024]{3,2,1,0:T(8,128)(2,1)}, u32[]{:S(2)}) copy-start(bf16[8,2,128,1024]{3,2,1,0:T(8,128)(2,1)} %all-gather.2.cloned.1.call-done.refs_3_.refs_4_.refs_5_.refs_7_) | copy-start | bytes 12582916
  123.5 1.0 copy-start.17
  127.2 0.8 copy-start.12
  128.0 0.8 copy-start.18
  132.5 15.2 %all-to-all-start.4 = ((bf16[8,304,128]{2,1,0:T(8,128)(2,1)}), bf16[8,304,128]{2,1,0:T(8,128)(2,1)S(1)}, u32[]{:S(2)}, u32[]{:S(2)}) async-start(bf16[8,304,128]{2,1,0:T(8,128)(2,1)} %copy-done.12), calls=%async_computation.5 | async-start | bytes 1245184 | tf_op jit(solution)/shard_map/all_to_all | solution.py:478
  147.7 1.0 copy-start.8
  150.9 20.3 %all-to-all-start.5 = ((f32[16,24,128]{2,1,0:T(8,128)}), f32[16,24,128]{2,1,0:T(8,128)S(1)}, u32[]{:S(2)}, u32[]{:S(2)}) async-start(f32[16,24,128]{2,1,0:T(8,128)} %map_gradient.1), calls=%async_computation.6 | async-start | bytes 393216 | tf_op jit(solution)/shard_map/all_to_all | solution.py:616
  157.8 2.2 %copy-start.3 = (bf16[8,2,128,1024]{3,2,1,0:T(8,128)(2,1)S(1)}, bf16[8,2,128,1024]{3,2,1,0:T(8,128)(2,1)}, u32[]{:S(2)}) copy-start(bf16[8,2,128,1024]{3,2,1,0:T(8,128)(2,1)} %all-gather.2.cloned.1.call-done.refs_3_.refs_4_.refs_5_.refs_7_) | copy-start | bytes 12582916
  160.0 1.0 copy-start.19
  165.5 12.8 %collective-permute-start.2 = (bf16[96,1024]{1,0:T(8,128)(2,1)}, bf16[96,1024]{1,0:T(8,128)(2,1)}, u32[]{:S(2)}, u32[]{:S(2)}) collective-permute-start(bf16[96,1024]{1,0:T(8,128)(2,1)} %select_bitcast_fusion), channel_id=1, source_target_pairs={{0,256},{256,0},{1,257},{257,1},{2,258},{258,2},{3,259},{259,3},{4... | collective-permute-start | bytes 589832 | tf_op jit(solution)/shard_map/ppermute | solution.py:474
  167.5 0.8 copy-start.23
  168.9 32.5 %collective-permute-start.1 = (bf16[256,1024]{1,0:T(8,128)(2,1)S(1)}, bf16[256,1024]{1,0:T(8,128)(2,1)}, u32[]{:S(2)}, u32[]{:S(2)}) collective-permute-start(bf16[256,1024]{1,0:T(8,128)(2,1)S(1)} %broadcast_select_fusion.2), channel_id=1, source_target_pairs={{0,256},{256,0},{1,257},{257,1},{2,258},{258,2},{3,259},{259,3},{4... | collective-permute-start | bytes 1572872 | tf_op jit(solution)/shard_map/ppermute | solution.py:474
  172.0 13.7 %all-to-all-start.6 = ((bf16[8,2,24,128]{3,2,1,0:T(8,128)(2,1)}), bf16[8,2,24,128]{3,2,1,0:T(8,128)(2,1)S(1)}, u32[]{:S(2)}, u32[]{:S(2)}) async-start(bf16[8,2,24,128]{3,2,1,0:T(8,128)(2,1)} %near_sum.1), calls=%async_computation.7 | async-start | bytes 196608 | tf_op jit(solution)/shard_map/all_to_all | solution.py:618
  186.5 14.0 %all-to-all-start.7 = ((bf16[8,2,24,128]{3,2,1,0:T(8,128)(2,1)}), bf16[8,2,24,128]{3,2,1,0:T(8,128)(2,1)S(1)}, u32[]{:S(2)}, u32[]{:S(2)}) async-start(bf16[8,2,24,128]{3,2,1,0:T(8,128)(2,1)} %far_sum.1), calls=%async_computation.8 | async-start | bytes 196608 | tf_op jit(solution)/shard_map/all_to_all | solution.py:621
Sparse Core Ops, SparseCore 0:
  33.5 59.0 all-gather.1
  132.6 34.4 reduce-scatter.1

commit v4 on v3

--- a/solution.py
+++ b/solution.py
@@ -103,103 +103,28 @@
     return lax.rsqrt(squares / MODEL_WIDTH + EPS)
 
 
-class Loaded:
-    def __init__(self, buffer, copies):
-        self.buffer, self.copies, self.done = buffer, copies, set()
-        for copy in copies:
-            copy.start()
-
-    def __call__(self, part=None):
-        for at in range(len(self.copies)) if part is None else (part,):
-            if at not in self.done:
-                self.copies[at].wait()
-                self.done.add(at)
-        return self.buffer
-
-
-class Stored:
-    def __init__(self, buffer, target, semaphores):
-        self.buffer, self.target, self.semaphores, self.copies = buffer, target, semaphores, []
-
-    def send(self, repeated=False):
-        targets = [self.target.at[peer] for peer in range(PEERS)] if repeated else [self.target]
-        for at, target in enumerate(targets):
-            copy = pltpu.make_async_copy(self.buffer, target, self.semaphores.at[at])
-            copy.start()
-            self.copies.append(copy)
-
-    def finish(self):
-        for copy in self.copies:
-            copy.wait()
-
-
-def whole(scalars, ref, buffer):
-    return [(ref, buffer)]
-
-
-def columns_of(layer):
-    def view(scalars, ref, buffer):
-        pairs = [pl.ds(2 * at, 2) for at in range(KVH // 2)]
-        return [(ref.at[pair, layer], buffer.at[pair]) for pair in pairs]
-
-    return view
-
-
-def call(kernel, name, results, scalars, operands):
-    arrays = [o[0] if isinstance(o, tuple) else o for o in operands]
-    manual_in = [isinstance(o, tuple) for o in operands]
-    manual_out = [len(r) == 3 for r in results]
-    n_scalars, n_arrays, n_results = len(scalars), len(arrays), len(results)
-    most = KVH // 2
+def call(kernel, name, results, scalars, arrays, after=(), scratch=()):
+    n_read = len(scalars) + len(arrays)
 
     def body(*refs):
-        scalar_refs = refs[:n_scalars]
-        ins = list(refs[n_scalars : n_scalars + n_arrays])
-        outs = list(refs[n_scalars + n_arrays : n_scalars + n_arrays + n_results])
-        scratch = list(refs[n_scalars + n_arrays + n_results :])
-        in_semaphores, out_semaphores = scratch.pop(), None
-        out_semaphores, in_semaphores = in_semaphores, scratch.pop()
-        loads, stores = [], []
-        for at in range(n_arrays):
-            if manual_in[at]:
-                buffer = scratch.pop(0)
-                pairs = operands[at][2](scalar_refs, ins[at], buffer)
-                copies = [
-                    pltpu.make_async_copy(*pair, in_semaphores.at[at * most + k])
-                    for k, pair in enumerate(pairs)
-                ]
-                ins[at] = Loaded(buffer, copies)
-                loads.append(ins[at])
-        for at in range(n_results):
-            if manual_out[at]:
-                outs[at] = Stored(scratch.pop(0), outs[at], out_semaphores.at[at])
-                stores.append(outs[at])
-        kernel(*scalar_refs, *ins, *outs)
-        for load in loads:
-            load()
-        for store in stores:
-            store.finish()
+        kernel(*refs[:n_read], *refs[n_read + len(after) :])
 
     moved = sum(a.size * a.dtype.itemsize for a in arrays)
-    moved += sum(math.prod(r[0]) * jnp.dtype(r[1]).itemsize for r in results)
+    moved += sum(math.prod(shape) * jnp.dtype(dtype).itemsize for shape, dtype in results)
     in_vmem = pl.BlockSpec(memory_space=pltpu.VMEM)
-    in_hbm = pl.BlockSpec(memory_space=pltpu.HBM)
+    anywhere = pl.BlockSpec(memory_space=pl.ANY)
     return pl.pallas_call(
         body,
-        out_shape=[jax.ShapeDtypeStruct(r[0], r[1]) for r in results],
-        in_specs=[pl.BlockSpec(memory_space=pltpu.SMEM)] * n_scalars
-        + [in_hbm if manual else in_vmem for manual in manual_in],
-        out_specs=[in_hbm if manual else in_vmem for manual in manual_out],
-        scratch_shapes=[pltpu.VMEM(o[1], o[0].dtype) for o in operands if isinstance(o, tuple)]
-        + [pltpu.VMEM(r[2], r[1]) for r in results if len(r) == 3]
-        + [
-            pltpu.SemaphoreType.DMA((n_arrays * most,)),
-            pltpu.SemaphoreType.DMA((n_results, PEERS)),
-        ],
+        out_shape=[jax.ShapeDtypeStruct(shape, dtype) for shape, dtype in results],
+        in_specs=[pl.BlockSpec(memory_space=pltpu.SMEM)] * len(scalars)
+        + [in_vmem] * len(arrays)
+        + [anywhere] * len(after),
+        out_specs=[in_vmem] * len(results),
+        scratch_shapes=list(scratch),
         compiler_params=pltpu.CompilerParams(vmem_limit_bytes=VMEM_BYTES),
         cost_estimate=pl.CostEstimate(flops=0, bytes_accessed=moved, transcendentals=0),
         name=name,
-    )(*scalars, *arrays)
+    )(*scalars, *arrays, *after)
 
 
 def pack_kernel(core, visual, queries, keys, down, up, gain, out):
@@ -297,7 +222,7 @@
 def partial_values(rows, down, up, columns, out):
     adapter = (ADAPTER_SCALE * nt(rows, down)).astype(BF)
     for pair in range(KVH // 2):
-        weight = columns(pair)[2 * pair : 2 * pair + 2].reshape(2 * HD, HALF)
+        weight = columns[2 * pair : 2 * pair + 2].reshape(2 * HD, HALF)
         span = slice(2 * pair * HD, (2 * pair + 2) * HD)
         partial = (nt(rows, weight) + nn(adapter, up[:, span])).astype(BF)
         for at in range(2):
@@ -308,29 +233,23 @@
     partial_values(normed[...], downs[0], ups[0], columns, out)
 
 
-def second_values_kernel(hidden, totals, gains, downs, ups, columns, out):
-    column = inverse_of(rows_to_columns(totals[...])[:, 0:1])
-    gain = gains[1][0:1, :].astype(F32)
-    normed = (hidden[...].astype(F32) * gain * column).astype(BF)
-    partial_values(normed, downs[1], ups[1], columns, out)
-
-
 def weighted_gradient(gradient_of, lora_gradient, down, gain, columns):
     grad = tn(lora_gradient.astype(BF), down)
     for pair in range(KVH // 2):
-        weight = columns(pair)[2 * pair : 2 * pair + 2].reshape(2 * HD, HALF)
+        weight = columns[2 * pair : 2 * pair + 2].reshape(2 * HD, HALF)
         grad = grad + nn(gradient_of(pair), weight)
     return grad * gain[0:1, :].astype(F32)
 
 
 def scaled_kernel(full_gradient, lora_gradient, downs, gains, columns, scaled):
-    scaled[...] = weighted_gradient(
+    grad = weighted_gradient(
         lambda pair: full_gradient[:, 2 * pair * HD : (2 * pair + 2) * HD],
         lora_gradient[...],
         downs[1],
         gains[1],
         columns,
     )
+    scaled[...] = grad.astype(BF)
 
 
 def attended_rows(weights, layer, value_rows):
@@ -343,7 +262,10 @@
     )
 
 
-def first_output_kernel(received, weights, entry, scaled, hidden, value_rows, payload):
+def first_output_kernel(
+    received, weights, entry, scaled, gains, downs, ups, columns,
+    hidden, value_rows, payload, partial,
+):
     values = received[0].astype(F32)
     for peer in range(1, PEERS):
         values = values + received[peer].astype(F32)
@@ -353,10 +275,12 @@
     hidden[...] = output
     output_float = output.astype(F32)
     squares = jnp.sum(output_float * output_float, axis=-1, keepdims=True)
-    dots = jnp.sum(output_float * scaled[...], axis=-1, keepdims=True)
+    dots = jnp.sum(output_float * scaled[...].astype(F32), axis=-1, keepdims=True)
     block = columns_to_rows(squares, dots)
     for peer in range(PEERS):
         payload[peer] = block
+    gained = (output_float * gains[1][0:1, :].astype(F32)).astype(BF)
+    partial_values(gained, downs[1], ups[1], columns, partial)
 
 
 def first_gradient_kernel(
@@ -372,10 +296,9 @@
     factor = column * column * column * sums[:, 1:2] / MODEL_WIDTH
     hidden_float = hidden[...].astype(F32)
     grad = (
-        cotangent_half[...].astype(F32) + column * scaled[...] - hidden_float * factor
+        cotangent_half[...].astype(F32) + column * scaled[...].astype(F32) - hidden_float * factor
     ).astype(BF)
-    gradient.buffer[...] = grad
-    gradient.send()
+    gradient[...] = grad
     gained = hidden_float * gains[1][0:1, :].astype(F32)
     low_rank = nt(downs[1], gained.astype(BF))
     value_gradient = jnp.concatenate(
@@ -383,8 +306,9 @@
         axis=0,
     ).astype(BF)
     dots = jnp.sum(value_gradient.astype(F32) * value_rows[...], axis=-1, keepdims=True)
-    payload.buffer[...] = payload_block(value_gradient, dots, low_rank)
-    payload.send(repeated=True)
+    block = payload_block(value_gradient, dots, low_rank)
+    for peer in range(PEERS):
+        payload[peer] = block
     normed = (gained * column).astype(BF)
     down_gradient[...] = nn(lora_gradient[...].astype(BF), normed)
 
@@ -400,7 +324,7 @@
     lora_0 = ADAPTER_SCALE * nt(ups[0], gathered_gradient(received))
     own = received[core[0] * 4 + core[1], :ROWS, :]
     adapter_1 = (low_rank * inverse_of(totals[0:1, :])).astype(BF)
-    down = (nn(lora_0.astype(BF), normed_0()[...]), down_gradient_1[...])
+    down = (nn(lora_0.astype(BF), normed_0[...]), down_gradient_1[...])
     up = (
         ADAPTER_SCALE * nn(adapter_0[...].astype(BF), own),
         ADAPTER_SCALE * nn(adapter_1, gradient_1[...]),
@@ -430,17 +354,34 @@
         out[peer] = total.astype(BF)
 
 
-def maps_kernel(received, down_sum, up_sum, *, scale):
+def finish_kernel(
+    core, received, own_hidden, other_hidden, own_slots, other_slots,
+    hidden, slots, down_sum, up_sum, semaphores, *, scale,
+):
+    copies = []
+    own = core[0]
+    for at, (part, own_part, other_part) in enumerate(
+        ((hidden, own_hidden, other_hidden), (slots, own_slots, other_slots))
+    ):
+        for k, (half, block) in enumerate(((own, own_part), (1 - own, other_part))):
+            to = pl.ds(pl.multiple_of(half * HALF, HALF), HALF)
+            copy = pltpu.make_async_copy(block, part.at[:, to], semaphores.at[2 * at + k])
+            copy.start()
+            copies.append(copy)
     for half in range(2):
         for y in range(8):
             block = received[y, half].astype(F32) * scale
             at = half * HALF + y * HD
             down_sum[:, at : at + HD] = block[:RANK, :]
             up_sum[2 * y : 2 * y + 2, half * HD : (half + 1) * HD] = block[RANK : RANK + 2, :]
+    for copy in copies:
+        copy.wait()
 
 
 def slot_gradient_kernel(
-    counts, starts, received, ups, downs, gains, sums, columns, gradient, entry, slots
+    core, counts, starts,
+    received, ups, downs, gains, sums, columns, gradient, entry,
+    own_slots, other_slots,
 ):
     rows, _ = total_of_payloads(received)
     lora_gradient = ADAPTER_SCALE * nt(ups[0], gathered_gradient(received))
@@ -456,18 +397,28 @@
     column = inverse_of(rows_to_columns(sums[...])[:, 0:1])
     factor = column * column * rows_to_columns(rows)[:, 0:1] / MODEL_WIDTH
     grad = (
-        gradient()[...].astype(F32) + column * scaled - entry()[...].astype(F32) * factor
+        gradient[...].astype(F32) + column * scaled - entry[...].astype(F32) * factor
     ).astype(BF)
     slot = lax.broadcasted_iota(jnp.int32, (VIS, SEQ), 0)
     position = lax.broadcasted_iota(jnp.int32, (VIS, SEQ), 1)
-    for m in range(MB):
-        picking = ((position == starts[m] + slot) & (slot < counts[m] * TOKT)).astype(F32).astype(BF)
-        slots[m] = nn(picking, grad[m * SEQ : (m + 1) * SEQ, :]).astype(BF)
-
-
-def second_output_kernel(values, weights, hidden, out):
-    attended = attended_rows(weights, 1, values[...])
-    out[...] = (hidden[...].astype(F32) + attended).astype(BF)
+    first = core[0] == 0
+    above, below = grad[:SEQ, :], grad[SEQ:, :]
+    for index, rows, out in (
+        (core[0], jnp.where(first, above, below), own_slots),
+        (1 - core[0], jnp.where(first, below, above), other_slots),
+    ):
+        inside = (position == starts[index] + slot) & (slot < counts[index] * TOKT)
+        out[...] = nn(inside.astype(F32).astype(BF), rows).astype(BF)
+
+
+def second_output_kernel(core, values, totals, weights, hidden, own_hidden, other_hidden):
+    column = inverse_of(rows_to_columns(totals[...])[:, 0:1])
+    value_rows = (values[...].astype(F32) * column).astype(BF)
+    attended = attended_rows(weights, 1, value_rows)
+    output = (hidden[...].astype(F32) + attended).astype(BF)
+    first = core[0] == 0
+    own_hidden[...] = jnp.where(first, hidden[...], output)
+    other_hidden[...] = jnp.where(first, output, hidden[...])
 
 
 def swap_cores(block):
@@ -538,8 +489,7 @@
         (swap_cores(packed), *own, embeddings, cotangent),
     )
 
-    def weight_of(layer):
-        return (columns, (KVH, HD, HALF), columns_of(layer))
+    columns_0, columns_1 = columns[:, 0], columns[:, 1]
 
     normed_0, sums_0, adapter_0, full_gradient_1, own_gradient_1, lora_gradient_1 = call(
         entry_norm_kernel,
@@ -549,30 +499,31 @@
         (to_heads(payload), entry, ups, gains),
     )
     (partial_0,) = call(
-        first_values_kernel, "values_0", [blocks], (), (normed_0, downs, ups, weight_of(0))
+        first_values_kernel, "values_0", [blocks], (), (normed_0, downs, ups, columns_0)
     )
     (scaled_1,) = call(
         scaled_kernel,
         "scaled_1",
-        [((ROWS, HALF), F32)],
+        [wide],
         (),
-        (full_gradient_1, lora_gradient_1, downs, gains, weight_of(1)),
-    )
-    hidden_0, value_rows, payload = call(
+        (full_gradient_1, lora_gradient_1, downs, gains, columns_1),
+    )
+    hidden_0, value_rows, payload, partial_1 = call(
         first_output_kernel,
         "first_output",
-        [wide, ((ROWS, HD), F32), ((PEERS, SUBLANES, ROWS), F32)],
+        [wide, ((ROWS, HD), F32), ((PEERS, SUBLANES, ROWS), F32), blocks],
         (),
-        (to_heads(partial_0), weights, entry, scaled_1),
-    )
+        (to_heads(partial_0), weights, entry, scaled_1, gains, downs, ups, columns_1),
+    )
+    values_1 = lax.psum_scatter(partial_1, ("section", "tp"), scatter_dimension=0)
     gradient, totals, down_gradient_1, payload = call(
         first_gradient_kernel,
         "first_gradient",
         [
-            wide + ((ROWS, HALF),),
+            wide,
             sums,
             ((RANK, HALF), F32),
-            mixed + ((R_PAY, HD),),
+            mixed,
         ],
         (),
         (
@@ -588,15 +539,6 @@
         ),
     )
     gathered = to_heads(payload)
-    (partial_1,) = call(
-        second_values_kernel,
-        "values_1",
-        [blocks],
-        (),
-        (hidden_0, totals, gains, downs, ups, weight_of(1)),
-    )
-    values_1 = lax.psum_scatter(partial_1, ("section", "tp"), scatter_dimension=0)
-
     (chunks,) = call(
         map_gradient_kernel,
         "map_gradient",
@@ -609,60 +551,50 @@
             totals,
             own_gradient_1,
             down_gradient_1,
-            (normed_0, normed_0.shape, whole),
+            normed_0,
         ),
     )
+    own_slots, other_slots = call(
+        slot_gradient_kernel,
+        "slot_gradient",
+        [((VIS, HALF), BF)] * 2,
+        (core, counts, begins),
+        (gathered, ups, downs, gains, sums_0, columns_0, gradient, entry),
+    )
+    other_slots = swap_cores(other_slots)
+    own_hidden, other_hidden = call(
+        second_output_kernel, "second_output", [wide] * 2, (core,), (values_1, totals, weights, hidden_0)
+    )
+    other_hidden = swap_cores(other_hidden)
+
     halves_of_maps = ((8, 2, M_ROWS, HD), BF)
     near = lax.all_to_all(chunks, ("section", "fsdp"), 0, 0, axis_index_groups=head_groups)
-    (near,) = call(near_sum_kernel, "near_sum", [halves_of_maps], (), (near,))
+    (near,) = call(
+        near_sum_kernel, "near_sum", [halves_of_maps], (), (near,), after=(other_slots,)
+    )
     far = lax.all_to_all(near, "fsdp", 0, 0, axis_index_groups=row_groups)
     (far,) = call(far_sum_kernel, "far_sum", [halves_of_maps], (), (far,))
     y_groups = [[z * n_y + y for y in range(n_y)] for z in range(KVH)]
     summed = lax.all_to_all(far, "fsdp", 0, 0, axis_index_groups=y_groups)
-    down_sum, up_sum = call(
-        functools.partial(maps_kernel, scale=1.0 / math.sqrt(MB * SEQ * n_fsdp)),
-        "maps",
-        [((RANK, 2 * HALF), F32), ((RANK, 2 * HD), F32)],
-        (),
-        (summed,),
-    )
-
-    (slots,) = call(
-        slot_gradient_kernel,
-        "slot_gradient",
-        [((MB, VIS, HALF), BF)],
-        (counts, begins),
-        (
-            gathered,
-            ups,
-            downs,
-            gains,
-            sums_0,
-            weight_of(0),
-            (gradient, gradient.shape, whole),
-            (entry, entry.shape, whole),
-        ),
-    )
-    (hidden_1,) = call(
-        second_output_kernel, "second_output", [wide], (), (values_1, weights, hidden_0)
-    )
-
-    first = section == 0
-
-    def halves(mine, theirs):
-        left = jnp.where(first, mine, theirs)
-        right = jnp.where(first, theirs, mine)
-        return jnp.concatenate([left, right], axis=-1)
-
-    slot_rows = halves(
-        jnp.where(first, slots[0], slots[1]), swap_cores(jnp.where(first, slots[1], slots[0]))
-    )
-    hidden = halves(
-        jnp.where(first, hidden_0, hidden_1), swap_cores(jnp.where(first, hidden_1, hidden_0))
-    )
+
+    in_vmem = pl.BlockSpec(memory_space=pltpu.VMEM)
+    anywhere = pl.BlockSpec(memory_space=pl.ANY)
+    hidden, slots, down_sum, up_sum = pl.pallas_call(
+        functools.partial(finish_kernel, scale=1.0 / math.sqrt(MB * SEQ * n_fsdp)),
+        out_shape=[
+            jax.ShapeDtypeStruct((ROWS, 2 * HALF), BF),
+            jax.ShapeDtypeStruct((VIS, 2 * HALF), BF),
+            jax.ShapeDtypeStruct((RANK, 2 * HALF), F32),
+            jax.ShapeDtypeStruct((RANK, 2 * HD), F32),
+        ],
+        in_specs=[pl.BlockSpec(memory_space=pltpu.SMEM), in_vmem] + [anywhere] * 4,
+        out_specs=[anywhere, anywhere, in_vmem, in_vmem],
+        scratch_shapes=[pltpu.SemaphoreType.DMA((4,))],
+        name="finish",
+    )(core, summed, own_hidden, other_hidden, own_slots, other_slots)
     return (
         hidden.reshape(1, MB, SEQ, 2 * HALF),
-        slot_rows[None, None],
+        slots[None, None],
         down_sum.T[None],
         up_sum[None],
     )

time: 213 us -> 259 us (1.22)
  blocking collectives: 46.9 us -> 87.5 us
  Pallas kernels: 26.5 us -> 62 us
  waiting for transfers between devices: 62.1 us -> 38.3 us
  starting transfers between devices: 35.6 us -> 19.5 us
  local copies, waits for them, and re-layouts: 20.2 us -> 34.1 us
  other arithmetic: 4.8 us -> 0.11 us
    pallas_call x14 -> x13, Pallas kernels: 26.5 us -> 62 us  [the longest x1 46.4 us: on_device(): pl.pallas_call(functools.partial(finish_kernel, scale=1.0 / math.sqrt(MB...]
    all_to_all x0 -> x2, blocking collectives: none -> 25.2 us  [the longest x1 13.8 us: on_device(): summed = lax.all_to_all(far, 'fsdp', 0, 0, axis_index_groups=y_groups)]
    all_to_all x2 -> x3, blocking collectives: 21.9 us -> 37.3 us  [to_heads(): return lax.all_to_all(block, ('section', 'tp'), 0, 0)]
    all_to_all x2 -> x0, waiting for transfers between devices: 13.3 us -> none  [the longest x1 6.82 us: on_device(): summed = lax.all_to_all(far, 'fsdp', 0, 0, axis_index_groups=y_groups)]
    all_to_all x2 -> x0, starting transfers between devices: 12.7 us -> none  [the longest x1 6.46 us: on_device(): summed = lax.all_to_all(far, 'fsdp', 0, 0, axis_index_groups=y_groups)]
    all_to_all x2 -> x1, waiting for transfers between devices: 16.1 us -> 5.2 us  [to_heads(): return lax.all_to_all(block, ('section', 'tp'), 0, 0)]
    unnamed x56 -> x106, local copies, waits for them, and re-layouts: 19.1 us -> 28.8 us
    squeeze x0 -> x1, local copies, waits for them, and re-layouts: none -> 4.31 us  [on_device(): columns_0, columns_1 = (columns[:, 0], columns[:, 1])]
  transfers between devices with their start and end apart: 10 -> 7, of which waited for: 6 -> 3; matrix products, arithmetic and copies ran while one was open for 1% -> 0% of each run, Pallas kernels for 8% -> 5%
where the time goes in v4:
time: 259 us; the launch traced here: 256 us
  blocking collectives  87.5 us (34%)
  Pallas kernels  62 us (24%)
  waiting for transfers between devices  38.3 us (15%)
  local copies, waits for them, and re-layouts  34.1 us (13%)
  starting transfers between devices  19.5 us (8%)
  between operations  14.5 us (6%)
    pallas_call x1, Pallas kernels, on_device(): pl.pallas_call(functools.partial(finish_kernel, scale=1.0 / math.sqrt(MB...  46.4 us
    all_to_all x3, blocking collectives, to_heads(): return lax.all_to_all(block, ('section', 'tp'), 0, 0)  37.3 us
    all_gather x1, waiting for transfers between devices, on_device(): lax.all_gather(head_columns, 'fsdp', axis=0, axis_index_groups=row_groups)  31 us
    unnamed x106, local copies, waits for them, and re-layouts  28.8 us
    all_to_all x1, blocking collectives, on_device(): lax.all_to_all(pieces, ('section', 'fsdp'), 0, 0, axis_index_groups=head_...  24.9 us
    pallas_call x12, Pallas kernels, call(): pl.pallas_call(body, out_shape=[jax.ShapeDtypeStruct(shape, dtype) for sh...  15.6 us
    all_to_all x1, blocking collectives, on_device(): summed = lax.all_to_all(far, 'fsdp', 0, 0, axis_index_groups=y_groups)  13.8 us
    all_to_all x1, blocking collectives, on_device(): far = lax.all_to_all(near, 'fsdp', 0, 0, axis_index_groups=row_groups)  11.3 us
  transfers between devices with their start and end apart: 7, of which 3 were waited for; matrix products, arithmetic and copies ran while one was open for 0% of the time, Pallas kernels for 5%

profile of v4, /device:TPU:1, one launch (start us, length us, event | category | flops | bytes accessed | tf_op | source)
XLA Modules:
  0.0 255.9 jit_solution(91500726228588810)
XLA Ops:
  7.2 0.0 all-gather.2.cloned.1.call-start
  7.3 1.0 reshape.18
  8.3 0.1 broadcast_in_dim.24
  8.4 24.9 %all_to_all.40 = bf16[16,16,1024]{2,1,0:T(8,128)(2,1)} all-to-all(bf16[16,16,1024]{2,1,0:T(8,128)(2,1)S(1)} %bitcast.46), channel_id=1, replica_groups={{0,4,8,12,16,20,24,28,256,260,264,268,272,276,280,284},{32,36,40,44,48,..., dimensions={0} | all-to-all | bytes 1048576 | tf_op jit(solution)/shard_map/all_to_all | solution.py:462
  33.3 0.0 all-gather.2.cloned.1.call-update
  33.4 0.1 pad_add_fusion.refs_0_.core
  33.5 0.6 pack.1
  34.1 2.9 %collective-permute-start = (bf16[432,1024]{1,0:T(8,128)(2,1)S(1)}, bf16[432,1024]{1,0:T(8,128)(2,1)S(1)}, u32[]{:S(2)}, u32[]{:S(2)}) collective-permute-start(bf16[432,1024]{1,0:T(8,128)(2,1)S(1)} %pack.1), channel_id=1, source_target_pairs={{0,256},{256,0},{1,257},{257,1},{2,258},{258,2},{3,259},{259,3},{4... | collective-permute-start | bytes 2654216 | tf_op jit(solution)/shard_map/ppermute | solution.py:425
  37.0 2.0 collective-permute-done.refs_4_
  39.1 1.2 copy-done.19
  40.3 1.2 copy-done.20
  41.5 2.6 %prepare.1 = (bf16[2,2,1024,128]{3,2,1,0:T(8,128)(2,1)S(1)}, bf16[256,1024]{1,0:T(8,128)(2,1)S(1)}, bf16[256,1024]{1,0:T(8,128)(2,1)S(1)}, bf16[2,16,1024]{2,1,0...) custom-call(s32[2]{0:T(128)S(1)} %pad_add_fusion.refs_0_.core, ...), custom_call_target="tpu_custom_call" | custom-call | bytes 7634944 | tf_op jit(solution)/shard_map/prepare/pallas_call | solution.py:116
  44.1 0.0 copy-start.30
  44.2 13.6 %all_to_all.41.refs_1_ = bf16[8,304,128]{2,1,0:T(8,128)(2,1)S(1)} all-to-all(bf16[8,304,128]{2,1,0:T(8,128)(2,1)S(1)} %get-tuple-element.33), channel_id=1, replica_groups=mesh['section'=2,'fsdp'=64,'tp'=4] {'section','tp'}, dimensions={0} | all-to-all | bytes 1245184 | tf_op jit(solution)/shard_map/all_to_all | solution.py:429
  57.8 0.9 entry_norm.1
  58.7 0.8 copy-done.11
  59.5 0.8 copy-done.25
  60.3 0.6 copy-done.42
  61.0 0.6 copy-done.44
  61.5 31.0 %all-gather.2.cloned.1.call-done = bf16[8,2,128,1024]{3,2,0,1:T(8,128)(2,1)} async-done(((bf16[1,2,128,1024]{3,2,0,1:T(8,128)(2,1)}), bf16[8,2,128,1024]{3,2,0,1:T(8,128)(2,1)}) %all-gather.2.cloned.1.call-update) | async-done | bytes 4194320 | tf_op jit(solution)/shard_map/all_gather | solution.py:466
  92.5 4.3 %slice_bitcast_fusion = (bf16[8,128,1024]{2,1,0:T(8,128)(2,1)}, bf16[8,128,1024]{2,1,0:T(8,128)(2,1)S(1)}) fusion(bf16[8,2,128,1024]{3,2,0,1:T(8,128)(2,1)} %all-gather.2.cloned.1.call-done), kind=kLoop, calls=%fused_computation | loop fusion | bytes 8388608 | tf_op jit(solution)/shard_map/squeeze | solution.py:492
  96.9 1.0 values_0.1
  97.9 0.8 copy-done.14
  98.7 5.0 %all-to-all-start.2 = ((bf16[8,256,128]{2,1,0:T(8,128)(2,1)}), bf16[8,256,128]{2,1,0:T(8,128)(2,1)}, u32[]{:S(2)}, u32[]{:S(2)}) async-start(bf16[8,256,128]{2,1,0:T(8,128)(2,1)} %copy-done.14), calls=%async_computation.2 | async-start | bytes 1048576 | tf_op jit(solution)/shard_map/all_to_all | solution.py:429
  103.7 1.6 copy-done
  105.3 1.0 copy-done.26
  106.3 0.8 scaled_1.1.refs_3_.refs_2_
  107.2 0.8 copy-done.7
  108.0 5.2 %all-to-all-done.2.refs_0_ = bf16[8,256,128]{2,1,0:T(8,128)(2,1)} async-done(((bf16[8,256,128]{2,1,0:T(8,128)(2,1)}), bf16[8,256,128]{2,1,0:T(8,128)(2,1)}, u32[]{:S(2)}, u32[]{:S(2)}) %all-to-all-start.2) | async-done | bytes 524320 | tf_op jit(solution)/shard_map/all_to_all | solution.py:429
  113.2 1.6 copy-done.1
  114.8 1.0 copy-done.5
  115.8 1.0 copy-done.8
  116.9 2.5 first_output.1
  119.4 0.8 copy-done.15
  120.2 0.8 copy-done.28
  121.0 0.6 copy-done.36
  121.6 8.6 %all_to_all.42.refs_0_ = f32[8,8,256]{2,1,0:T(8,128)S(1)} all-to-all(f32[8,8,256]{2,1,0:T(8,128)} %copy-done.36), channel_id=1, replica_groups=mesh['section'=2,'fsdp'=64,'tp'=4] {'section','tp'}, dimensions={0} | all-to-all | bytes 131072 | tf_op jit(solution)/shard_map/all_to_all | solution.py:429
  130.2 1.0 copy-done.9
  131.3 1.0 copy-done.16
  132.3 1.0 copy-done.31
  133.4 0.9 first_gradient.1
  134.3 15.1 %all_to_all.43.refs_1_.refs_3_ = bf16[8,304,128]{2,1,0:T(8,128)(2,1)S(1)} all-to-all(bf16[8,304,128]{2,1,0:T(8,128)(2,1)S(1)} %get-tuple-element.46), channel_id=1, replica_groups=mesh['section'=2,'fsdp'=64,'tp'=4] {'section','tp'}, dimensions={0} | all-to-all | bytes 1245184 | tf_op jit(solution)/shard_map/all_to_all | solution.py:429
  149.5 1.1 map_gradient.1
  150.6 0.8 copy-done.2
  151.4 0.7 copy-done.21
  152.1 7.2 %all-to-all-start.5 = ((f32[16,24,128]{2,1,0:T(8,128)}), f32[16,24,128]{2,1,0:T(8,128)S(1)}, u32[]{:S(2)}, u32[]{:S(2)}) async-start(f32[16,24,128]{2,1,0:T(8,128)} %copy-done.21), calls=%async_computation.5 | async-start | bytes 393216 | tf_op jit(solution)/shard_map/all_to_all | solution.py:571
  159.4 1.1 copy-done.3
  160.4 1.0 copy-done.6
  161.5 1.0 copy-done.24
  162.5 0.7 copy-done.45
  163.2 0.7 copy-done.49
  163.9 3.1 %slot_gradient.1 = (bf16[96,1024]{1,0:T(8,128)(2,1)S(1)}, bf16[96,1024]{1,0:T(8,128)(2,1)}) custom-call(s32[2]{0:T(128)S(1)} %copy-done.41, s32[2]{0:T(128)S(1)} %bitcast.41, s32[2]{0:T(128)S(1)} %bitcast.43, bf16[8,304,128]{2,1,0:T(8,128)(2,1)S(1)} %copy-done.3, bf16[2,16,1024]{2,1,0:T(8,128)(2,1)S(1)} %get-tuple-element.35.refs_3_.refs_2_.refs_6_.refs_4_, ...), custom_call_target="tpu_custom_call" | custom-call | bytes 4366336 | tf_op jit(solution)/shard_map/slot_gradient/pallas_call | solution.py:116
  166.9 0.7 copy-done.33
  167.6 2.0 collective-permute-start.1
  169.6 0.0 reduce-scatter.2.cloned.1.call-done
  169.7 1.0 copy-done.17
  170.7 0.8 copy-done.35
  171.6 2.0 second_output.1
  173.5 0.8 copy-done.29
  174.3 2.3 collective-permute-start.2
  176.7 11.3 %all_to_all.44.refs_0_ = bf16[8,2,24,128]{3,2,1,0:T(8,128)(2,1)S(1)} all-to-all(bf16[8,2,24,128]{3,2,1,0:T(8,128)(2,1)S(1)} %near_sum.1), channel_id=1, replica_groups={{0,32,64,96,128,160,192,224},{4,36,68,100,132,164,196,228},{8,40,72,104..., dimensions={0} | all-to-all | bytes 196608 | tf_op jit(solution)/shard_map/all_to_all | solution.py:575
  188.1 13.8 %all_to_all.45.received = bf16[8,2,24,128]{3,2,1,0:T(8,128)(2,1)} all-to-all(bf16[8,2,24,128]{3,2,1,0:T(8,128)(2,1)S(1)} %far_sum.1), channel_id=1, replica_groups={{0,4,8,12,16,20,24,28},{32,36,40,44,48,52,56,60},{64,68,72,76,80,84,88,..., dimensions={0} | all-to-all | bytes 196608 | tf_op jit(solution)/shard_map/all_to_all | solution.py:578
  201.9 0.8 copy-done.51
  202.7 46.4 %finish.1 = (bf16[256,2048]{1,0:T(8,128)(2,1)}, bf16[96,2048]{1,0:T(8,128)(2,1)}, f32[16,2048]{1,0:T(8,128)}, f32[16,256]{1,0:T(8,128)}) custom-call(s32[2]{0:T(128)} %copy-done.39, bf16[8,2,24,128]{3,2,1,0:T(8,128)(2,1)} %all_to_all.45.received, bf16[256,1024]{1,0:T(8,128)(2,1)} %copy-done.29, bf16[256,1024]{1,0:T(8,128)(2,1)} %copy-done.51, ...), custom_call_target="tpu_custom_call" | custom-call | tf_op jit(solution)/shard_map/finish/pallas_call | solution.py:582
  (84 shorter events, 0.3 us)
Async XLA Ops:
  7.2 26.2 %copy-start.52 = (bf16[1,2048]{1,0:T(2,128)(2,1)S(1)}, bf16[1,2048]{1,0:T(2,128)(2,1)}, u32[]{:S(2)}) copy-start(bf16[1,2048]{1,0:T(2,128)(2,1)} %param.19) | copy-start | bytes 12292
  7.2 26.3 %copy-start.34 = (bf16[1,16,1024]{2,1,0:T(8,128)(2,1)S(1)}, bf16[1,16,1024]{2,1,0:T(8,128)(2,1)}, u32[]{:S(2)}) copy-start(bf16[1,16,1024]{2,1,0:T(8,128)(2,1)} %param.22) | copy-start | bytes 98308
  7.2 26.3 %copy-start.32 = (bf16[1,2048,16]{1,2,0:T(8,128)(2,1)S(1)}, bf16[1,2048,16]{1,2,0:T(8,128)(2,1)}, u32[]{:S(2)}) copy-start(bf16[1,2048,16]{1,2,0:T(8,128)(2,1)} %param.21) | copy-start | bytes 196612
  7.2 26.3 %copy-start.27 = (bf16[1,2,128,256]{3,2,1,0:T(8,128)(2,1)S(1)}, bf16[1,2,128,256]{3,2,1,0:T(8,128)(2,1)}, u32[]{:S(2)}) copy-start(bf16[1,2,128,256]{3,2,1,0:T(8,128)(2,1)} %param.18) | copy-start | bytes 393220
  7.2 26.3 %copy-start.10 = (bf16[1,2,128,2048]{3,2,1,0:T(8,128)(2,1)S(1)}, bf16[1,2,128,2048]{3,2,1,0:T(8,128)(2,1)}, u32[]{:S(2)}) copy-start(bf16[1,2,128,2048]{3,2,1,0:T(8,128)(2,1)} %param.17) | copy-start | bytes 3145732
  7.2 26.3 %copy-start.18 = (bf16[1,1,96,2048]{3,2,1,0:T(8,128)(2,1)S(1)}, bf16[1,1,96,2048]{3,2,1,0:T(8,128)(2,1)}, u32[]{:S(2)}) copy-start(bf16[1,1,96,2048]{3,2,1,0:T(8,128)(2,1)} %param.13) | copy-start | bytes 1179652
  7.2 85.3 %all-gather.2.cloned.1.call-start = ((), (), s32[]{:S(2)}) async-start(), calls=%async_computation.9 | async-start | bytes 4718592 | tf_op jit(solution)/shard_map/all_gather | solution.py:466
  8.3 30.7 %copy-start.46 = (s32[2,1]{0,1:T(1,128)S(1)}, s32[2,1]{0,1:T(1,128)}, u32[]{:S(2)}) copy-start(s32[2,1]{0,1:T(1,128)} %param.14) | copy-start | bytes 28
  8.4 30.7 %copy-start.48 = (s32[2,1]{0,1:T(1,128)S(1)}, s32[2,1]{0,1:T(1,128)}, u32[]{:S(2)}) copy-start(s32[2,1]{0,1:T(1,128)} %param.15) | copy-start | bytes 28
  8.4 30.7 %copy-start.50 = (s32[2,1]{0,1:T(1,128)S(1)}, s32[2,1]{0,1:T(1,128)}, u32[]{:S(2)}) copy-start(s32[2,1]{0,1:T(1,128)} %param.16) | copy-start | bytes 28
  33.5 24.3 %copy-start.39 = (s32[2]{0:T(128)}, s32[2]{0:T(128)S(1)}, u32[]{:S(2)}) copy-start(s32[2]{0:T(128)S(1)} %pad_add_fusion.refs_0_.core) | copy-start | bytes 28
  34.1 4.9 %collective-permute-start = (bf16[432,1024]{1,0:T(8,128)(2,1)S(1)}, bf16[432,1024]{1,0:T(8,128)(2,1)S(1)}, u32[]{:S(2)}, u32[]{:S(2)}) collective-permute-start(bf16[432,1024]{1,0:T(8,128)(2,1)S(1)} %pack.1), channel_id=1, source_target_pairs={{0,256},{256,0},{1,257},{257,1},{2,258},{258,2},{3,259},{259,3},{4... | collective-permute-start | bytes 2654216 | tf_op jit(solution)/shard_map/ppermute | solution.py:425
  39.1 1.2 copy-start.19
  40.3 1.2 copy-start.20
  44.1 13.7 %copy-start.30 = (bf16[256,1024]{1,0:T(8,128)(2,1)}, bf16[256,1024]{1,0:T(8,128)(2,1)S(1)}, u32[]{:S(2)}) copy-start(bf16[256,1024]{1,0:T(8,128)(2,1)S(1)} %get-tuple-element.44.refs_3_) | copy-start | bytes 1572868
  44.1 13.6 %copy-start.4 = (bf16[256,1024]{1,0:T(8,128)(2,1)}, bf16[256,1024]{1,0:T(8,128)(2,1)S(1)}, u32[]{:S(2)}) copy-start(bf16[256,1024]{1,0:T(8,128)(2,1)S(1)} %get-tuple-element.34.refs_2_.refs_10_) | copy-start | bytes 1572868
  58.7 0.8 copy-start.11
  59.5 0.8 copy-start.25
  60.3 0.6 copy-start.42
  60.9 0.6 copy-start.44
  92.5 4.3 %copy-start.12 = (bf16[256,1024]{1,0:T(8,128)(2,1)S(1)}, bf16[256,1024]{1,0:T(8,128)(2,1)}, u32[]{:S(2)}) copy-start(bf16[256,1024]{1,0:T(8,128)(2,1)} %copy-done.11) | copy-start | bytes 1572868
  97.9 0.8 copy-start.14
  98.7 14.5 %all-to-all-start.2 = ((bf16[8,256,128]{2,1,0:T(8,128)(2,1)}), bf16[8,256,128]{2,1,0:T(8,128)(2,1)}, u32[]{:S(2)}, u32[]{:S(2)}) async-start(bf16[8,256,128]{2,1,0:T(8,128)(2,1)} %copy-done.14), calls=%async_computation.2 | async-start | bytes 1048576 | tf_op jit(solution)/shard_map/all_to_all | solution.py:429
  103.7 66.0 %reduce-scatter.2.cloned.1.call-start = ((), (), s32[]{:S(2)}) async-start(), calls=%async_computation.10 | async-start | bytes 589824 | tf_op jit(solution)/shard_map/reduce_scatter | solution.py:518
  103.7 1.6 copy-start
  105.3 1.0 copy-start.26
  107.2 0.8 copy-start.7
  113.2 1.6 copy-start.1
  114.8 1.0 copy-start.5
  115.8 1.0 copy-start.8
  119.4 0.8 copy-start.15
  120.2 0.8 copy-start.28
  121.0 0.6 copy-start.36
  130.2 1.0 copy-start.9
  131.3 1.0 copy-start.16
  132.3 1.0 copy-start.31
  133.3 16.1 %copy-start.13 = (bf16[256,1024]{1,0:T(8,128)(2,1)S(1)}, bf16[256,1024]{1,0:T(8,128)(2,1)}, u32[]{:S(2)}) copy-start(bf16[256,1024]{1,0:T(8,128)(2,1)} %copy-done.11) | copy-start | bytes 1572868
  133.3 16.1 %copy-start.40 = (s32[2]{0:T(128)S(1)}, s32[2]{0:T(128)}, u32[]{:S(2)}) copy-start(s32[2]{0:T(128)} %copy-done.39) | copy-start | bytes 28
  133.4 16.1 %copy-start.43 = (f32[16,256]{1,0:T(8,128)S(1)}, f32[16,256]{1,0:T(8,128)}, u32[]{:S(2)}) copy-start(f32[16,256]{1,0:T(8,128)} %copy-done.42) | copy-start | bytes 49156
  134.3 15.2 %copy-start.23 = (bf16[256,1024]{1,0:T(8,128)(2,1)}, bf16[256,1024]{1,0:T(8,128)(2,1)S(1)}, u32[]{:S(2)}) copy-start(bf16[256,1024]{1,0:T(8,128)(2,1)S(1)} %get-tuple-element.52.refs_9_) | copy-start | bytes 1572868
  134.3 15.2 %copy-start.37 = (f32[8,256]{1,0:T(8,128)}, f32[8,256]{1,0:T(8,128)S(1)}, u32[]{:S(2)}) copy-start(f32[8,256]{1,0:T(8,128)S(1)} %get-tuple-element.48.refs_4_.refs_2_) | copy-start | bytes 24580
  134.3 25.0 %copy-start.41 = (s32[2]{0:T(128)S(1)}, s32[2]{0:T(128)}, u32[]{:S(2)}) copy-start(s32[2]{0:T(128)} %copy-done.39) | copy-start | bytes 28
  134.3 25.0 %copy-start.47 = (s32[2,1]{0,1:T(1,128)S(1)}, s32[2,1]{0,1:T(1,128)}, u32[]{:S(2)}) copy-start(s32[2,1]{0,1:T(1,128)} %param.14) | copy-start | bytes 28
  150.6 0.8 copy-start.2
  151.4 0.7 copy-start.21
  152.1 17.6 %copy-start.38 = (f32[8,256]{1,0:T(8,128)S(1)}, f32[8,256]{1,0:T(8,128)}, u32[]{:S(2)}) copy-start(f32[8,256]{1,0:T(8,128)} %copy-done.37) | copy-start | bytes 24580
  152.1 24.6 %all-to-all-start.5 = ((f32[16,24,128]{2,1,0:T(8,128)}), f32[16,24,128]{2,1,0:T(8,128)S(1)}, u32[]{:S(2)}, u32[]{:S(2)}) async-start(f32[16,24,128]{2,1,0:T(8,128)} %copy-done.21), calls=%async_computation.5 | async-start | bytes 393216 | tf_op jit(solution)/shard_map/all_to_all | solution.py:571
  159.4 1.1 copy-start.3
  160.4 1.0 copy-start.6
  161.5 1.0 copy-start.24
  162.5 0.7 copy-start.45
  163.2 0.7 copy-start.49
  166.9 0.7 copy-start.33
  167.6 9.0 %collective-permute-start.1 = (bf16[96,1024]{1,0:T(8,128)(2,1)}, bf16[96,1024]{1,0:T(8,128)(2,1)S(1)}, u32[]{:S(2)}, u32[]{:S(2)}) collective-permute-start(bf16[96,1024]{1,0:T(8,128)(2,1)} %get-tuple-element.53), channel_id=1, source_target_pairs={{0,256},{256,0},{1,257},{257,1},{2,258},{258,2},{3,259},{259,3},{4... | collective-permute-start | bytes 589832 | tf_op jit(solution)/shard_map/ppermute | solution.py:425
  169.7 1.0 copy-start.17
  170.7 0.8 copy-start.35
  173.5 0.8 copy-start.29
  174.3 27.6 %collective-permute-start.2 = (bf16[256,1024]{1,0:T(8,128)(2,1)}, bf16[256,1024]{1,0:T(8,128)(2,1)S(1)}, u32[]{:S(2)}, u32[]{:S(2)}) collective-permute-start(bf16[256,1024]{1,0:T(8,128)(2,1)} %get-tuple-element.56), channel_id=1, source_target_pairs={{0,256},{256,0},{1,257},{257,1},{2,258},{258,2},{3,259},{259,3},{4... | collective-permute-start | bytes 1572872 | tf_op jit(solution)/shard_map/ppermute | solution.py:425
  176.7 25.3 %copy-start.22 = (bf16[96,1024]{1,0:T(8,128)(2,1)}, bf16[96,1024]{1,0:T(8,128)(2,1)S(1)}, u32[]{:S(2)}) copy-start(bf16[96,1024]{1,0:T(8,128)(2,1)S(1)} %collective-permute-done.1.refs_1_.other_slots) | copy-start | bytes 589828
  201.9 0.8 copy-start.51
Sparse Core Ops, SparseCore 0:
  33.5 59.0 all-gather.1
  121.8 36.0 reduce-scatter.1

commit v5 on v1

--- a/solution.py
+++ b/solution.py
@@ -29,7 +29,8 @@
 F32 = jnp.float32
 
 R_VIS, R_Q, R_K, R_DN, R_UP, R_GN, R_END = 0, 96, 352, 384, 400, 416, 432
-SMALL = 2 * RANK
+R_SUM, R_LOW, R_PAY = ROWS, ROWS + RANK, ROWS + RANK + 2 * RANK
+SUBLANES = 8
 
 
 def block_of(head):
@@ -61,24 +62,40 @@
     square = jnp.zeros((ROWS, HD), F32)
     for at, column in enumerate(columns):
         square = jnp.where(lane == at, column, square)
-    return square.T[:RANK, :]
+    return square.T[:SUBLANES, :]
 
 
 def rows_to_columns(rows):
-    padded = jnp.concatenate([rows, jnp.zeros((HD - RANK, ROWS), F32)], axis=0)
+    padded = jnp.concatenate([rows, jnp.zeros((HD - SUBLANES, ROWS), F32)], axis=0)
     return padded.T
 
 
-def split_parts(rows):
-    high = rows.astype(BF)
-    low = (rows - high.astype(F32)).astype(BF)
-    parts = [part[:, at : at + HD] for part in (high, low) for at in (0, HD)]
-    return jnp.concatenate(parts, axis=0)
-
-
-def join_parts(block, count):
-    parts = [block[at * count : (at + 1) * count, :].astype(F32) for at in range(4)]
-    return jnp.concatenate([parts[0] + parts[2], parts[1] + parts[3]], axis=1)
+def payload_block(values, column, low_rank):
+    row = columns_to_rows(column)[0:1, :]
+    high = row.astype(BF).astype(F32)
+    low = row - high
+    at = lax.broadcasted_iota(jnp.int32, (RANK, HD), 0)
+    sums = jnp.zeros((RANK, HD), F32)
+    for index, part in enumerate((high[:, :HD], high[:, HD:], low[:, :HD], low[:, HD:])):
+        sums = jnp.where(at == index, part, sums)
+    low_rank = low_rank.astype(BF)
+    return jnp.concatenate(
+        [values, sums.astype(BF), low_rank[:, :HD], low_rank[:, HD:]], axis=0
+    )
+
+
+def total_of_payloads(blocks):
+    sums = blocks[0, R_SUM:R_LOW, :].astype(F32)
+    low_rank = blocks[0, R_LOW:, :].astype(F32)
+    for peer in range(1, PEERS):
+        sums = sums + blocks[peer, R_SUM:R_LOW, :].astype(F32)
+        low_rank = low_rank + blocks[peer, R_LOW:, :].astype(F32)
+    left = sums[0:1, :] + sums[2:3, :]
+    right = sums[1:2, :] + sums[3:4, :]
+    row = jnp.concatenate([left, right], axis=1)
+    at = lax.broadcasted_iota(jnp.int32, (SUBLANES, ROWS), 0)
+    rows = jnp.where(at == 0, row, 0.0)
+    return rows, jnp.concatenate([low_rank[:RANK, :], low_rank[RANK:, :]], axis=1)
 
 
 def inverse_of(squares):
@@ -157,25 +174,24 @@
     entry_float = entry[...].astype(F32)
     squares = jnp.sum(entry_float * entry_float, axis=-1, keepdims=True)
     gained = (entry_float * gains[0][0:1, :].astype(F32)).astype(BF)
-    small = jnp.concatenate([nt(downs[0], gained), columns_to_rows(squares)], axis=0)
-    block = jnp.concatenate([value_gradient, split_parts(small)], axis=0)
+    block = payload_block(value_gradient, squares, nt(downs[0], gained))
     for peer in range(PEERS):
         payload[peer] = block
 
 
 def entry_norm_kernel(
-    received, entry, downs, ups, gains, normed, inverse, adapter_rows, full_gradient, lora_gradient
+    core, received, entry, ups, gains,
+    normed, inverse, adapter_rows, full_gradient, own_gradient, lora_gradient,
 ):
-    total = jnp.zeros((SMALL, ROWS), F32)
-    for peer in range(PEERS):
-        total = total + join_parts(received[peer, ROWS:, :], SMALL)
-    column = inverse_of(rows_to_columns(total[RANK:, :])[:, 0:1])
+    rows, low_rank = total_of_payloads(received)
+    column = inverse_of(rows_to_columns(rows)[:, 0:1])
     inverse[...] = jnp.broadcast_to(column, (ROWS, HD))
-    adapter_rows[...] = total[:RANK, :] * inverse_of(total[RANK : RANK + 1, :])
+    adapter_rows[...] = low_rank * inverse_of(rows[0:1, :])
     gain = gains[0][0:1, :].astype(F32)
     normed[...] = (entry[...].astype(F32) * column * gain).astype(BF)
     for head in range(KVH):
         full_gradient[:, head * HD : (head + 1) * HD] = received[block_of(head), :ROWS, :]
+    own_gradient[...] = received[core[0] * 4 + core[1], :ROWS, :]
     lora_gradient[...] = ADAPTER_SCALE * nt(ups[1], full_gradient[...])
 
 
@@ -207,7 +223,7 @@
 
 
 def first_output_kernel(
-    received, weights, entry, scaled, downs, gains, hidden, value_rows, payload
+    received, weights, entry, scaled, hidden, value_rows, payload
 ):
     values = received[0].astype(F32)
     for peer in range(1, PEERS):
@@ -219,26 +235,27 @@
     output_float = output.astype(F32)
     squares = jnp.sum(output_float * output_float, axis=-1, keepdims=True)
     dots = jnp.sum(output_float * scaled[...], axis=-1, keepdims=True)
-    gained = (output_float * gains[1][0:1, :].astype(F32)).astype(BF)
-    small = jnp.concatenate([nt(downs[1], gained), columns_to_rows(squares, dots)], axis=0)
+    block = columns_to_rows(squares, dots)
     for peer in range(PEERS):
-        payload[peer] = small
+        payload[peer] = block
 
 
 def first_gradient_kernel(
-    received, weights, hidden, scaled, cotangent_half, gains, value_rows,
-    gradient, normed, adapter_rows, payload,
+    received, weights, hidden, scaled, cotangent_half, gains, downs, value_rows, lora_gradient,
+    gradient, normed, inverse_row, down_gradient, payload,
 ):
     total = received[0]
     for peer in range(1, PEERS):
         total = total + received[peer]
-    sums = rows_to_columns(total[RANK:, :])
+    sums = rows_to_columns(total)
     column = inverse_of(sums[:, 0:1])
     factor = column * column * column * sums[:, 1:2] / MODEL_WIDTH
-    adapter_rows[...] = total[:RANK, :] * inverse_of(total[RANK : RANK + 1, :])
+    inverse_row[...] = inverse_of(total)
     hidden_float = hidden[...].astype(F32)
-    gain = gains[1][0:1, :].astype(F32)
-    normed[...] = (hidden_float * column * gain).astype(BF)
+    gained = hidden_float * gains[1][0:1, :].astype(F32)
+    rows = (gained * column).astype(BF)
+    normed[...] = rows
+    down_gradient[...] = nn(lora_gradient[...].astype(BF), rows)
     grad = (
         cotangent_half[...].astype(F32) + column * scaled[...] - hidden_float * factor
     ).astype(BF)
@@ -248,7 +265,7 @@
         axis=0,
     ).astype(BF)
     dots = jnp.sum(value_gradient.astype(F32) * value_rows[...], axis=-1, keepdims=True)
-    block = jnp.concatenate([value_gradient, split_parts(columns_to_rows(dots))], axis=0)
+    block = payload_block(value_gradient, dots, nt(downs[1], gained.astype(BF)))
     for peer in range(PEERS):
         payload[peer] = block
 
@@ -262,68 +279,110 @@
     return jnp.concatenate([left, right], axis=1)
 
 
+def gathered_gradient(received):
+    return jnp.concatenate([received[block_of(head), :ROWS, :] for head in range(KVH)], axis=1)
+
+
 def map_gradient_kernel(
-    core, received, ups, normed_0, adapter_0, normed_1, adapter_1, full_gradient, lora_gradient_1,
-    last_gradient, lora_gradient_0, out,
+    core, received, ups, normed_0, adapter_0, inverse_row, gradient_1, down_gradient_1, out
 ):
-    own = core[0] * 4 + core[1]
-    for head in range(KVH):
-        last_gradient[:, head * HD : (head + 1) * HD] = received[block_of(head), :ROWS, :]
-    lora_0 = ADAPTER_SCALE * nt(ups[0], last_gradient[...])
-    lora_gradient_0[...] = lora_0
+    _, low_rank = total_of_payloads(received)
+    lora_0 = ADAPTER_SCALE * nt(ups[0], gathered_gradient(received))
+    own = received[core[0] * 4 + core[1], :ROWS, :]
     down_0 = nn(lora_0.astype(BF), normed_0[...])
-    up_0 = ADAPTER_SCALE * nn(adapter_0[...].astype(BF), received[own, :ROWS, :])
-    out[0] = map_chunks(down_0, up_0)
-    own_columns = pl.ds(pl.multiple_of((2 * core[1] + core[0]) * HD, HD), HD)
-    down_1 = nn(lora_gradient_1[...].astype(BF), normed_1[...])
-    up_1 = ADAPTER_SCALE * nn(adapter_1[...].astype(BF), full_gradient[:, own_columns])
-    out[1] = map_chunks(down_1, up_1)
+    up_0 = ADAPTER_SCALE * nn(adapter_0[...].astype(BF), own)
+    adapter_1 = (low_rank * inverse_row[0:1, :]).astype(BF)
+    up_1 = ADAPTER_SCALE * nn(adapter_1, gradient_1[...])
+    chunks = (map_chunks(down_0, up_0), map_chunks(down_gradient_1[...], up_1))
+    for layer in range(2):
+        out[layer * 4 * RANK : (layer + 1) * 4 * RANK] = chunks[layer][:, None, :]
 
 
 def slot_gradient_kernel(
-    core, counts, starts,
-    received, last_gradient, lora_gradient, columns, downs, gains, entry, inverse, gradient,
-    slots,
+    core, counts, starts, received, ups, columns, downs, gains, entry, inverse, gradient,
+    own_slots, other_slots,
 ):
-    total = jnp.zeros((RANK, ROWS), F32)
-    for peer in range(PEERS):
-        total = total + join_parts(received[peer, ROWS:, :], RANK)
+    dots, _ = total_of_payloads(received)
+    full_gradient = gathered_gradient(received)
+    lora_gradient = ADAPTER_SCALE * nt(ups[0], full_gradient)
     column = inverse[:, 0:1]
-    factor = column * column * rows_to_columns(total)[:, 0:1] / MODEL_WIDTH
+    factor = column * column * rows_to_columns(dots)[:, 0:1] / MODEL_WIDTH
     weight = columns[:, 0].reshape(KVH * HD, HALF)
-    grad = nn(last_gradient[...], weight) + tn(lora_gradient[...].astype(BF), downs[0])
+    grad = nn(full_gradient, weight) + tn(lora_gradient.astype(BF), downs[0])
     scaled = grad * gains[0][0:1, :].astype(F32)
     rows = (
         gradient[...].astype(F32) + column * scaled - entry[...].astype(F32) * factor
     ).astype(BF)
     slot = lax.broadcasted_iota(jnp.int32, (VIS, SEQ), 0)
     position = lax.broadcasted_iota(jnp.int32, (VIS, SEQ), 1)
-    for m in range(MB):
-        picking = ((position == starts[m] + slot) & (slot < counts[m] * TOKT)).astype(F32).astype(BF)
-        slots[m] = nn(picking, rows[m * SEQ : (m + 1) * SEQ, :]).astype(BF)
-
-
-def second_output_kernel(values, weights, hidden, out):
+    first = core[0] == 0
+    above, below = rows[:SEQ, :], rows[SEQ:, :]
+    for index, block, out in (
+        (core[0], jnp.where(first, above, below), own_slots),
+        (1 - core[0], jnp.where(first, below, above), other_slots),
+    ):
+        inside = (position == starts[index] + slot) & (slot < counts[index] * TOKT)
+        out[...] = nn(inside.astype(F32).astype(BF), block).astype(BF)
+
+
+def second_output_kernel(core, values, weights, hidden, own_hidden, other_hidden):
     attended = attended_rows(weights, 1, values[...])
-    out[...] = (hidden[...].astype(F32) + attended).astype(BF)
-
-
-def call(kernel, name, shapes, scalars, arrays, flops=0):
-    in_specs = [pl.BlockSpec(memory_space=pltpu.SMEM)] * len(scalars)
-    in_specs += [pl.BlockSpec(memory_space=pltpu.VMEM)] * len(arrays)
-    outs = [jax.ShapeDtypeStruct(shape, dtype) for shape, dtype in shapes]
+    output = (hidden[...].astype(F32) + attended).astype(BF)
+    first = core[0] == 0
+    own_hidden[...] = jnp.where(first, hidden[...], output)
+    other_hidden[...] = jnp.where(first, output, hidden[...])
+
+
+def sum_kernel(arrived, out, token):
+    token[...] = jnp.zeros_like(token)
+    n_fsdp = arrived.shape[0] // 2
+    halves = [jnp.sum(arrived[h * n_fsdp : (h + 1) * n_fsdp], axis=0) for h in range(2)]
+    row = jnp.concatenate(halves, axis=1)
+    for at in range(n_fsdp):
+        out[at] = row
+
+
+def maps_kernel(arrived, down_sum, up_sum, *, scale):
+    rows = arrived[...].reshape(4 * RANK, 2 * (HALF // 4 + HD)) * scale
+    quarter, width = HALF // 4, HALF // 4 + HD
+    for half in range(2):
+        for q in range(4):
+            to = half * HALF + q * quarter
+            down_sum[:, to : to + quarter] = rows[
+                q * RANK : (q + 1) * RANK, half * width : half * width + quarter
+            ]
+        up_sum[:, half * HD : (half + 1) * HD] = rows[
+            :RANK, half * width + quarter : (half + 1) * width
+        ]
+
+
+def place_kernel(core, own, other, out, token):
+    token[...] = jnp.zeros_like(token)
+    at = pl.multiple_of(core[0] * HALF, HALF)
+    out[:, pl.ds(at, HALF)] = own[...]
+    out[:, pl.ds(HALF - at, HALF)] = other[...]
+
+
+def call(kernel, name, results, scalars, arrays, after=()):
+    n_read = len(scalars) + len(arrays)
+
+    def body(*refs):
+        kernel(*refs[:n_read], *refs[n_read + len(after) :])
+
     moved = sum(a.size * a.dtype.itemsize for a in arrays)
-    moved += sum(math.prod(shape) * jnp.dtype(dtype).itemsize for shape, dtype in shapes)
-    result = pl.pallas_call(
-        kernel,
-        out_shape=outs,
-        in_specs=in_specs,
-        out_specs=[pl.BlockSpec(memory_space=pltpu.VMEM)] * len(outs),
+    moved += sum(math.prod(shape) * jnp.dtype(dtype).itemsize for shape, dtype in results)
+    in_vmem = pl.BlockSpec(memory_space=pltpu.VMEM)
+    return pl.pallas_call(
+        body,
+        out_shape=[jax.ShapeDtypeStruct(shape, dtype) for shape, dtype in results],
+        in_specs=[pl.BlockSpec(memory_space=pltpu.SMEM)] * len(scalars)
+        + [in_vmem] * len(arrays)
+        + [pl.BlockSpec(memory_space=pl.ANY)] * len(after),
+        out_specs=[in_vmem] * len(results),
         compiler_params=pltpu.CompilerParams(vmem_limit_bytes=VMEM_BYTES),
-        cost_estimate=pl.CostEstimate(flops=flops, bytes_accessed=moved, transcendentals=0),
+        cost_estimate=pl.CostEstimate(flops=0, bytes_accessed=moved, transcendentals=0),
         name=name,
-    )(*scalars, *arrays)
-    return result
+    )(*scalars, *arrays, *after)
 
 
 def swap_cores(block):
@@ -393,17 +452,17 @@
             maps,
             maps,
             maps,
-            ((PEERS, ROWS + 4 * SMALL, HD), BF),
+            ((PEERS, R_PAY, HD), BF),
         ],
         (core, counts, begins, seq_lengths),
         (received, *own, embeddings, cotangent),
     )
-    normed_0, inverse_0, adapter_0, full_gradient, lora_gradient_1 = call(
+    normed_0, inverse_0, adapter_0, full_gradient, own_gradient_1, lora_gradient_1 = call(
         entry_norm_kernel,
         "entry_norm",
-        [wide, ((ROWS, HD), F32), small, wide, small],
-        (),
-        (to_heads(payload), entry, downs, ups, gains),
+        [wide, ((ROWS, HD), F32), small, wide, ((ROWS, HD), BF), small],
+        (core,),
+        (to_heads(payload), entry, ups, gains),
     )
 
     blocks = ((PEERS, ROWS, HD), BF)
@@ -420,16 +479,32 @@
     hidden_0, value_rows, payload = call(
         first_output_kernel,
         "first_output",
-        [wide, ((ROWS, HD), F32), ((PEERS, SMALL, ROWS), F32)],
+        [wide, ((ROWS, HD), F32), ((PEERS, SUBLANES, ROWS), F32)],
         (),
-        (to_heads(partial_0), weights, entry, scaled_1, downs, gains),
-    )
-    gradient, normed_1, adapter_1, payload = call(
+        (to_heads(partial_0), weights, entry, scaled_1),
+    )
+    gradient, normed_1, inverse_row, down_gradient_1, payload = call(
         first_gradient_kernel,
         "first_gradient",
-        [wide, wide, small, ((PEERS, ROWS + 4 * RANK, HD), BF)],
+        [
+            wide,
+            wide,
+            ((SUBLANES, ROWS), F32),
+            ((RANK, HALF), F32),
+            ((PEERS, R_PAY, HD), BF),
+        ],
         (),
-        (to_heads(payload), weights, hidden_0, scaled_1, cotangent_half, gains, value_rows),
+        (
+            to_heads(payload),
+            weights,
+            hidden_0,
+            scaled_1,
+            cotangent_half,
+            gains,
+            downs,
+            value_rows,
+            lora_gradient_1,
+        ),
     )
     gathered = to_heads(payload)
     (partial_1,) = call(
@@ -437,65 +512,62 @@
     )
     values_1 = lax.psum_scatter(partial_1, ("section", "tp"), scatter_dimension=0)
 
-    last_gradient, lora_gradient_0, chunks = call(
+    (chunks,) = call(
         map_gradient_kernel,
         "map_gradient",
-        [wide, small, ((2, 4 * RANK, HALF // 4 + HD), F32)],
+        [((2 * n_fsdp, 1, HALF // 4 + HD), F32)],
         (core,),
-        (gathered, ups, normed_0, adapter_0, normed_1, adapter_1, full_gradient, lora_gradient_1),
+        (gathered, ups, normed_0, adapter_0, inverse_row, own_gradient_1, down_gradient_1),
     )
     width = HALF // 4 + HD
-    arrived = lax.all_to_all(
-        chunks.reshape(2 * n_fsdp, 1, width), ("section", "fsdp"), 0, 0
-    ).reshape(2, n_fsdp, width)
-    summed = jnp.sum(arrived, axis=1)
-    everywhere = lax.all_to_all(
-        jnp.broadcast_to(summed.reshape(1, 1, 2 * width), (n_fsdp, 1, 2 * width)), "fsdp", 0, 0
-    ).reshape(4, RANK, 2, width)
-    everywhere = everywhere * (1.0 / math.sqrt(MB * SEQ * n_fsdp))
-    down_sum = (
-        everywhere[..., : HALF // 4].transpose(1, 2, 0, 3).reshape(RANK, 2 * HALF).T
-    )
-    up_sum = everywhere[0, :, :, HALF // 4 :].reshape(RANK, 2 * HD)
-
-    (slots,) = call(
+    arrived = lax.all_to_all(chunks, ("section", "fsdp"), 0, 0)
+    token = ((SUBLANES, HD), F32)
+    summed, summed_token = call(
+        sum_kernel, "sum_maps", [((n_fsdp, 1, 2 * width), F32), token], (), (arrived,)
+    )
+    everywhere = lax.all_to_all(summed, "fsdp", 0, 0)
+
+    own_slots, other_slots = call(
         slot_gradient_kernel,
         "slot_gradient",
-        [((MB, VIS, HALF), BF)],
+        [((VIS, HALF), BF)] * 2,
         (core, counts, begins),
-        (
-            gathered,
-            last_gradient,
-            lora_gradient_0,
-            columns,
-            downs,
-            gains,
-            entry,
-            inverse_0,
-            gradient,
-        ),
-    )
-    (hidden_1,) = call(
-        second_output_kernel, "second_output", [wide], (), (values_1, weights, hidden_0)
-    )
-
-    first = section == 0
-
-    def halves(mine, theirs):
-        left = jnp.where(first, mine, theirs)
-        right = jnp.where(first, theirs, mine)
-        return jnp.concatenate([left, right], axis=-1)
-
-    slot_rows = halves(
-        jnp.where(first, slots[0], slots[1]), swap_cores(jnp.where(first, slots[1], slots[0]))
-    )
-    hidden = halves(
-        jnp.where(first, hidden_0, hidden_1), swap_cores(jnp.where(first, hidden_1, hidden_0))
+        (gathered, ups, columns, downs, gains, entry, inverse_0, gradient),
+    )
+    own_hidden, other_hidden = call(
+        second_output_kernel,
+        "second_output",
+        [wide] * 2,
+        (core,),
+        (values_1, weights, hidden_0),
+        after=(summed_token,),
+    )
+    slots, slots_placed = call(
+        place_kernel,
+        "place_slots",
+        [((VIS, 2 * HALF), BF), token],
+        (core,),
+        (own_slots, swap_cores(other_slots)),
+    )
+    hidden, hidden_placed = call(
+        place_kernel,
+        "place_hidden",
+        [((ROWS, 2 * HALF), BF), token],
+        (core,),
+        (own_hidden, swap_cores(other_hidden)),
+    )
+    down_sum, up_sum = call(
+        functools.partial(maps_kernel, scale=1.0 / math.sqrt(MB * SEQ * n_fsdp)),
+        "maps",
+        [((RANK, 2 * HALF), F32), ((RANK, 2 * HD), F32)],
+        (),
+        (everywhere,),
+        after=(slots_placed, hidden_placed),
     )
     return (
         hidden.reshape(1, MB, SEQ, 2 * HALF),
-        slot_rows[None, None],
-        down_sum[None],
+        slots[None, None],
+        down_sum.T[None],
         up_sum[None],
     )
 

time: 208 us -> 203 us (0.976)
  blocking collectives: 50.3 us -> 86.4 us
  waiting for transfers between devices: 66.5 us -> 38.5 us
  starting transfers between devices: 32.2 us -> 17.2 us
  Pallas kernels: 14.1 us -> 19.8 us
    all_to_all x0 -> x1, blocking collectives: none -> 24.4 us  [on_device(): arrived = lax.all_to_all(chunks, ('section', 'fsdp'), 0, 0)]
    all_to_all x2 -> x1, waiting for transfers between devices: 21.6 us -> 0.86 us  [on_device(): everywhere = lax.all_to_all(summed, 'fsdp', 0, 0)]
    all_to_all x2 -> x3, blocking collectives: 25.3 us -> 37.2 us  [to_heads(): return lax.all_to_all(block, ('section', 'tp'), 0, 0)]
    all_to_all x2 -> x1, starting transfers between devices: 15.5 us -> 4.63 us  [on_device(): everywhere = lax.all_to_all(summed, 'fsdp', 0, 0)]
    all_to_all x2 -> x1, waiting for transfers between devices: 12.1 us -> 5.26 us  [to_heads(): return lax.all_to_all(block, ('section', 'tp'), 0, 0)]
    pallas_call x11 -> x15, Pallas kernels: 14.1 us -> 19.8 us  [call(): pl.pallas_call(body, out_shape=[jax.ShapeDtypeStruct(shape, dtype) for sh...]
    all_to_all x2 -> x1, starting transfers between devices: 8.75 us -> 4.93 us  [to_heads(): return lax.all_to_all(block, ('section', 'tp'), 0, 0)]
    unnamed x61 -> x76, local copies, waits for them, and re-layouts: 21.5 us -> 24 us
  transfers between devices with their start and end apart: 9 -> 7, of which waited for: 6 -> 5; matrix products, arithmetic and copies ran while one was open for 2% -> 0% of each run, Pallas kernels for 5% -> 6%
where the time goes in v5:
time: 203 us; the launch traced here: 202 us
  blocking collectives  86.4 us (43%)
  waiting for transfers between devices  38.5 us (19%)
  local copies, waits for them, and re-layouts  25 us (12%)
  Pallas kernels  19.8 us (10%)
  starting transfers between devices  17.2 us (8%)
  between operations  14.3 us (7%)
    all_to_all x3, blocking collectives, to_heads(): return lax.all_to_all(block, ('section', 'tp'), 0, 0)  37.2 us
    all_gather x1, waiting for transfers between devices, on_device(): lax.all_gather(head_columns, 'fsdp', axis=0, axis_index_groups=row_groups)  28.9 us
    all_to_all x1, blocking collectives, on_device(): lax.all_to_all(pieces, ('section', 'fsdp'), 0, 0, axis_index_groups=head_...  24.8 us
    all_to_all x1, blocking collectives, on_device(): arrived = lax.all_to_all(chunks, ('section', 'fsdp'), 0, 0)  24.4 us
    unnamed x76, local copies, waits for them, and re-layouts  24 us
    pallas_call x15, Pallas kernels, call(): pl.pallas_call(body, out_shape=[jax.ShapeDtypeStruct(shape, dtype) for sh...  19.8 us
    ppermute x3, starting transfers between devices, swap_cores(): return lax.ppermute(block, 'section', [(0, 1), (1, 0)])  7.6 us
    all_to_all x1, waiting for transfers between devices, to_heads(): return lax.all_to_all(block, ('section', 'tp'), 0, 0)  5.26 us
  transfers between devices with their start and end apart: 7, of which 5 were waited for; matrix products, arithmetic and copies ran while one was open for 0% of the time, Pallas kernels for 6%

profile of v5, /device:TPU:1, one launch (start us, length us, event | category | flops | bytes accessed | tf_op | source)
XLA Modules:
  0.0 202.0 jit_solution(1131488449175371283)
XLA Ops:
  7.2 0.0 copy-start.35
  7.2 0.0 copy-start.33
  7.2 0.0 all-gather.2.cloned.1.call-start
  7.3 1.0 reshape.18
  8.2 0.1 broadcast_in_dim.24
  8.3 24.8 %all_to_all.35 = bf16[16,16,1024]{2,1,0:T(8,128)(2,1)} all-to-all(bf16[16,16,1024]{2,1,0:T(8,128)(2,1)S(1)} %bitcast.42), channel_id=1, replica_groups={{0,4,8,12,16,20,24,28,256,260,264,268,272,276,280,284},{32,36,40,44,48,..., dimensions={0} | all-to-all | bytes 1048576 | tf_op jit(solution)/shard_map/all_to_all | solution.py:426
  33.1 0.0 all-gather.2.cloned.1.call-update
  33.1 0.7 reduce
  33.8 0.1 pad_add_fusion.refs_0_
  33.9 0.0 copy-start.4
  33.9 1.2 copy-done.4
  35.2 1.0 copy-done.9
  36.2 0.9 copy-done.15
  37.1 0.8 copy-done.22
  37.9 0.8 copy-done.23
  38.7 0.6 pack.1
  39.3 2.9 %collective-permute-start = (bf16[432,1024]{1,0:T(8,128)(2,1)S(1)}, bf16[432,1024]{1,0:T(8,128)(2,1)S(1)}, u32[]{:S(2)}, u32[]{:S(2)}) collective-permute-start(bf16[432,1024]{1,0:T(8,128)(2,1)S(1)} %pack.1), channel_id=1, source_target_pairs={{0,256},{256,0},{1,257},{257,1},{2,258},{258,2},{3,259},{259,3},{4... | collective-permute-start | bytes 2654216 | tf_op jit(solution)/shard_map/ppermute | solution.py:389
  42.2 2.0 %collective-permute-done.refs_4_ = bf16[432,1024]{1,0:T(8,128)(2,1)S(1)} collective-permute-done((bf16[432,1024]{1,0:T(8,128)(2,1)S(1)}, bf16[432,1024]{1,0:T(8,128)(2,1)S(1)}, u32[]{:S(2)}, u32[]{:S(2)}) %collective-permute-start) | collective-permute-done | bytes 884768 | tf_op jit(solution)/shard_map/ppermute | solution.py:389
  44.2 1.2 copy-done.11
  45.4 2.6 %prepare.1 = (bf16[2,2,1024,128]{3,2,1,0:T(8,128)(2,1)S(1)}, bf16[256,1024]{1,0:T(8,128)(2,1)S(1)}, bf16[256,1024]{1,0:T(8,128)(2,1)S(1)}, bf16[2,16,1024]{2,1,0...) custom-call(s32[2]{0:T(128)S(1)} %pad_add_fusion.refs_0_, ...), custom_call_target="tpu_custom_call" | custom-call | bytes 7634944 | tf_op jit(solution)/shard_map/prepare/pallas_call | solution.py:375
  48.0 0.0 copy-start.18
  48.1 13.6 %all_to_all.36.refs_1_ = bf16[8,304,128]{2,1,0:T(8,128)(2,1)S(1)} all-to-all(bf16[8,304,128]{2,1,0:T(8,128)(2,1)S(1)} %get-tuple-element.37), channel_id=1, replica_groups=mesh['section'=2,'fsdp'=64,'tp'=4] {'section','tp'}, dimensions={0} | all-to-all | bytes 1245184 | tf_op jit(solution)/shard_map/all_to_all | solution.py:393
  61.7 0.9 entry_norm.1
  62.6 0.8 copy-done.13
  63.4 28.9 %all-gather.2.cloned.1.call-done.refs_1_.refs_2_.refs_5_ = bf16[8,2,128,1024]{3,2,1,0:T(8,128)(2,1)} async-done(((bf16[1,2,128,1024]{3,2,1,0:T(8,128)(2,1)}), bf16[8,2,128,1024]{3,2,1,0:T(8,128)(2,1)}) %all-gather.2.cloned.1.call-update) | async-done | bytes 4194320 | tf_op jit(solution)/shard_map/all_gather | solution.py:430
  92.3 2.2 %copy-done = bf16[8,2,128,1024]{3,2,1,0:T(8,128)(2,1)S(1)} copy-done((bf16[8,2,128,1024]{3,2,1,0:T(8,128)(2,1)S(1)}, bf16[8,2,128,1024]{3,2,1,0:T(8,128)(2,1)}, u32[]{:S(2)}) %copy-start) | copy-done | bytes 4194328
  94.5 1.8 values_0.1
  96.3 4.9 %all-to-all-start.2 = ((bf16[8,256,128]{2,1,0:T(8,128)(2,1)}), bf16[8,256,128]{2,1,0:T(8,128)(2,1)S(1)}, u32[]{:S(2)}, u32[]{:S(2)}) async-start(bf16[8,256,128]{2,1,0:T(8,128)(2,1)} %values_0.1), calls=%async_computation.2 | async-start | bytes 1048576 | tf_op jit(solution)/shard_map/all_to_all | solution.py:393
  101.3 2.2 %copy-done.1 = bf16[8,2,128,1024]{3,2,1,0:T(8,128)(2,1)S(1)} copy-done((bf16[8,2,128,1024]{3,2,1,0:T(8,128)(2,1)S(1)}, bf16[8,2,128,1024]{3,2,1,0:T(8,128)(2,1)}, u32[]{:S(2)}) %copy-start.1) | copy-done | bytes 4194328
  103.5 1.0 copy-done.14
  104.5 0.9 scaled_1.1.refs_3_
  105.4 5.3 %all-to-all-done.2.refs_0_ = bf16[8,256,128]{2,1,0:T(8,128)(2,1)S(1)} async-done(((bf16[8,256,128]{2,1,0:T(8,128)(2,1)}), bf16[8,256,128]{2,1,0:T(8,128)(2,1)S(1)}, u32[]{:S(2)}, u32[]{:S(2)}) %all-to-all-start.2) | async-done | bytes 524320 | tf_op jit(solution)/shard_map/all_to_all | solution.py:393
  110.6 0.8 copy-done.5
  111.4 1.2 copy-done.6
  112.6 0.6 first_output.1
  113.2 8.2 %all_to_all.37.refs_0_ = f32[8,8,256]{2,1,0:T(8,128)S(1)} all-to-all(f32[8,8,256]{2,1,0:T(8,128)S(1)} %get-tuple-element.46), channel_id=1, replica_groups=mesh['section'=2,'fsdp'=64,'tp'=4] {'section','tp'}, dimensions={0} | all-to-all | bytes 131072 | tf_op jit(solution)/shard_map/all_to_all | solution.py:393
  121.4 1.0 copy-done.19
  122.5 1.0 first_gradient.1
  123.5 0.0 copy-start.12
  123.5 0.8 copy-done.12
  124.3 0.8 copy-done.20
  125.1 0.6 copy-done.25
  125.7 0.6 copy-done.31
  126.3 1.8 values_1.1
  128.2 0.0 reduce-scatter.2.cloned.1.call-update
  128.2 15.4 %all_to_all.38.refs_1_.refs_3_ = bf16[8,304,128]{2,1,0:T(8,128)(2,1)S(1)} all-to-all(bf16[8,304,128]{2,1,0:T(8,128)(2,1)} %copy-done.12), channel_id=1, replica_groups=mesh['section'=2,'fsdp'=64,'tp'=4] {'section','tp'}, dimensions={0} | all-to-all | bytes 1245184 | tf_op jit(solution)/shard_map/all_to_all | solution.py:393
  143.6 1.0 copy-done.8
  144.6 1.1 map_gradient.1
  145.7 24.4 %all_to_all.39.refs_0_ = f32[128,1,384]{2,1,0:T(1,128)S(1)} all-to-all(f32[128,1,384]{2,1,0:T(1,128)S(1)} %map_gradient.1), channel_id=1, replica_groups=mesh['section'=2,'fsdp'=64,'tp'=4] {'section','fsdp'}, dimensions={0} | all-to-all | bytes 393216 | tf_op jit(solution)/shard_map/all_to_all | solution.py:523
  170.1 0.8 sum_maps.1
  170.9 0.8 copy-done.24
  171.8 1.7 second_output.1
  173.5 0.8 copy-done.16
  174.2 2.8 %collective-permute-start.1 = (bf16[256,1024]{1,0:T(8,128)(2,1)}, bf16[256,1024]{1,0:T(8,128)(2,1)S(1)}, u32[]{:S(2)}, u32[]{:S(2)}) collective-permute-start(bf16[256,1024]{1,0:T(8,128)(2,1)} %get-tuple-element.58), channel_id=1, source_target_pairs={{0,256},{256,0},{1,257},{257,1},{2,258},{258,2},{3,259},{259,3},{4... | collective-permute-start | bytes 1572872 | tf_op jit(solution)/shard_map/ppermute | solution.py:389
  177.0 4.6 %all-to-all-start.6 = ((f32[64,1,768]{2,1,0:T(1,128)}), f32[64,1,768]{2,1,0:T(1,128)S(1)}, u32[]{:S(2)}, u32[]{:S(2)}) async-start(f32[64,1,768]{2,1,0:T(1,128)} %get-tuple-element.65), calls=%async_computation.7 | async-start | bytes 393216 | tf_op jit(solution)/shard_map/all_to_all | solution.py:528
  181.7 2.2 %copy-done.3 = bf16[8,2,128,1024]{3,2,1,0:T(8,128)(2,1)S(1)} copy-done((bf16[8,2,128,1024]{3,2,1,0:T(8,128)(2,1)S(1)}, bf16[8,2,128,1024]{3,2,1,0:T(8,128)(2,1)}, u32[]{:S(2)}) %copy-start.3) | copy-done | bytes 4194328
  183.9 1.0 copy-done.21
  184.9 2.4 %slot_gradient.1 = (bf16[96,1024]{1,0:T(8,128)(2,1)S(1)}, bf16[96,1024]{1,0:T(8,128)(2,1)S(1)}) custom-call(s32[2]{0:T(128)S(1)} %copy-done.28, s32[2]{0:T(128)S(1)} %bitcast.37, s32[2]{0:T(128)S(1)} %bitcast.39, bf16[8,304,128]{2,1,0:T(8,128)(2,1)S(1)} %all_to_all.38.refs_1_.refs_3_, bf16[2,16,1024]{2,1,0:T(8,128)(2,1)S(1)} %get-tuple-element.39.refs_3_.refs_2_.refs_4_, ...), custom_call_target="tpu_custom_call" | custom-call | bytes 6586368 | tf_op jit(solution)/shard_map/slot_gradient/pallas_call | solution.py:375
  187.3 2.0 collective-permute-start.2
  189.3 1.4 collective-permute-done.2.refs_2_
  190.7 1.3 place_slots.1
  192.0 1.6 place_hidden.1
  193.6 0.9 all-to-all-done.6.refs_0_
  194.4 0.7 maps.1
  (54 shorter events, 0.1 us)
Async XLA Ops:
  7.2 37.0 %copy-start.37 = (s32[2,1]{0,1:T(1,128)S(1)}, s32[2,1]{0,1:T(1,128)}, u32[]{:S(2)}) copy-start(s32[2,1]{0,1:T(1,128)} %param.16) | copy-start | bytes 28
  7.2 37.0 %copy-start.35 = (s32[2,1]{0,1:T(1,128)S(1)}, s32[2,1]{0,1:T(1,128)}, u32[]{:S(2)}) copy-start(s32[2,1]{0,1:T(1,128)} %param.15) | copy-start | bytes 28
  7.2 37.0 %copy-start.33 = (s32[2,1]{0,1:T(1,128)S(1)}, s32[2,1]{0,1:T(1,128)}, u32[]{:S(2)}) copy-start(s32[2,1]{0,1:T(1,128)} %param.14) | copy-start | bytes 28
  7.2 37.0 %copy-start.10 = (bf16[2,128,2048]{2,1,0:T(8,128)(2,1)S(1)}, bf16[2,128,2048]{2,1,0:T(8,128)(2,1)}, u32[]{:S(2)}) copy-start(bf16[2,128,2048]{2,1,0:T(8,128)(2,1)} %refs_11_.1) | copy-start | bytes 3145732
  7.2 85.1 %all-gather.2.cloned.1.call-start = ((), (), s32[]{:S(2)}) async-start(), calls=%async_computation.8 | async-start | bytes 4718592 | tf_op jit(solution)/shard_map/all_gather | solution.py:430
  33.9 27.8 %copy-start.27 = (s32[2]{0:T(128)}, s32[2]{0:T(128)S(1)}, u32[]{:S(2)}) copy-start(s32[2]{0:T(128)S(1)} %pad_add_fusion.refs_0_) | copy-start | bytes 28
  33.9 1.2 copy-start.4
  35.2 1.0 copy-start.9
  36.2 0.9 copy-start.15
  37.1 0.8 copy-start.22
  37.9 0.8 copy-start.23
  39.3 4.9 %collective-permute-start = (bf16[432,1024]{1,0:T(8,128)(2,1)S(1)}, bf16[432,1024]{1,0:T(8,128)(2,1)S(1)}, u32[]{:S(2)}, u32[]{:S(2)}) collective-permute-start(bf16[432,1024]{1,0:T(8,128)(2,1)S(1)} %pack.1), channel_id=1, source_target_pairs={{0,256},{256,0},{1,257},{257,1},{2,258},{258,2},{3,259},{259,3},{4... | collective-permute-start | bytes 2654216 | tf_op jit(solution)/shard_map/ppermute | solution.py:389
  44.2 1.2 copy-start.11
  48.0 13.7 %copy-start.18 = (bf16[256,1024]{1,0:T(8,128)(2,1)}, bf16[256,1024]{1,0:T(8,128)(2,1)S(1)}, u32[]{:S(2)}) copy-start(bf16[256,1024]{1,0:T(8,128)(2,1)S(1)} %get-tuple-element.48.refs_4_) | copy-start | bytes 1572868
  62.6 0.8 copy-start.13
  63.4 37.9 %copy-start.7 = (bf16[256,1024]{1,0:T(8,128)(2,1)}, bf16[256,1024]{1,0:T(8,128)(2,1)S(1)}, u32[]{:S(2)}) copy-start(bf16[256,1024]{1,0:T(8,128)(2,1)S(1)} %get-tuple-element.41.refs_0_.refs_3_) | copy-start | bytes 1572868
  63.4 37.9 %copy-start.29 = (f32[16,256]{1,0:T(8,128)}, f32[16,256]{1,0:T(8,128)S(1)}, u32[]{:S(2)}) copy-start(f32[16,256]{1,0:T(8,128)S(1)} %get-tuple-element.52.refs_4_) | copy-start | bytes 49156
  92.3 2.2 %copy-start = (bf16[8,2,128,1024]{3,2,1,0:T(8,128)(2,1)S(1)}, bf16[8,2,128,1024]{3,2,1,0:T(8,128)(2,1)}, u32[]{:S(2)}) copy-start(bf16[8,2,128,1024]{3,2,1,0:T(8,128)(2,1)} %all-gather.2.cloned.1.call-done.refs_1_.refs_2_.refs_5_) | copy-start | bytes 12582916
  96.3 14.3 %all-to-all-start.2 = ((bf16[8,256,128]{2,1,0:T(8,128)(2,1)}), bf16[8,256,128]{2,1,0:T(8,128)(2,1)S(1)}, u32[]{:S(2)}, u32[]{:S(2)}) async-start(bf16[8,256,128]{2,1,0:T(8,128)(2,1)} %values_0.1), calls=%async_computation.2 | async-start | bytes 1048576 | tf_op jit(solution)/shard_map/all_to_all | solution.py:393
  101.3 69.7 %reduce-scatter.2.cloned.1.call-start = ((), (), s32[]{:S(2)}) async-start(), calls=%async_computation.9 | async-start | bytes 589824 | tf_op jit(solution)/shard_map/reduce_scatter | solution.py:513
  101.3 2.2 %copy-start.1 = (bf16[8,2,128,1024]{3,2,1,0:T(8,128)(2,1)S(1)}, bf16[8,2,128,1024]{3,2,1,0:T(8,128)(2,1)}, u32[]{:S(2)}) copy-start(bf16[8,2,128,1024]{3,2,1,0:T(8,128)(2,1)} %all-gather.2.cloned.1.call-done.refs_1_.refs_2_.refs_5_) | copy-start | bytes 12582916
  103.5 1.0 copy-start.14
  110.6 0.8 copy-start.5
  111.4 14.9 %copy-start.2 = (bf16[8,2,128,1024]{3,2,1,0:T(8,128)(2,1)S(1)}, bf16[8,2,128,1024]{3,2,1,0:T(8,128)(2,1)}, u32[]{:S(2)}) copy-start(bf16[8,2,128,1024]{3,2,1,0:T(8,128)(2,1)} %all-gather.2.cloned.1.call-done.refs_1_.refs_2_.refs_5_) | copy-start | bytes 12582916
  111.4 1.2 copy-start.6
  121.4 1.0 copy-start.19
  123.5 0.8 copy-start.12
  124.3 0.8 copy-start.20
  125.1 0.6 copy-start.25
  125.7 0.6 copy-start.31
  126.3 17.3 %copy-start.28 = (s32[2]{0:T(128)S(1)}, s32[2]{0:T(128)}, u32[]{:S(2)}) copy-start(s32[2]{0:T(128)} %copy-done.27) | copy-start | bytes 28
  126.3 17.3 %copy-start.30 = (f32[16,256]{1,0:T(8,128)S(1)}, f32[16,256]{1,0:T(8,128)}, u32[]{:S(2)}) copy-start(f32[16,256]{1,0:T(8,128)} %copy-done.29) | copy-start | bytes 49156
  126.3 17.2 %copy-start.26 = (f32[16,1024]{1,0:T(8,128)S(1)}, f32[16,1024]{1,0:T(8,128)}, u32[]{:S(2)}) copy-start(f32[16,1024]{1,0:T(8,128)} %copy-done.25) | copy-start | bytes 196612
  126.3 17.3 %copy-start.32 = (f32[8,256]{1,0:T(8,128)S(1)}, f32[8,256]{1,0:T(8,128)}, u32[]{:S(2)}) copy-start(f32[8,256]{1,0:T(8,128)} %copy-done.31) | copy-start | bytes 24580
  128.2 53.5 %copy-start.34 = (s32[2,1]{0,1:T(1,128)S(1)}, s32[2,1]{0,1:T(1,128)}, u32[]{:S(2)}) copy-start(s32[2,1]{0,1:T(1,128)} %param.14) | copy-start | bytes 28
  128.2 53.5 %copy-start.36 = (s32[2,1]{0,1:T(1,128)S(1)}, s32[2,1]{0,1:T(1,128)}, u32[]{:S(2)}) copy-start(s32[2,1]{0,1:T(1,128)} %param.15) | copy-start | bytes 28
  143.6 1.0 copy-start.8
  170.9 0.8 copy-start.24
  173.5 0.8 copy-start.16
  174.2 17.7 %collective-permute-start.1 = (bf16[256,1024]{1,0:T(8,128)(2,1)}, bf16[256,1024]{1,0:T(8,128)(2,1)S(1)}, u32[]{:S(2)}, u32[]{:S(2)}) collective-permute-start(bf16[256,1024]{1,0:T(8,128)(2,1)} %get-tuple-element.58), channel_id=1, source_target_pairs={{0,256},{256,0},{1,257},{257,1},{2,258},{258,2},{3,259},{259,3},{4... | collective-permute-start | bytes 1572872 | tf_op jit(solution)/shard_map/ppermute | solution.py:389
  177.0 17.4 %all-to-all-start.6 = ((f32[64,1,768]{2,1,0:T(1,128)}), f32[64,1,768]{2,1,0:T(1,128)S(1)}, u32[]{:S(2)}, u32[]{:S(2)}) async-start(f32[64,1,768]{2,1,0:T(1,128)} %get-tuple-element.65), calls=%async_computation.7 | async-start | bytes 393216 | tf_op jit(solution)/shard_map/all_to_all | solution.py:528
  181.7 2.2 %copy-start.3 = (bf16[8,2,128,1024]{3,2,1,0:T(8,128)(2,1)S(1)}, bf16[8,2,128,1024]{3,2,1,0:T(8,128)(2,1)}, u32[]{:S(2)}) copy-start(bf16[8,2,128,1024]{3,2,1,0:T(8,128)(2,1)} %all-gather.2.cloned.1.call-done.refs_1_.refs_2_.refs_5_) | copy-start | bytes 12582916
  183.9 1.0 copy-start.21
  184.9 7.1 %copy-start.17 = (bf16[256,1024]{1,0:T(8,128)(2,1)S(1)}, bf16[256,1024]{1,0:T(8,128)(2,1)}, u32[]{:S(2)}) copy-start(bf16[256,1024]{1,0:T(8,128)(2,1)} %copy-done.16) | copy-start | bytes 1572868
  187.3 3.3 %collective-permute-start.2 = (bf16[96,1024]{1,0:T(8,128)(2,1)S(1)}, bf16[96,1024]{1,0:T(8,128)(2,1)S(1)}, u32[]{:S(2)}, u32[]{:S(2)}) collective-permute-start(bf16[96,1024]{1,0:T(8,128)(2,1)S(1)} %get-tuple-element.63), channel_id=1, source_target_pairs={{0,256},{256,0},{1,257},{257,1},{2,258},{258,2},{3,259},{259,3},{4... | collective-permute-start | bytes 589832 | tf_op jit(solution)/shard_map/ppermute | solution.py:389
Sparse Core Ops, SparseCore 0:
  33.2 59.0 all-gather.1
  128.3 34.1 reduce-scatter.1

commit v6 on v5

--- a/solution.py
+++ b/solution.py
@@ -242,7 +242,7 @@
 
 def first_gradient_kernel(
     received, weights, hidden, scaled, cotangent_half, gains, downs, value_rows, lora_gradient,
-    gradient, normed, inverse_row, down_gradient, payload,
+    gradient, normed, kept, payload,
 ):
     total = received[0]
     for peer in range(1, PEERS):
@@ -250,12 +250,13 @@
     sums = rows_to_columns(total)
     column = inverse_of(sums[:, 0:1])
     factor = column * column * column * sums[:, 1:2] / MODEL_WIDTH
-    inverse_row[...] = inverse_of(total)
     hidden_float = hidden[...].astype(F32)
     gained = hidden_float * gains[1][0:1, :].astype(F32)
     rows = (gained * column).astype(BF)
     normed[...] = rows
-    down_gradient[...] = nn(lora_gradient[...].astype(BF), rows)
+    kept[:RANK, :] = nn(lora_gradient[...].astype(BF), rows)
+    kept[RANK:, :ROWS] = inverse_of(total)
+    kept[RANK:, ROWS:] = jnp.zeros((SUBLANES, HALF - ROWS), F32)
     grad = (
         cotangent_half[...].astype(F32) + column * scaled[...] - hidden_float * factor
     ).astype(BF)
@@ -284,16 +285,16 @@
 
 
 def map_gradient_kernel(
-    core, received, ups, normed_0, adapter_0, inverse_row, gradient_1, down_gradient_1, out
+    core, received, ups, normed_0, adapter_0, gradient_1, kept, out
 ):
     _, low_rank = total_of_payloads(received)
     lora_0 = ADAPTER_SCALE * nt(ups[0], gathered_gradient(received))
     own = received[core[0] * 4 + core[1], :ROWS, :]
     down_0 = nn(lora_0.astype(BF), normed_0[...])
     up_0 = ADAPTER_SCALE * nn(adapter_0[...].astype(BF), own)
-    adapter_1 = (low_rank * inverse_row[0:1, :]).astype(BF)
+    adapter_1 = (low_rank * kept[RANK : RANK + 1, :ROWS]).astype(BF)
     up_1 = ADAPTER_SCALE * nn(adapter_1, gradient_1[...])
-    chunks = (map_chunks(down_0, up_0), map_chunks(down_gradient_1[...], up_1))
+    chunks = (map_chunks(down_0, up_0), map_chunks(kept[:RANK, :], up_1))
     for layer in range(2):
         out[layer * 4 * RANK : (layer + 1) * 4 * RANK] = chunks[layer][:, None, :]
 
@@ -483,14 +484,13 @@
         (),
         (to_heads(partial_0), weights, entry, scaled_1),
     )
-    gradient, normed_1, inverse_row, down_gradient_1, payload = call(
+    gradient, normed_1, kept, payload = call(
         first_gradient_kernel,
         "first_gradient",
         [
             wide,
             wide,
-            ((SUBLANES, ROWS), F32),
-            ((RANK, HALF), F32),
+            ((RANK + SUBLANES, HALF), F32),
             ((PEERS, R_PAY, HD), BF),
         ],
         (),
@@ -517,7 +517,7 @@
         "map_gradient",
         [((2 * n_fsdp, 1, HALF // 4 + HD), F32)],
         (core,),
-        (gathered, ups, normed_0, adapter_0, inverse_row, own_gradient_1, down_gradient_1),
+        (gathered, ups, normed_0, adapter_0, own_gradient_1, kept),
     )
     width = HALF // 4 + HD
     arrived = lax.all_to_all(chunks, ("section", "fsdp"), 0, 0)
@@ -540,7 +540,6 @@
         [wide] * 2,
         (core,),
         (values_1, weights, hidden_0),
-        after=(summed_token,),
     )
     slots, slots_placed = call(
         place_kernel,

time: 203 us -> 203 us (level)
  blocking collectives: 86.4 us -> 62 us
  starting transfers between devices: 17.2 us -> 32.9 us
  waiting for transfers between devices: 38.5 us -> 46.2 us
    all_to_all x1 -> x0, blocking collectives: 24.4 us -> none  [on_device(): arrived = lax.all_to_all(chunks, ('section', 'fsdp'), 0, 0)]
    all_to_all x0 -> x1, starting transfers between devices: none -> 10.2 us  [on_device(): arrived = lax.all_to_all(chunks, ('section', 'fsdp'), 0, 0)]
    reduce_scatter x1, waiting for transfers between devices: 0.01 us -> 5.94 us  [on_device(): lax.psum_scatter(partial_1, ('section', 'tp'), scatter_dimension=0)]
    all_to_all x1, starting transfers between devices: 4.63 us -> 10.2 us  [on_device(): everywhere = lax.all_to_all(summed, 'fsdp', 0, 0)]
    all_to_all x0 -> x1, waiting for transfers between devices: none -> 2.98 us  [on_device(): arrived = lax.all_to_all(chunks, ('section', 'fsdp'), 0, 0)]
    unnamed x76 -> x72, local copies, waits for them, and re-layouts: 24 us -> 23.4 us
  transfers between devices with their start and end apart: 7 -> 8, of which waited for: 5 -> 6; matrix products, arithmetic and copies ran while one was open for 0% -> 0% of each run, Pallas kernels for 6% -> 7%
where the time goes in v6:
time: 203 us; the launch traced here: 201 us
  blocking collectives  62 us (31%)
  waiting for transfers between devices  46.2 us (23%)
  starting transfers between devices  32.9 us (16%)
  local copies, waits for them, and re-layouts  24.4 us (12%)
  Pallas kernels  20.5 us (10%)
  between operations  14.3 us (7%)
    all_to_all x3, blocking collectives, to_heads(): return lax.all_to_all(block, ('section', 'tp'), 0, 0)  37.2 us
    all_gather x1, waiting for transfers between devices, on_device(): lax.all_gather(head_columns, 'fsdp', axis=0, axis_index_groups=row_groups)  28.9 us
    all_to_all x1, blocking collectives, on_device(): lax.all_to_all(pieces, ('section', 'fsdp'), 0, 0, axis_index_groups=head_...  24.8 us
    unnamed x72, local copies, waits for them, and re-layouts  23.4 us
    pallas_call x15, Pallas kernels, call(): pl.pallas_call(body, out_shape=[jax.ShapeDtypeStruct(shape, dtype) for sh...  20.5 us
    all_to_all x1, starting transfers between devices, on_device(): arrived = lax.all_to_all(chunks, ('section', 'fsdp'), 0, 0)  10.2 us
    all_to_all x1, starting transfers between devices, on_device(): everywhere = lax.all_to_all(summed, 'fsdp', 0, 0)  10.2 us
    ppermute x3, starting transfers between devices, swap_cores(): return lax.ppermute(block, 'section', [(0, 1), (1, 0)])  7.59 us
  transfers between devices with their start and end apart: 8, of which 6 were waited for; matrix products, arithmetic and copies ran while one was open for 0% of the time, Pallas kernels for 7%

profile of v6, /device:TPU:1, one launch (start us, length us, event | category | flops | bytes accessed | tf_op | source)
XLA Modules:
  0.0 201.1 jit_solution(6430299791128421790)
XLA Ops:
  7.2 0.0 copy-start.33
  7.2 0.0 copy-start.31
  7.2 0.0 all-gather.2.cloned.1.call-start
  7.3 1.0 reshape.18
  8.2 0.1 broadcast_in_dim.24
  8.3 24.8 %all_to_all.35 = bf16[16,16,1024]{2,1,0:T(8,128)(2,1)} all-to-all(bf16[16,16,1024]{2,1,0:T(8,128)(2,1)S(1)} %bitcast.42), channel_id=1, replica_groups={{0,4,8,12,16,20,24,28,256,260,264,268,272,276,280,284},{32,36,40,44,48,..., dimensions={0} | all-to-all | bytes 1048576 | tf_op jit(solution)/shard_map/all_to_all | solution.py:427
  33.1 0.0 all-gather.2.cloned.1.call-update
  33.1 0.7 reduce
  33.8 0.1 pad_add_fusion.refs_0_
  33.9 0.0 copy-start.4
  33.9 1.2 copy-done.4
  35.2 1.0 copy-done.9
  36.2 0.9 copy-done.15
  37.1 0.8 copy-done.22
  37.9 0.8 copy-done.23
  38.7 0.6 pack.1
  39.3 2.9 %collective-permute-start = (bf16[432,1024]{1,0:T(8,128)(2,1)S(1)}, bf16[432,1024]{1,0:T(8,128)(2,1)S(1)}, u32[]{:S(2)}, u32[]{:S(2)}) collective-permute-start(bf16[432,1024]{1,0:T(8,128)(2,1)S(1)} %pack.1), channel_id=1, source_target_pairs={{0,256},{256,0},{1,257},{257,1},{2,258},{258,2},{3,259},{259,3},{4... | collective-permute-start | bytes 2654216 | tf_op jit(solution)/shard_map/ppermute | solution.py:390
  42.2 2.0 %collective-permute-done.refs_4_ = bf16[432,1024]{1,0:T(8,128)(2,1)S(1)} collective-permute-done((bf16[432,1024]{1,0:T(8,128)(2,1)S(1)}, bf16[432,1024]{1,0:T(8,128)(2,1)S(1)}, u32[]{:S(2)}, u32[]{:S(2)}) %collective-permute-start) | collective-permute-done | bytes 884768 | tf_op jit(solution)/shard_map/ppermute | solution.py:390
  44.2 0.0 copy-start.11
  44.2 1.2 copy-done.11
  45.4 2.6 %prepare.1 = (bf16[2,2,1024,128]{3,2,1,0:T(8,128)(2,1)S(1)}, bf16[256,1024]{1,0:T(8,128)(2,1)S(1)}, bf16[256,1024]{1,0:T(8,128)(2,1)S(1)}, bf16[2,16,1024]{2,1,0...) custom-call(s32[2]{0:T(128)S(1)} %pad_add_fusion.refs_0_, ...), custom_call_target="tpu_custom_call" | custom-call | bytes 7634944 | tf_op jit(solution)/shard_map/prepare/pallas_call | solution.py:376
  48.0 0.0 copy-start.18
  48.1 13.6 %all_to_all.36.refs_1_ = bf16[8,304,128]{2,1,0:T(8,128)(2,1)S(1)} all-to-all(bf16[8,304,128]{2,1,0:T(8,128)(2,1)S(1)} %get-tuple-element.35), channel_id=1, replica_groups=mesh['section'=2,'fsdp'=64,'tp'=4] {'section','tp'}, dimensions={0} | all-to-all | bytes 1245184 | tf_op jit(solution)/shard_map/all_to_all | solution.py:394
  61.7 0.9 entry_norm.1
  62.6 0.8 copy-done.13
  63.4 28.9 %all-gather.2.cloned.1.call-done.refs_1_.refs_2_.refs_5_ = bf16[8,2,128,1024]{3,2,1,0:T(8,128)(2,1)} async-done(((bf16[1,2,128,1024]{3,2,1,0:T(8,128)(2,1)}), bf16[8,2,128,1024]{3,2,1,0:T(8,128)(2,1)}) %all-gather.2.cloned.1.call-update) | async-done | bytes 4194320 | tf_op jit(solution)/shard_map/all_gather | solution.py:431
  92.3 2.2 %copy-done = bf16[8,2,128,1024]{3,2,1,0:T(8,128)(2,1)S(1)} copy-done((bf16[8,2,128,1024]{3,2,1,0:T(8,128)(2,1)S(1)}, bf16[8,2,128,1024]{3,2,1,0:T(8,128)(2,1)}, u32[]{:S(2)}) %copy-start) | copy-done | bytes 4194328
  94.5 1.8 values_0.1
  96.3 4.9 %all-to-all-start.2 = ((bf16[8,256,128]{2,1,0:T(8,128)(2,1)}), bf16[8,256,128]{2,1,0:T(8,128)(2,1)S(1)}, u32[]{:S(2)}, u32[]{:S(2)}) async-start(bf16[8,256,128]{2,1,0:T(8,128)(2,1)} %values_0.1), calls=%async_computation.2 | async-start | bytes 1048576 | tf_op jit(solution)/shard_map/all_to_all | solution.py:394
  101.3 2.2 %copy-done.1 = bf16[8,2,128,1024]{3,2,1,0:T(8,128)(2,1)S(1)} copy-done((bf16[8,2,128,1024]{3,2,1,0:T(8,128)(2,1)S(1)}, bf16[8,2,128,1024]{3,2,1,0:T(8,128)(2,1)}, u32[]{:S(2)}) %copy-start.1) | copy-done | bytes 4194328
  103.5 1.0 copy-done.14
  104.5 0.9 scaled_1.1.refs_3_
  105.4 5.3 %all-to-all-done.2.refs_0_ = bf16[8,256,128]{2,1,0:T(8,128)(2,1)S(1)} async-done(((bf16[8,256,128]{2,1,0:T(8,128)(2,1)}), bf16[8,256,128]{2,1,0:T(8,128)(2,1)S(1)}, u32[]{:S(2)}, u32[]{:S(2)}) %all-to-all-start.2) | async-done | bytes 524320 | tf_op jit(solution)/shard_map/all_to_all | solution.py:394
  110.6 0.8 copy-done.5
  111.4 1.2 copy-done.6
  112.6 0.6 first_output.1
  113.2 8.2 %all_to_all.37.refs_0_ = f32[8,8,256]{2,1,0:T(8,128)S(1)} all-to-all(f32[8,8,256]{2,1,0:T(8,128)S(1)} %get-tuple-element.44), channel_id=1, replica_groups=mesh['section'=2,'fsdp'=64,'tp'=4] {'section','tp'}, dimensions={0} | all-to-all | bytes 131072 | tf_op jit(solution)/shard_map/all_to_all | solution.py:394
  121.4 1.0 copy-done.19
  122.5 1.0 first_gradient.1
  123.5 0.8 copy-done.12
  124.3 0.8 copy-done.20
  125.1 0.6 copy-done.24
  125.7 1.9 values_1.1
  127.6 0.0 reduce-scatter.2.cloned.1.call-update
  127.6 15.4 %all_to_all.38.refs_3_.refs_1_ = bf16[8,304,128]{2,1,0:T(8,128)(2,1)S(1)} all-to-all(bf16[8,304,128]{2,1,0:T(8,128)(2,1)} %copy-done.12), channel_id=1, replica_groups=mesh['section'=2,'fsdp'=64,'tp'=4] {'section','tp'}, dimensions={0} | all-to-all | bytes 1245184 | tf_op jit(solution)/shard_map/all_to_all | solution.py:394
  143.0 1.0 copy-done.8
  144.0 1.8 map_gradient.1
  145.8 10.2 %all-to-all-start.5 = ((f32[128,1,384]{2,1,0:T(1,128)}), f32[128,1,384]{2,1,0:T(1,128)S(1)}, u32[]{:S(2)}, u32[]{:S(2)}) async-start(f32[128,1,384]{2,1,0:T(1,128)} %map_gradient.1), calls=%async_computation.6 | async-start | bytes 393216 | tf_op jit(solution)/shard_map/all_to_all | solution.py:523
  156.0 5.9 %reduce-scatter.2.cloned.1.call-done = bf16[1,256,128]{2,1,0:T(8,128)(2,1)} async-done(((bf16[8,256,128]{2,1,0:T(8,128)(2,1)}), bf16[1,256,128]{2,1,0:T(8,128)(2,1)}) %reduce-scatter.2.cloned.1.call-update) | async-done | bytes 65552 | tf_op jit(solution)/shard_map/reduce_scatter | solution.py:513
  161.9 0.8 copy-done.26
  162.8 1.7 second_output.1
  164.4 0.8 copy-done.16
  165.2 2.2 %collective-permute-start.1 = (bf16[256,1024]{1,0:T(8,128)(2,1)}, bf16[256,1024]{1,0:T(8,128)(2,1)S(1)}, u32[]{:S(2)}, u32[]{:S(2)}) collective-permute-start(bf16[256,1024]{1,0:T(8,128)(2,1)} %get-tuple-element.50), channel_id=1, source_target_pairs={{0,256},{256,0},{1,257},{257,1},{2,258},{258,2},{3,259},{259,3},{4... | collective-permute-start | bytes 1572872 | tf_op jit(solution)/shard_map/ppermute | solution.py:390
  167.4 3.0 %all-to-all-done.5.refs_0_ = f32[128,1,384]{2,1,0:T(1,128)S(1)} async-done(((f32[128,1,384]{2,1,0:T(1,128)}), f32[128,1,384]{2,1,0:T(1,128)S(1)}, u32[]{:S(2)}, u32[]{:S(2)}) %all-to-all-start.5) | async-done | bytes 196640 | tf_op jit(solution)/shard_map/all_to_all | solution.py:523
  170.4 0.8 sum_maps.1
  171.2 10.2 %all-to-all-start.6 = ((f32[64,1,768]{2,1,0:T(1,128)}), f32[64,1,768]{2,1,0:T(1,128)S(1)}, u32[]{:S(2)}, u32[]{:S(2)}) async-start(f32[64,1,768]{2,1,0:T(1,128)} %get-tuple-element.61), calls=%async_computation.7 | async-start | bytes 393216 | tf_op jit(solution)/shard_map/all_to_all | solution.py:528
  181.4 2.2 %copy-done.3 = bf16[8,2,128,1024]{3,2,1,0:T(8,128)(2,1)S(1)} copy-done((bf16[8,2,128,1024]{3,2,1,0:T(8,128)(2,1)S(1)}, bf16[8,2,128,1024]{3,2,1,0:T(8,128)(2,1)}, u32[]{:S(2)}) %copy-start.3) | copy-done | bytes 4194328
  183.6 1.0 copy-done.21
  184.6 2.4 %slot_gradient.1 = (bf16[96,1024]{1,0:T(8,128)(2,1)S(1)}, bf16[96,1024]{1,0:T(8,128)(2,1)S(1)}) custom-call(s32[2]{0:T(128)S(1)} %copy-done.28, s32[2]{0:T(128)S(1)} %bitcast.37, s32[2]{0:T(128)S(1)} %bitcast.39, bf16[8,304,128]{2,1,0:T(8,128)(2,1)S(1)} %all_to_all.38.refs_3_.refs_1_, bf16[2,16,1024]{2,1,0:T(8,128)(2,1)S(1)} %get-tuple-element.37.refs_3_.refs_4_.refs_2_, ...), custom_call_target="tpu_custom_call" | custom-call | bytes 6586368 | tf_op jit(solution)/shard_map/slot_gradient/pallas_call | solution.py:376
  187.1 2.5 %collective-permute-start.2 = (bf16[96,1024]{1,0:T(8,128)(2,1)S(1)}, bf16[96,1024]{1,0:T(8,128)(2,1)S(1)}, u32[]{:S(2)}, u32[]{:S(2)}) collective-permute-start(bf16[96,1024]{1,0:T(8,128)(2,1)S(1)} %get-tuple-element.56), channel_id=1, source_target_pairs={{0,256},{256,0},{1,257},{257,1},{2,258},{258,2},{3,259},{259,3},{4... | collective-permute-start | bytes 589832 | tf_op jit(solution)/shard_map/ppermute | solution.py:390
  189.6 1.0 collective-permute-done.2.refs_2_
  190.7 1.3 place_slots.1
  192.0 1.6 place_hidden.1
  193.6 0.7 maps.1
  (51 shorter events, 0.1 us)
Async XLA Ops:
  7.2 37.0 %copy-start.35 = (s32[2,1]{0,1:T(1,128)S(1)}, s32[2,1]{0,1:T(1,128)}, u32[]{:S(2)}) copy-start(s32[2,1]{0,1:T(1,128)} %param.16) | copy-start | bytes 28
  7.2 37.0 %copy-start.33 = (s32[2,1]{0,1:T(1,128)S(1)}, s32[2,1]{0,1:T(1,128)}, u32[]{:S(2)}) copy-start(s32[2,1]{0,1:T(1,128)} %param.15) | copy-start | bytes 28
  7.2 37.0 %copy-start.31 = (s32[2,1]{0,1:T(1,128)S(1)}, s32[2,1]{0,1:T(1,128)}, u32[]{:S(2)}) copy-start(s32[2,1]{0,1:T(1,128)} %param.14) | copy-start | bytes 28
  7.2 37.0 %copy-start.10 = (bf16[2,128,2048]{2,1,0:T(8,128)(2,1)S(1)}, bf16[2,128,2048]{2,1,0:T(8,128)(2,1)}, u32[]{:S(2)}) copy-start(bf16[2,128,2048]{2,1,0:T(8,128)(2,1)} %refs_11_.1) | copy-start | bytes 3145732
  7.2 85.1 %all-gather.2.cloned.1.call-start = ((), (), s32[]{:S(2)}) async-start(), calls=%async_computation.8 | async-start | bytes 4718592 | tf_op jit(solution)/shard_map/all_gather | solution.py:431
  33.9 27.8 %copy-start.27 = (s32[2]{0:T(128)}, s32[2]{0:T(128)S(1)}, u32[]{:S(2)}) copy-start(s32[2]{0:T(128)S(1)} %pad_add_fusion.refs_0_) | copy-start | bytes 28
  33.9 1.2 copy-start.4
  35.2 1.0 copy-start.9
  36.2 0.9 copy-start.15
  37.1 0.8 copy-start.22
  37.9 0.8 copy-start.23
  39.3 4.9 %collective-permute-start = (bf16[432,1024]{1,0:T(8,128)(2,1)S(1)}, bf16[432,1024]{1,0:T(8,128)(2,1)S(1)}, u32[]{:S(2)}, u32[]{:S(2)}) collective-permute-start(bf16[432,1024]{1,0:T(8,128)(2,1)S(1)} %pack.1), channel_id=1, source_target_pairs={{0,256},{256,0},{1,257},{257,1},{2,258},{258,2},{3,259},{259,3},{4... | collective-permute-start | bytes 2654216 | tf_op jit(solution)/shard_map/ppermute | solution.py:390
  44.2 1.2 copy-start.11
  48.0 13.7 %copy-start.18 = (bf16[256,1024]{1,0:T(8,128)(2,1)}, bf16[256,1024]{1,0:T(8,128)(2,1)S(1)}, u32[]{:S(2)}) copy-start(bf16[256,1024]{1,0:T(8,128)(2,1)S(1)} %get-tuple-element.46.refs_4_) | copy-start | bytes 1572868
  62.6 0.8 copy-start.13
  63.4 37.9 %copy-start.7 = (bf16[256,1024]{1,0:T(8,128)(2,1)}, bf16[256,1024]{1,0:T(8,128)(2,1)S(1)}, u32[]{:S(2)}) copy-start(bf16[256,1024]{1,0:T(8,128)(2,1)S(1)} %get-tuple-element.39.refs_0_.refs_3_) | copy-start | bytes 1572868
  63.4 37.9 %copy-start.29 = (f32[16,256]{1,0:T(8,128)}, f32[16,256]{1,0:T(8,128)S(1)}, u32[]{:S(2)}) copy-start(f32[16,256]{1,0:T(8,128)S(1)} %get-tuple-element.58.refs_4_) | copy-start | bytes 49156
  92.3 2.2 %copy-start = (bf16[8,2,128,1024]{3,2,1,0:T(8,128)(2,1)S(1)}, bf16[8,2,128,1024]{3,2,1,0:T(8,128)(2,1)}, u32[]{:S(2)}) copy-start(bf16[8,2,128,1024]{3,2,1,0:T(8,128)(2,1)} %all-gather.2.cloned.1.call-done.refs_1_.refs_2_.refs_5_) | copy-start | bytes 12582916
  96.3 14.3 %all-to-all-start.2 = ((bf16[8,256,128]{2,1,0:T(8,128)(2,1)}), bf16[8,256,128]{2,1,0:T(8,128)(2,1)S(1)}, u32[]{:S(2)}, u32[]{:S(2)}) async-start(bf16[8,256,128]{2,1,0:T(8,128)(2,1)} %values_0.1), calls=%async_computation.2 | async-start | bytes 1048576 | tf_op jit(solution)/shard_map/all_to_all | solution.py:394
  101.3 60.7 %reduce-scatter.2.cloned.1.call-start = ((), (), s32[]{:S(2)}) async-start(), calls=%async_computation.9 | async-start | bytes 589824 | tf_op jit(solution)/shard_map/reduce_scatter | solution.py:513
  101.3 2.2 %copy-start.1 = (bf16[8,2,128,1024]{3,2,1,0:T(8,128)(2,1)S(1)}, bf16[8,2,128,1024]{3,2,1,0:T(8,128)(2,1)}, u32[]{:S(2)}) copy-start(bf16[8,2,128,1024]{3,2,1,0:T(8,128)(2,1)} %all-gather.2.cloned.1.call-done.refs_1_.refs_2_.refs_5_) | copy-start | bytes 12582916
  103.5 1.0 copy-start.14
  110.6 0.8 copy-start.5
  111.4 14.3 %copy-start.2 = (bf16[8,2,128,1024]{3,2,1,0:T(8,128)(2,1)S(1)}, bf16[8,2,128,1024]{3,2,1,0:T(8,128)(2,1)}, u32[]{:S(2)}) copy-start(bf16[8,2,128,1024]{3,2,1,0:T(8,128)(2,1)} %all-gather.2.cloned.1.call-done.refs_1_.refs_2_.refs_5_) | copy-start | bytes 12582916
  111.4 1.2 copy-start.6
  121.4 1.0 copy-start.19
  123.5 0.8 copy-start.12
  124.3 0.8 copy-start.20
  125.1 0.6 copy-start.24
  125.7 17.2 %copy-start.28 = (s32[2]{0:T(128)S(1)}, s32[2]{0:T(128)}, u32[]{:S(2)}) copy-start(s32[2]{0:T(128)} %copy-done.27) | copy-start | bytes 28
  125.7 17.2 %copy-start.30 = (f32[16,256]{1,0:T(8,128)S(1)}, f32[16,256]{1,0:T(8,128)}, u32[]{:S(2)}) copy-start(f32[16,256]{1,0:T(8,128)} %copy-done.29) | copy-start | bytes 49156
  125.7 17.2 %copy-start.25 = (f32[24,1024]{1,0:T(8,128)S(1)}, f32[24,1024]{1,0:T(8,128)}, u32[]{:S(2)}) copy-start(f32[24,1024]{1,0:T(8,128)} %copy-done.24) | copy-start | bytes 294916
  127.6 53.8 %copy-start.32 = (s32[2,1]{0,1:T(1,128)S(1)}, s32[2,1]{0,1:T(1,128)}, u32[]{:S(2)}) copy-start(s32[2,1]{0,1:T(1,128)} %param.14) | copy-start | bytes 28
  127.6 53.8 %copy-start.34 = (s32[2,1]{0,1:T(1,128)S(1)}, s32[2,1]{0,1:T(1,128)}, u32[]{:S(2)}) copy-start(s32[2,1]{0,1:T(1,128)} %param.15) | copy-start | bytes 28
  143.0 1.0 copy-start.8
  145.8 24.6 %all-to-all-start.5 = ((f32[128,1,384]{2,1,0:T(1,128)}), f32[128,1,384]{2,1,0:T(1,128)S(1)}, u32[]{:S(2)}, u32[]{:S(2)}) async-start(f32[128,1,384]{2,1,0:T(1,128)} %map_gradient.1), calls=%async_computation.6 | async-start | bytes 393216 | tf_op jit(solution)/shard_map/all_to_all | solution.py:523
  161.9 0.8 copy-start.26
  164.4 0.8 copy-start.16
  165.2 26.8 %copy-start.17 = (bf16[256,1024]{1,0:T(8,128)(2,1)S(1)}, bf16[256,1024]{1,0:T(8,128)(2,1)}, u32[]{:S(2)}) copy-start(bf16[256,1024]{1,0:T(8,128)(2,1)} %copy-done.16) | copy-start | bytes 1572868
  165.2 26.7 %collective-permute-start.1 = (bf16[256,1024]{1,0:T(8,128)(2,1)}, bf16[256,1024]{1,0:T(8,128)(2,1)S(1)}, u32[]{:S(2)}, u32[]{:S(2)}) collective-permute-start(bf16[256,1024]{1,0:T(8,128)(2,1)} %get-tuple-element.50), channel_id=1, source_target_pairs={{0,256},{256,0},{1,257},{257,1},{2,258},{258,2},{3,259},{259,3},{4... | collective-permute-start | bytes 1572872 | tf_op jit(solution)/shard_map/ppermute | solution.py:390
  171.2 22.4 %all-to-all-start.6 = ((f32[64,1,768]{2,1,0:T(1,128)}), f32[64,1,768]{2,1,0:T(1,128)S(1)}, u32[]{:S(2)}, u32[]{:S(2)}) async-start(f32[64,1,768]{2,1,0:T(1,128)} %get-tuple-element.61), calls=%async_computation.7 | async-start | bytes 393216 | tf_op jit(solution)/shard_map/all_to_all | solution.py:528
  181.4 2.2 %copy-start.3 = (bf16[8,2,128,1024]{3,2,1,0:T(8,128)(2,1)S(1)}, bf16[8,2,128,1024]{3,2,1,0:T(8,128)(2,1)}, u32[]{:S(2)}) copy-start(bf16[8,2,128,1024]{3,2,1,0:T(8,128)(2,1)} %all-gather.2.cloned.1.call-done.refs_1_.refs_2_.refs_5_) | copy-start | bytes 12582916
  183.6 1.0 copy-start.21
  187.1 3.6 %collective-permute-start.2 = (bf16[96,1024]{1,0:T(8,128)(2,1)S(1)}, bf16[96,1024]{1,0:T(8,128)(2,1)S(1)}, u32[]{:S(2)}, u32[]{:S(2)}) collective-permute-start(bf16[96,1024]{1,0:T(8,128)(2,1)S(1)} %get-tuple-element.56), channel_id=1, source_target_pairs={{0,256},{256,0},{1,257},{257,1},{2,258},{258,2},{3,259},{259,3},{4... | collective-permute-start | bytes 589832 | tf_op jit(solution)/shard_map/ppermute | solution.py:390
Sparse Core Ops, SparseCore 0:
  33.2 59.0 all-gather.1
  127.7 34.1 reduce-scatter.1

commit v7 on v6

--- a/solution.py
+++ b/solution.py
@@ -301,8 +301,9 @@
 
 def slot_gradient_kernel(
     core, counts, starts, received, ups, columns, downs, gains, entry, inverse, gradient,
-    own_slots, other_slots,
+    own_slots, other_slots, token,
 ):
+    token[...] = jnp.zeros_like(token)
     dots, _ = total_of_payloads(received)
     full_gradient = gathered_gradient(received)
     lora_gradient = ADAPTER_SCALE * nt(ups[0], full_gradient)
@@ -527,10 +528,10 @@
     )
     everywhere = lax.all_to_all(summed, "fsdp", 0, 0)
 
-    own_slots, other_slots = call(
+    own_slots, other_slots, slots_token = call(
         slot_gradient_kernel,
         "slot_gradient",
-        [((VIS, HALF), BF)] * 2,
+        [((VIS, HALF), BF)] * 2 + [token],
         (core, counts, begins),
         (gathered, ups, columns, downs, gains, entry, inverse_0, gradient),
     )
@@ -540,6 +541,7 @@
         [wide] * 2,
         (core,),
         (values_1, weights, hidden_0),
+        after=(slots_token,),
     )
     slots, slots_placed = call(
         place_kernel,

time: 203 us -> 201 us (level)
    reduce_scatter x1, waiting for transfers between devices: 5.94 us -> 0.01 us  [on_device(): lax.psum_scatter(partial_1, ('section', 'tp'), scatter_dimension=0)]
    all_to_all x1, waiting for transfers between devices: 0.01 us -> 5.39 us  [on_device(): everywhere = lax.all_to_all(summed, 'fsdp', 0, 0)]
    unnamed x72 -> x70, local copies, waits for them, and re-layouts: 23.4 us -> 23.3 us
where the time goes in v7:
time: 201 us; the launch traced here: 199 us
  blocking collectives  62 us (31%)
  waiting for transfers between devices  46.7 us (23%)
  starting transfers between devices  31.5 us (16%)
  local copies, waits for them, and re-layouts  24.3 us (12%)
  Pallas kernels  19.7 us (10%)
  between operations  14.3 us (7%)
    all_to_all x3, blocking collectives, to_heads(): return lax.all_to_all(block, ('section', 'tp'), 0, 0)  37.1 us
    all_gather x1, waiting for transfers between devices, on_device(): lax.all_gather(head_columns, 'fsdp', axis=0, axis_index_groups=row_groups)  28.9 us
    all_to_all x1, blocking collectives, on_device(): lax.all_to_all(pieces, ('section', 'fsdp'), 0, 0, axis_index_groups=head_...  24.8 us
    unnamed x70, local copies, waits for them, and re-layouts  23.3 us
    pallas_call x15, Pallas kernels, call(): pl.pallas_call(body, out_shape=[jax.ShapeDtypeStruct(shape, dtype) for sh...  19.7 us
    all_to_all x1, starting transfers between devices, on_device(): arrived = lax.all_to_all(chunks, ('section', 'fsdp'), 0, 0)  10.2 us
    all_to_all x1, starting transfers between devices, on_device(): everywhere = lax.all_to_all(summed, 'fsdp', 0, 0)  8.42 us
    ppermute x3, starting transfers between devices, swap_cores(): return lax.ppermute(block, 'section', [(0, 1), (1, 0)])  7.93 us
  transfers between devices with their start and end apart: 8, of which 6 were waited for; matrix products, arithmetic and copies ran while one was open for 0% of the time, Pallas kernels for 7%

profile of v7, /device:TPU:1, one launch (start us, length us, event | category | flops | bytes accessed | tf_op | source)
XLA Modules:
  0.0 199.4 jit_solution(8039636582459381691)
XLA Ops:
  7.2 0.0 copy-start.31
  7.2 0.0 all-gather.2.cloned.1.call-start
  7.3 1.0 reshape.18
  8.2 0.1 broadcast_in_dim.24
  8.3 24.8 %all_to_all.35 = bf16[16,16,1024]{2,1,0:T(8,128)(2,1)} all-to-all(bf16[16,16,1024]{2,1,0:T(8,128)(2,1)S(1)} %bitcast.42), channel_id=1, replica_groups={{0,4,8,12,16,20,24,28,256,260,264,268,272,276,280,284},{32,36,40,44,48,..., dimensions={0} | all-to-all | bytes 1048576 | tf_op jit(solution)/shard_map/all_to_all | solution.py:428
  33.1 0.0 all-gather.2.cloned.1.call-update
  33.1 0.7 reduce
  33.9 0.1 pad_add_fusion.refs_0_
  34.0 0.0 copy-start.4
  34.0 1.2 copy-done.4
  35.2 1.0 copy-done.9
  36.2 0.9 copy-done.15
  37.1 0.8 copy-done.20
  37.9 0.8 copy-done.21
  38.7 0.6 pack.1
  39.3 2.9 %collective-permute-start = (bf16[432,1024]{1,0:T(8,128)(2,1)S(1)}, bf16[432,1024]{1,0:T(8,128)(2,1)S(1)}, u32[]{:S(2)}, u32[]{:S(2)}) collective-permute-start(bf16[432,1024]{1,0:T(8,128)(2,1)S(1)} %pack.1), channel_id=1, source_target_pairs={{0,256},{256,0},{1,257},{257,1},{2,258},{258,2},{3,259},{259,3},{4... | collective-permute-start | bytes 2654216 | tf_op jit(solution)/shard_map/ppermute | solution.py:391
  42.2 2.0 %collective-permute-done.refs_4_ = bf16[432,1024]{1,0:T(8,128)(2,1)S(1)} collective-permute-done((bf16[432,1024]{1,0:T(8,128)(2,1)S(1)}, bf16[432,1024]{1,0:T(8,128)(2,1)S(1)}, u32[]{:S(2)}, u32[]{:S(2)}) %collective-permute-start) | collective-permute-done | bytes 884768 | tf_op jit(solution)/shard_map/ppermute | solution.py:391
  44.2 0.0 copy-start.11
  44.2 1.2 copy-done.11
  45.5 2.6 %prepare.1 = (bf16[2,2,1024,128]{3,2,1,0:T(8,128)(2,1)S(1)}, bf16[256,1024]{1,0:T(8,128)(2,1)S(1)}, bf16[256,1024]{1,0:T(8,128)(2,1)S(1)}, bf16[2,16,1024]{2,1,0...) custom-call(s32[2]{0:T(128)S(1)} %pad_add_fusion.refs_0_, ...), custom_call_target="tpu_custom_call" | custom-call | bytes 7634944 | tf_op jit(solution)/shard_map/prepare/pallas_call | solution.py:377
  48.1 0.0 copy-start.16
  48.1 13.6 %all_to_all.36.refs_1_ = bf16[8,304,128]{2,1,0:T(8,128)(2,1)S(1)} all-to-all(bf16[8,304,128]{2,1,0:T(8,128)(2,1)S(1)} %get-tuple-element.36), channel_id=1, replica_groups=mesh['section'=2,'fsdp'=64,'tp'=4] {'section','tp'}, dimensions={0} | all-to-all | bytes 1245184 | tf_op jit(solution)/shard_map/all_to_all | solution.py:395
  61.7 0.9 entry_norm.1
  62.6 0.8 copy-done.13
  63.4 28.9 %all-gather.2.cloned.1.call-done.refs_1_.refs_2_.refs_5_ = bf16[8,2,128,1024]{3,2,1,0:T(8,128)(2,1)} async-done(((bf16[1,2,128,1024]{3,2,1,0:T(8,128)(2,1)}), bf16[8,2,128,1024]{3,2,1,0:T(8,128)(2,1)}) %all-gather.2.cloned.1.call-update) | async-done | bytes 4194320 | tf_op jit(solution)/shard_map/all_gather | solution.py:432
  92.3 2.2 %copy-done = bf16[8,2,128,1024]{3,2,1,0:T(8,128)(2,1)S(1)} copy-done((bf16[8,2,128,1024]{3,2,1,0:T(8,128)(2,1)S(1)}, bf16[8,2,128,1024]{3,2,1,0:T(8,128)(2,1)}, u32[]{:S(2)}) %copy-start) | copy-done | bytes 4194328
  94.5 1.8 values_0.1
  96.3 4.9 %all-to-all-start.2 = ((bf16[8,256,128]{2,1,0:T(8,128)(2,1)}), bf16[8,256,128]{2,1,0:T(8,128)(2,1)S(1)}, u32[]{:S(2)}, u32[]{:S(2)}) async-start(bf16[8,256,128]{2,1,0:T(8,128)(2,1)} %values_0.1), calls=%async_computation.2 | async-start | bytes 1048576 | tf_op jit(solution)/shard_map/all_to_all | solution.py:395
  101.3 2.2 %copy-done.1 = bf16[8,2,128,1024]{3,2,1,0:T(8,128)(2,1)S(1)} copy-done((bf16[8,2,128,1024]{3,2,1,0:T(8,128)(2,1)S(1)}, bf16[8,2,128,1024]{3,2,1,0:T(8,128)(2,1)}, u32[]{:S(2)}) %copy-start.1) | copy-done | bytes 4194328
  103.5 1.0 copy-done.14
  104.5 0.9 scaled_1.1.refs_3_
  105.4 5.3 %all-to-all-done.2.refs_0_ = bf16[8,256,128]{2,1,0:T(8,128)(2,1)S(1)} async-done(((bf16[8,256,128]{2,1,0:T(8,128)(2,1)}), bf16[8,256,128]{2,1,0:T(8,128)(2,1)S(1)}, u32[]{:S(2)}, u32[]{:S(2)}) %all-to-all-start.2) | async-done | bytes 524320 | tf_op jit(solution)/shard_map/all_to_all | solution.py:395
  110.6 0.8 copy-done.5
  111.4 1.2 copy-done.6
  112.6 0.6 first_output.1
  113.2 8.2 %all_to_all.37.refs_0_ = f32[8,8,256]{2,1,0:T(8,128)S(1)} all-to-all(f32[8,8,256]{2,1,0:T(8,128)S(1)} %get-tuple-element.45), channel_id=1, replica_groups=mesh['section'=2,'fsdp'=64,'tp'=4] {'section','tp'}, dimensions={0} | all-to-all | bytes 131072 | tf_op jit(solution)/shard_map/all_to_all | solution.py:395
  121.4 1.0 copy-done.17
  122.5 1.0 first_gradient.1
  123.5 0.0 copy-start.12
  123.5 0.8 copy-done.12
  124.3 0.8 copy-done.18
  125.1 0.6 copy-done.22
  125.8 1.8 values_1.1
  127.6 0.0 reduce-scatter.2.cloned.1.call-update
  127.6 15.3 %all_to_all.38.refs_3_.refs_1_ = bf16[8,304,128]{2,1,0:T(8,128)(2,1)S(1)} all-to-all(bf16[8,304,128]{2,1,0:T(8,128)(2,1)} %copy-done.12), channel_id=1, replica_groups=mesh['section'=2,'fsdp'=64,'tp'=4] {'section','tp'}, dimensions={0} | all-to-all | bytes 1245184 | tf_op jit(solution)/shard_map/all_to_all | solution.py:395
  143.0 1.0 copy-done.8
  144.0 1.8 map_gradient.1
  145.8 10.2 %all-to-all-start.5 = ((f32[128,1,384]{2,1,0:T(1,128)}), f32[128,1,384]{2,1,0:T(1,128)S(1)}, u32[]{:S(2)}, u32[]{:S(2)}) async-start(f32[128,1,384]{2,1,0:T(1,128)} %map_gradient.1), calls=%async_computation.6 | async-start | bytes 393216 | tf_op jit(solution)/shard_map/all_to_all | solution.py:524
  156.1 2.2 %copy-done.3 = bf16[8,2,128,1024]{3,2,1,0:T(8,128)(2,1)S(1)} copy-done((bf16[8,2,128,1024]{3,2,1,0:T(8,128)(2,1)S(1)}, bf16[8,2,128,1024]{3,2,1,0:T(8,128)(2,1)}, u32[]{:S(2)}) %copy-start.3) | copy-done | bytes 4194328
  158.3 1.0 copy-done.19
  159.3 2.4 %slot_gradient.1 = (bf16[96,1024]{1,0:T(8,128)(2,1)S(1)}, bf16[96,1024]{1,0:T(8,128)(2,1)S(1)}, f32[8,128]{1,0:T(8,128)S(1)}) custom-call(s32[2]{0:T(128)S(1)} %copy-done.26, s32[2]{0:T(128)S(1)} %bitcast.37, s32[2]{0:T(128)S(1)} %bitcast.39, bf16[8,304,128]{2,1,0:T(8,128)(2,1)S(1)} %all_to_all.38.refs_3_.refs_1_, ...), custom_call_target="tpu_custom_call" | custom-call | bytes 6590464 | tf_op jit(solution)/shard_map/slot_gradient/pallas_call | solution.py:377
  161.8 0.7 copy-done.34
  162.4 0.8 copy-done.24
  163.3 0.9 second_output.1
  164.1 2.5 %collective-permute-start.1 = (bf16[256,1024]{1,0:T(8,128)(2,1)S(1)}, bf16[256,1024]{1,0:T(8,128)(2,1)S(1)}, u32[]{:S(2)}, u32[]{:S(2)}) collective-permute-start(bf16[256,1024]{1,0:T(8,128)(2,1)S(1)} %get-tuple-element.55), channel_id=1, source_target_pairs={{0,256},{256,0},{1,257},{257,1},{2,258},{258,2},{3,259},{259,3},{4... | collective-permute-start | bytes 1572872 | tf_op jit(solution)/shard_map/ppermute | solution.py:391
  166.6 3.8 %all-to-all-done.5.refs_0_ = f32[128,1,384]{2,1,0:T(1,128)S(1)} async-done(((f32[128,1,384]{2,1,0:T(1,128)}), f32[128,1,384]{2,1,0:T(1,128)S(1)}, u32[]{:S(2)}, u32[]{:S(2)}) %all-to-all-start.5) | async-done | bytes 196640 | tf_op jit(solution)/shard_map/all_to_all | solution.py:524
  170.4 0.8 sum_maps.1
  171.3 8.4 %all-to-all-start.6 = ((f32[64,1,768]{2,1,0:T(1,128)}), f32[64,1,768]{2,1,0:T(1,128)S(1)}, u32[]{:S(2)}, u32[]{:S(2)}) async-start(f32[64,1,768]{2,1,0:T(1,128)} %get-tuple-element.63), calls=%async_computation.7 | async-start | bytes 393216 | tf_op jit(solution)/shard_map/all_to_all | solution.py:529
  179.7 2.6 %collective-permute-start.2 = (bf16[96,1024]{1,0:T(8,128)(2,1)}, bf16[96,1024]{1,0:T(8,128)(2,1)S(1)}, u32[]{:S(2)}, u32[]{:S(2)}) collective-permute-start(bf16[96,1024]{1,0:T(8,128)(2,1)} %copy-done.34), channel_id=1, source_target_pairs={{0,256},{256,0},{1,257},{257,1},{2,258},{258,2},{3,259},{259,3},{4... | collective-permute-start | bytes 589832 | tf_op jit(solution)/shard_map/ppermute | solution.py:391
  182.3 1.3 collective-permute-done.2.refs_2_
  183.5 1.3 place_slots.1
  184.9 1.6 place_hidden.1
  186.4 5.4 %all-to-all-done.6.refs_0_ = f32[64,1,768]{2,1,0:T(1,128)S(1)} async-done(((f32[64,1,768]{2,1,0:T(1,128)}), f32[64,1,768]{2,1,0:T(1,128)S(1)}, u32[]{:S(2)}, u32[]{:S(2)}) %all-to-all-start.6) | async-done | bytes 196640 | tf_op jit(solution)/shard_map/all_to_all | solution.py:529
  191.8 0.7 maps.1
  (49 shorter events, 0.1 us)
Async XLA Ops:
  7.2 37.1 %copy-start.33 = (s32[2,1]{0,1:T(1,128)S(1)}, s32[2,1]{0,1:T(1,128)}, u32[]{:S(2)}) copy-start(s32[2,1]{0,1:T(1,128)} %param.16) | copy-start | bytes 28
  7.2 37.1 %copy-start.31 = (s32[2,1]{0,1:T(1,128)S(1)}, s32[2,1]{0,1:T(1,128)}, u32[]{:S(2)}) copy-start(s32[2,1]{0,1:T(1,128)} %param.15) | copy-start | bytes 28
  7.2 37.0 %copy-start.29 = (s32[2,1]{0,1:T(1,128)S(1)}, s32[2,1]{0,1:T(1,128)}, u32[]{:S(2)}) copy-start(s32[2,1]{0,1:T(1,128)} %param.14) | copy-start | bytes 28
  7.2 37.0 %copy-start.10 = (bf16[2,128,2048]{2,1,0:T(8,128)(2,1)S(1)}, bf16[2,128,2048]{2,1,0:T(8,128)(2,1)}, u32[]{:S(2)}) copy-start(bf16[2,128,2048]{2,1,0:T(8,128)(2,1)} %refs_11_.1) | copy-start | bytes 3145732
  7.2 85.1 %all-gather.2.cloned.1.call-start = ((), (), s32[]{:S(2)}) async-start(), calls=%async_computation.8 | async-start | bytes 4718592 | tf_op jit(solution)/shard_map/all_gather | solution.py:432
  34.0 27.8 %copy-start.25 = (s32[2]{0:T(128)}, s32[2]{0:T(128)S(1)}, u32[]{:S(2)}) copy-start(s32[2]{0:T(128)S(1)} %pad_add_fusion.refs_0_) | copy-start | bytes 28
  34.0 1.2 copy-start.4
  35.2 1.0 copy-start.9
  36.2 0.9 copy-start.15
  37.1 0.8 copy-start.20
  37.9 0.8 copy-start.21
  39.3 4.9 %collective-permute-start = (bf16[432,1024]{1,0:T(8,128)(2,1)S(1)}, bf16[432,1024]{1,0:T(8,128)(2,1)S(1)}, u32[]{:S(2)}, u32[]{:S(2)}) collective-permute-start(bf16[432,1024]{1,0:T(8,128)(2,1)S(1)} %pack.1), channel_id=1, source_target_pairs={{0,256},{256,0},{1,257},{257,1},{2,258},{258,2},{3,259},{259,3},{4... | collective-permute-start | bytes 2654216 | tf_op jit(solution)/shard_map/ppermute | solution.py:391
  44.2 1.2 copy-start.11
  48.1 13.6 %copy-start.16 = (bf16[256,1024]{1,0:T(8,128)(2,1)}, bf16[256,1024]{1,0:T(8,128)(2,1)S(1)}, u32[]{:S(2)}) copy-start(bf16[256,1024]{1,0:T(8,128)(2,1)S(1)} %get-tuple-element.47.refs_4_) | copy-start | bytes 1572868
  62.6 0.8 copy-start.13
  63.4 37.9 %copy-start.7 = (bf16[256,1024]{1,0:T(8,128)(2,1)}, bf16[256,1024]{1,0:T(8,128)(2,1)S(1)}, u32[]{:S(2)}) copy-start(bf16[256,1024]{1,0:T(8,128)(2,1)S(1)} %get-tuple-element.40.refs_0_.refs_3_) | copy-start | bytes 1572868
  63.4 37.9 %copy-start.27 = (f32[16,256]{1,0:T(8,128)}, f32[16,256]{1,0:T(8,128)S(1)}, u32[]{:S(2)}) copy-start(f32[16,256]{1,0:T(8,128)S(1)} %get-tuple-element.60.refs_4_) | copy-start | bytes 49156
  92.3 2.2 %copy-start = (bf16[8,2,128,1024]{3,2,1,0:T(8,128)(2,1)S(1)}, bf16[8,2,128,1024]{3,2,1,0:T(8,128)(2,1)}, u32[]{:S(2)}) copy-start(bf16[8,2,128,1024]{3,2,1,0:T(8,128)(2,1)} %all-gather.2.cloned.1.call-done.refs_1_.refs_2_.refs_5_) | copy-start | bytes 12582916
  96.3 14.3 %all-to-all-start.2 = ((bf16[8,256,128]{2,1,0:T(8,128)(2,1)}), bf16[8,256,128]{2,1,0:T(8,128)(2,1)S(1)}, u32[]{:S(2)}, u32[]{:S(2)}) async-start(bf16[8,256,128]{2,1,0:T(8,128)(2,1)} %values_0.1), calls=%async_computation.2 | async-start | bytes 1048576 | tf_op jit(solution)/shard_map/all_to_all | solution.py:395
  101.3 61.2 %reduce-scatter.2.cloned.1.call-start = ((), (), s32[]{:S(2)}) async-start(), calls=%async_computation.9 | async-start | bytes 589824 | tf_op jit(solution)/shard_map/reduce_scatter | solution.py:514
  101.3 2.2 %copy-start.1 = (bf16[8,2,128,1024]{3,2,1,0:T(8,128)(2,1)S(1)}, bf16[8,2,128,1024]{3,2,1,0:T(8,128)(2,1)}, u32[]{:S(2)}) copy-start(bf16[8,2,128,1024]{3,2,1,0:T(8,128)(2,1)} %all-gather.2.cloned.1.call-done.refs_1_.refs_2_.refs_5_) | copy-start | bytes 12582916
  103.5 1.0 copy-start.14
  110.6 0.8 copy-start.5
  111.4 14.3 %copy-start.2 = (bf16[8,2,128,1024]{3,2,1,0:T(8,128)(2,1)S(1)}, bf16[8,2,128,1024]{3,2,1,0:T(8,128)(2,1)}, u32[]{:S(2)}) copy-start(bf16[8,2,128,1024]{3,2,1,0:T(8,128)(2,1)} %all-gather.2.cloned.1.call-done.refs_1_.refs_2_.refs_5_) | copy-start | bytes 12582916
  111.4 1.2 copy-start.6
  121.4 1.0 copy-start.17
  123.5 0.8 copy-start.12
  124.3 0.8 copy-start.18
  125.1 0.6 copy-start.22
  125.7 17.2 %copy-start.26 = (s32[2]{0:T(128)S(1)}, s32[2]{0:T(128)}, u32[]{:S(2)}) copy-start(s32[2]{0:T(128)} %copy-done.25) | copy-start | bytes 28
  125.7 17.2 %copy-start.28 = (f32[16,256]{1,0:T(8,128)S(1)}, f32[16,256]{1,0:T(8,128)}, u32[]{:S(2)}) copy-start(f32[16,256]{1,0:T(8,128)} %copy-done.27) | copy-start | bytes 49156
  125.7 17.2 %copy-start.23 = (f32[24,1024]{1,0:T(8,128)S(1)}, f32[24,1024]{1,0:T(8,128)}, u32[]{:S(2)}) copy-start(f32[24,1024]{1,0:T(8,128)} %copy-done.22) | copy-start | bytes 294916
  125.7 30.3 %copy-start.30 = (s32[2,1]{0,1:T(1,128)S(1)}, s32[2,1]{0,1:T(1,128)}, u32[]{:S(2)}) copy-start(s32[2,1]{0,1:T(1,128)} %param.14) | copy-start | bytes 28
  125.8 30.3 %copy-start.32 = (s32[2,1]{0,1:T(1,128)S(1)}, s32[2,1]{0,1:T(1,128)}, u32[]{:S(2)}) copy-start(s32[2,1]{0,1:T(1,128)} %param.15) | copy-start | bytes 28
  143.0 1.0 copy-start.8
  145.8 24.6 %all-to-all-start.5 = ((f32[128,1,384]{2,1,0:T(1,128)}), f32[128,1,384]{2,1,0:T(1,128)S(1)}, u32[]{:S(2)}, u32[]{:S(2)}) async-start(f32[128,1,384]{2,1,0:T(1,128)} %map_gradient.1), calls=%async_computation.6 | async-start | bytes 393216 | tf_op jit(solution)/shard_map/all_to_all | solution.py:524
  156.0 2.2 %copy-start.3 = (bf16[8,2,128,1024]{3,2,1,0:T(8,128)(2,1)S(1)}, bf16[8,2,128,1024]{3,2,1,0:T(8,128)(2,1)}, u32[]{:S(2)}) copy-start(bf16[8,2,128,1024]{3,2,1,0:T(8,128)(2,1)} %all-gather.2.cloned.1.call-done.refs_1_.refs_2_.refs_5_) | copy-start | bytes 12582916
  158.3 1.0 copy-start.19
  161.7 0.7 copy-start.34
  162.4 0.8 copy-start.24
  164.1 20.7 %collective-permute-start.1 = (bf16[256,1024]{1,0:T(8,128)(2,1)S(1)}, bf16[256,1024]{1,0:T(8,128)(2,1)S(1)}, u32[]{:S(2)}, u32[]{:S(2)}) collective-permute-start(bf16[256,1024]{1,0:T(8,128)(2,1)S(1)} %get-tuple-element.55), channel_id=1, source_target_pairs={{0,256},{256,0},{1,257},{257,1},{2,258},{258,2},{3,259},{259,3},{4... | collective-permute-start | bytes 1572872 | tf_op jit(solution)/shard_map/ppermute | solution.py:391
  171.3 20.6 %all-to-all-start.6 = ((f32[64,1,768]{2,1,0:T(1,128)}), f32[64,1,768]{2,1,0:T(1,128)S(1)}, u32[]{:S(2)}, u32[]{:S(2)}) async-start(f32[64,1,768]{2,1,0:T(1,128)} %get-tuple-element.63), calls=%async_computation.7 | async-start | bytes 393216 | tf_op jit(solution)/shard_map/all_to_all | solution.py:529
  179.7 3.9 %collective-permute-start.2 = (bf16[96,1024]{1,0:T(8,128)(2,1)}, bf16[96,1024]{1,0:T(8,128)(2,1)S(1)}, u32[]{:S(2)}, u32[]{:S(2)}) collective-permute-start(bf16[96,1024]{1,0:T(8,128)(2,1)} %copy-done.34), channel_id=1, source_target_pairs={{0,256},{256,0},{1,257},{257,1},{2,258},{258,2},{3,259},{259,3},{4... | collective-permute-start | bytes 589832 | tf_op jit(solution)/shard_map/ppermute | solution.py:391
Sparse Core Ops, SparseCore 0:
  33.3 59.0 all-gather.1
  127.7 34.4 reduce-scatter.1
